TPU v7x, 256 devices: a whole 4x4x8 slice. The times are simulated.
256 devices in a mesh: gx: 32 (over x_hi, z, core), gy: 8 (over x_lo, y).
Axes of the slice: x: 4 (x_hi: 2, x_lo: 2; x = x_hi * 2 + x_lo), y: 4, z: 8, core: 2. Of those that a mesh axis runs over, the one named last changes fastest.
Arguments:
- forward: float32 [19, 1024, 4096], P(None, 'gx', 'gy'), may hold values from 0.02 to 0.12
- adjoint: float32 [19, 1024, 4096], P(None, 'gx', 'gy'), may hold values from -6 to 6
- design: float32 [1024, 4096], P('gx', 'gy'), may hold values from 0 to 0.6
- node_type: int32 [1024, 4096], P('gx', 'gy'), may hold values from 0 to 3
Outputs:
- adjoint_new: float32 [19, 1024, 4096], P(None, 'gx', 'gy')
- filtered: float32 [1024, 4096], P('gx', 'gy')
Inputs may be any that keep to these rules, and one draw needn't show every extreme that they name: `node_type`: 0 fluid, 1 wall, 2 inlet, 3 outlet.
All inputs are finite; a program needn't handle non-finite values.
Results may differ from a plain program's by a relative error of at most 0.00019.
Values sent between devices are 32-bit elements; how exact they have to be, the bound alone decides.
No kernel may reach another device: no remote copies, remote signals or barrier semaphores. Data moves between devices by JAX's collectives and lax.ppermute only.
A program may use at most 64 MiB of HBM per device.

v0:
```python
import jax
import jax.numpy as jnp
import numpy as np
from jax import lax
from jax.sharding import PartitionSpec as P

NZ = 16
ITERS = 3


velocities = np.array(
    [
        [0, 0, 0],
        [1, 0, 0],
        [-1, 0, 0],
        [0, 1, 0],
        [0, -1, 0],
        [0, 0, 1],
        [0, 0, -1],
        [1, 1, 0],
        [-1, -1, 0],
        [1, -1, 0],
        [-1, 1, 0],
        [1, 0, 1],
        [-1, 0, -1],
        [1, 0, -1],
        [-1, 0, 1],
        [0, 1, 1],
        [0, -1, -1],
        [0, 1, -1],
        [0, -1, 1],
    ]
)
OPPOSITE = np.array(
    [0, 2, 1, 4, 3, 6, 5, 8, 7, 10, 9, 12, 11, 14, 13, 16, 15, 18, 17], dtype=np.int32
)
lattice_weights = np.array([1.0 / 3.0] + [1.0 / 18.0] * 6 + [1.0 / 36.0] * 12)
relax_rate = 1.25
radius_sq = 4.0


def padded_2(cells, sides, width, closed):
    for axis, dim in sides:
        count = lax.axis_size(axis)
        ends = count if closed else count - 1
        head = lax.slice_in_dim(cells, 0, width, axis=dim)
        tail = lax.slice_in_dim(cells, cells.shape[dim] - width, cells.shape[dim], axis=dim)
        cells = jnp.concatenate(
            [
                lax.ppermute(tail, axis, [(i, (i + 1) % count) for i in range(ends)]),
                cells,
                lax.ppermute(head, axis, [((i + 1) % count, i) for i in range(ends)]),
            ],
            axis=dim,
        )
    return cells


def adjoint_cell(read, forward, design, node_type):
    highest = lax.Precision.HIGHEST
    table = jnp.asarray(velocities, jnp.float32)
    weights = jnp.asarray(lattice_weights, jnp.float32)[:, None, None]
    density = jnp.sum(forward, axis=0)
    momentum = jnp.einsum("qk,qxw->kxw", table, forward, precision=highest)
    velocity = momentum / density
    projected = jnp.einsum("qk,kxw->qxw", table, velocity, precision=highest)
    speed_sq = jnp.sum(velocity * velocity, axis=0)
    equilibrium = (
        weights * density * (1.0 + 3.0 * projected + 4.5 * projected * projected - 1.5 * speed_sq)
    )
    collided = forward - relax_rate * (forward - equilibrium)
    is_fluid = node_type != 1
    sensitivity = jnp.where(is_fluid, jnp.sum(read * (collided[OPPOSITE] - collided), axis=0), 0.0)
    blended = (1.0 - design) * read + design * read[OPPOSITE]
    weighted = weights * blended
    zeroth = jnp.sum(weighted, axis=0)
    first_moment = jnp.einsum("qk,qxw->kxw", table, weighted, precision=highest)
    second = jnp.einsum("qk,qxw->kxw", table, weighted * projected, precision=highest)
    quadratic = jnp.sum(weighted * projected * projected, axis=0)
    combined = 3.0 * first_moment + 9.0 * second - 3.0 * velocity * zeroth
    projection = jnp.einsum("qk,kxw->qxw", table, combined, precision=highest)
    feq_adjoint = zeroth + projection - 4.5 * quadratic + 1.5 * speed_sq * zeroth
    relaxed = blended - relax_rate * (blended - feq_adjoint)
    source = (node_type == 2).astype(jnp.float32) - (node_type == 3).astype(jnp.float32)
    result = jnp.where(is_fluid, relaxed + source, read[OPPOSITE])
    return (result, sensitivity)


def gather_faces(adjoint):
    extended = padded_2(adjoint, (("gx", 1),), 1, True)
    return padded_2(extended, (("gy", 2),), NZ, False)


def pull_bordered(bordered, layers, columns):
    padded = jnp.pad(bordered, ((0, 0), (0, 0), (1, 1)))
    bounce = bordered[:, 1 : 1 + layers, NZ : NZ + columns]
    depth_index = jnp.arange(columns) % NZ
    pulled = []
    for member in range(19):
        step_x, step_y, step_z = [int(entry) for entry in velocities[member]]
        start = 1 + NZ + step_y * NZ + step_z
        moved = padded[member, 1 + step_x : 1 + step_x + layers, start : start + columns]
        if step_z != 0:
            outside = (depth_index + step_z < 0) | (depth_index + step_z >= NZ)
            moved = jnp.where(outside, bounce[int(OPPOSITE[member])], moved)
        pulled.append(moved)
    return jnp.stack(pulled)


def stencil_core(padded_field):
    rows, width = padded_field.shape
    inner_width = width - 2 * NZ
    center = padded_field[1:-1, NZ : NZ + inner_width]
    beside = padded_field[:-2, NZ : NZ + inner_width] + padded_field[2:, NZ : NZ + inner_width]
    beside = beside + padded_field[1:-1, :inner_width] + padded_field[1:-1, 2 * NZ :]
    depth_index = jnp.arange(inner_width) % NZ
    above = jnp.where(depth_index < NZ - 1, jnp.pad(center[:, 1:], ((0, 0), (0, 1))), 0.0)
    below = jnp.where(depth_index > 0, jnp.pad(center[:, :-1], ((0, 0), (1, 0))), 0.0)
    return (1.0 + 6.0 * radius_sq) * center - radius_sq * (beside + above + below)


def helmholtz(values):
    wide = padded_2(values, (("gx", 0),), 1, True)
    padded = padded_2(wide, (("gy", 1),), NZ, False)
    return stencil_core(padded)


def squares(residual):
    return lax.psum(jnp.sum(residual * residual), ("gx", "gy"))


def curvature_sum(product):
    return lax.psum(jnp.sum(product), ("gx", "gy"))


def solve_filter(sensitivity, apply_op, trim, inner):
    depth = ITERS
    filtered = jnp.zeros_like(sensitivity)
    residual = sensitivity
    direction = sensitivity
    norm_now = squares(inner(residual, depth))
    for iteration in range(ITERS):
        applied = apply_op(direction, depth)
        depth = depth - 1
        direction, residual, filtered = (trim(direction), trim(residual), trim(filtered))
        step_size = norm_now / curvature_sum(inner(direction * applied, depth))
        filtered = filtered + step_size * direction
        residual = residual - step_size * applied
        norm_next = squares(inner(residual, depth))
        direction = residual + norm_next / norm_now * direction
        norm_now = norm_next
    return filtered


def shards(forward, adjoint, design, node_type):
    populations, layers, columns = adjoint.shape
    read = pull_bordered(gather_faces(adjoint), layers, columns)
    adjoint_new, sensitivity = adjoint_cell(read, forward, design, node_type)

    def apply_plain(field, depth):
        return helmholtz(field)

    def keep(field):
        return field

    def whole(field, depth):
        return field

    filtered = solve_filter(sensitivity, apply_plain, keep, whole)
    return (adjoint_new, filtered)


def solution(mesh):
    placed = (P(None, "gx", "gy"), P(None, "gx", "gy"), P("gx", "gy"), P("gx", "gy"))
    return jax.shard_map(
        shards,
        mesh=mesh,
        in_specs=placed,
        out_specs=(P(None, "gx", "gy"), P("gx", "gy")),
        check_vma=False,
    )
```

profile of v0, /device:TPU:1, one launch (start us, length us, event | category | flops | bytes accessed | tf_op | source)
XLA Modules:
  0.0 500.0 jit_solution(3170402657674297901)
XLA Ops:
  0.7 2.1 copy.33
  3.4 3.0 collective-permute-start.1
  7.5 1.4 reduce_sum.100
  8.9 3.0 multiply_reduce_fusion.2
  16.4 3.0 collective-permute-start.3
  19.5 1.5 collective-permute-start.2
  20.9 1.5 pad_maximum_fusion.32
  22.4 2.0 collective-permute-done.3
  24.4 3.8 collective-permute-done.2
  32.4 2.0 stack.2
  35.2 1.7 gather_fusion
  36.9 6.7 %multiply_reduce_fusion = (f32[32,512]{1,0:T(8,128)}, f32[32,512]{1,0:T(8,128)S(1)}, f32[19,32,512]{2,0,1:T(8,128)S(1)}, f32[19,32,512]{2,0,1:T(8,128)S(1)}, f32[19,32,512]{2,0,1:T(8,128)}) fusion(f32[19]{0:T(128)S(1)} %copy-done.25, f32[19,32,512]{2,1,0:T(8,128)} %gather_fusion, f32[32,512]{1,0:T(8,128)} %param.12, f32[19,32,512]{2,0,1:T(8,128)S(1)} %stack.2, ...), kind=kOutput, calls=%fused_computation.26 | convolution fusion | flops 17088512 | bytes 8061232 | tf_op jit(solution)/shard_map/qk,kxw->qxw/dot_general | solution.py:66
  43.6 2.2 fusion.33
  45.8 1.8 copy.54
  47.6 3.0 gather_fusion.1
  50.6 3.0 fusion.12
  53.6 8.0 %collective-permute-start.5 = (f32[1,512]{1,0:T(1,128)S(1)}, f32[1,512]{1,0:T(1,128)S(1)}, u32[]{:S(2)}, u32[]{:S(2)}) collective-permute-start(f32[1,512]{1,0:T(1,128)S(1)} %get-tuple-element.69), channel_id=1, source_target_pairs={{8,0},{16,8},{24,16},{32,24},{40,32},{48,40},{56,48},{64,56},{72,6... | collective-permute-start | bytes 6152 | tf_op jit(solution)/shard_map/ppermute | solution.py:52
  62.4 1.3 collective-permute-done.4
  63.8 1.3 collective-permute-start.7
  65.1 4.0 collective-permute-start.6
  70.7 85.9 %all-reduce.7 = (f32[]{:T(128)}, f32[]{:T(128)}) all-reduce(f32[]{:T(128)} %get-tuple-element.9, f32[]{:T(128)} %get-tuple-element.8), channel_id=1, replica_groups=mesh['gx'=32,'gy'=8] {'gx','gy'}, use_global_device_ids=true, to_apply=%region_6.7 | all-reduce | flops 2 | bytes 16 | tf_op jit(solution)/shard_map/psum | solution.py:129
  158.5 73.4 %psum.44 = f32[]{:T(128)} all-reduce(f32[]{:T(128)} %get-tuple-element.14), channel_id=1, replica_groups=mesh['gx'=32,'gy'=8] {'gx','gy'}, use_global_device_ids=true, to_apply=%region_10.11 | all-reduce | flops 1 | bytes 8 | tf_op jit(solution)/shard_map/psum | solution.py:129
  235.1 3.4 fusion.30
  238.6 1.4 collective-permute-start.11
  240.0 4.0 collective-permute-start.10
  245.7 80.7 %psum.45 = f32[]{:T(128)} all-reduce(f32[]{:T(128)} %get-tuple-element.12), channel_id=1, replica_groups=mesh['gx'=32,'gy'=8] {'gx','gy'}, use_global_device_ids=true, to_apply=%region_12.13 | all-reduce | flops 1 | bytes 8 | tf_op jit(solution)/shard_map/psum | solution.py:133
  328.3 73.4 %psum.46 = f32[]{:T(128)} all-reduce(f32[]{:T(128)} %multiply_reduce_fusion.3), channel_id=1, replica_groups=mesh['gx'=32,'gy'=8] {'gx','gy'}, use_global_device_ids=true, to_apply=%region_14.15 | all-reduce | flops 1 | bytes 8 | tf_op jit(solution)/shard_map/psum | solution.py:129
  405.0 3.4 copy_select_fusion
  408.5 1.3 collective-permute-start.15
  409.7 4.0 collective-permute-start.14
  415.4 1.8 copy.56
  417.2 80.9 %psum.47 = f32[]{:T(128)} all-reduce(f32[]{:T(128)} %fusion.44), channel_id=1, replica_groups=mesh['gx'=32,'gy'=8] {'gx','gy'}, use_global_device_ids=true, to_apply=%region_16.17 | all-reduce | flops 1 | bytes 8 | tf_op jit(solution)/shard_map/psum | solution.py:133
  (110 shorter events, 22.7 us)
Async XLA Ops:
  0.6 6.8 %copy-start.26 = (s32[19]{0:T(128)S(1)}, s32[19]{0:T(128)}, u32[]{:S(2)}) copy-start(s32[19]{0:T(128)} %constant.89) | copy-start | bytes 232
  0.6 6.0 %copy-start.2 = (f32[19,32,512]{2,1,0:T(8,128)S(1)}, f32[19,32,512]{2,1,0:T(8,128)}, u32[]{:S(2)}) copy-start(f32[19,32,512]{2,1,0:T(8,128)} %param.11) | copy-start | bytes 3735556
  2.8 6.1 %copy-start.18 = (f32[19,3,1]{0,1,2:T(4,128)S(1)}, f32[19,3,1]{0,1,2:T(4,128)}, u32[]{:S(2)}) copy-start(f32[19,3,1]{0,1,2:T(4,128)} %constant.91) | copy-start | bytes 688
  3.4 10.5 %collective-permute-start.1 = (f32[19,1,512]{2,0,1:T(8,128)}, f32[19,1,512]{2,0,1:T(8,128)}, u32[]{:S(2)}, u32[]{:S(2)}) collective-permute-start(f32[19,1,512]{2,0,1:T(8,128)} %get-tuple-element.41), channel_id=1, source_target_pairs={{0,8},{8,16},{16,24},{24,32},{32,40},{40,48},{48,56},{56,64},{64,7... | collective-permute-start | bytes 116744 | tf_op jit(solution)/shard_map/ppermute | solution.py:50
  6.5 9.0 %collective-permute-start = (f32[19,1,512]{2,0,1:T(8,128)}, f32[19,1,512]{2,0,1:T(8,128)}, u32[]{:S(2)}, u32[]{:S(2)}) collective-permute-start(f32[19,1,512]{2,0,1:T(8,128)} %get-tuple-element.42), channel_id=1, source_target_pairs={{8,0},{16,8},{24,16},{32,24},{40,32},{48,40},{56,48},{64,56},{72,6... | collective-permute-start | bytes 116744 | tf_op jit(solution)/shard_map/ppermute | solution.py:52
  11.9 24.9 %copy-start.4 = (f32[3,32,512]{2,0,1:T(4,128)}, f32[3,32,512]{2,0,1:T(4,128)S(1)}, u32[]{:S(2)}) copy-start(f32[3,32,512]{2,0,1:T(4,128)S(1)} %get-tuple-element.76) | copy-start | bytes 589828
  16.4 8.0 %collective-permute-start.3 = (f32[19,34,16]{2,0,1:T(8,128)S(1)}, f32[19,34,16]{2,0,1:T(8,128)S(1)}, u32[]{:S(2)}, u32[]{:S(2)}) collective-permute-start(f32[19,34,16]{2,0,1:T(8,128)S(1)} %get-tuple-element.36), channel_id=1, source_target_pairs={{0,1},{1,2},{2,3},{3,4},{4,5},{5,6},{6,7},{8,9},{9,10},{10,11},{11... | collective-permute-start | bytes 124040 | tf_op jit(solution)/shard_map/ppermute | solution.py:50
  19.5 8.8 %collective-permute-start.2 = (f32[19,34,16]{2,0,1:T(8,128)S(1)}, f32[19,34,16]{2,0,1:T(8,128)S(1)}, u32[]{:S(2)}, u32[]{:S(2)}) collective-permute-start(f32[19,34,16]{2,0,1:T(8,128)S(1)} %get-tuple-element.37), channel_id=1, source_target_pairs={{1,0},{2,1},{3,2},{4,3},{5,4},{6,5},{7,6},{9,8},{10,9},{11,10},{12... | collective-permute-start | bytes 124040 | tf_op jit(solution)/shard_map/ppermute | solution.py:52
  22.4 6.8 %copy-start.13 = (f32[1,32,512]{2,1,0:T(8,128)S(1)}, f32[1,32,512]{2,1,0:T(8,128)}, u32[]{:S(2)}) copy-start(f32[1,32,512]{2,1,0:T(8,128)} %get-tuple-element.50) | copy-start | bytes 196612
  22.4 6.8 %copy-start.14 = (f32[1,32,512]{2,1,0:T(8,128)S(1)}, f32[1,32,512]{2,1,0:T(8,128)}, u32[]{:S(2)}) copy-start(f32[1,32,512]{2,1,0:T(8,128)} %get-tuple-element.51) | copy-start | bytes 196612
  50.6 11.0 %copy-start.16 = (f32[32,512]{1,0:T(8,128)S(1)}, f32[32,512]{1,0:T(8,128)}, u32[]{:S(2)}) copy-start(f32[32,512]{1,0:T(8,128)} %copy-done.15) | copy-start | bytes 196612
  50.6 19.4 %copy-start.19 = (pred[512]{0:T(512)(128)(4,1)S(1)}, pred[512]{0:T(512)(128)(4,1)}, u32[]{:S(2)}) copy-start(pred[512]{0:T(512)(128)(4,1)} %get-tuple-element.82) | copy-start | bytes 1540
  50.6 19.4 %copy-start.22 = (pred[512]{0:T(512)(128)(4,1)S(1)}, pred[512]{0:T(512)(128)(4,1)}, u32[]{:S(2)}) copy-start(pred[512]{0:T(512)(128)(4,1)} %get-tuple-element.83) | copy-start | bytes 1540
  53.6 181.5 %copy-start.3 = (f32[19,32,512]{2,0,1:T(8,128)S(1)}, f32[19,32,512]{2,0,1:T(8,128)}, u32[]{:S(2)}) copy-start(f32[19,32,512]{2,0,1:T(8,128)} %get-tuple-element.77) | copy-start | bytes 3735556
  53.6 8.8 %collective-permute-start.5 = (f32[1,512]{1,0:T(1,128)S(1)}, f32[1,512]{1,0:T(1,128)S(1)}, u32[]{:S(2)}, u32[]{:S(2)}) collective-permute-start(f32[1,512]{1,0:T(1,128)S(1)} %get-tuple-element.69), channel_id=1, source_target_pairs={{8,0},{16,8},{24,16},{32,24},{40,32},{48,40},{56,48},{64,56},{72,6... | collective-permute-start | bytes 6152 | tf_op jit(solution)/shard_map/ppermute | solution.py:52
  61.6 2.1 collective-permute-start.4
  63.8 5.4 %collective-permute-start.7 = (f32[34,16]{1,0:T(8,128)S(1)}, f32[34,16]{1,0:T(8,128)S(1)}, u32[]{:S(2)}, u32[]{:S(2)}) collective-permute-start(f32[34,16]{1,0:T(8,128)S(1)} %get-tuple-element.59), channel_id=1, source_target_pairs={{1,0},{2,1},{3,2},{4,3},{5,4},{6,5},{7,6},{9,8},{10,9},{11,10},{12... | collective-permute-start | bytes 6536 | tf_op jit(solution)/shard_map/ppermute | solution.py:52
  65.1 4.9 collective-permute-start.6
  233.3 5.3 %collective-permute-start.9 = (f32[1,512]{1,0:T(1,128)S(1)}, f32[1,512]{1,0:T(1,128)S(1)}, u32[]{:S(2)}, u32[]{:S(2)}) collective-permute-start(f32[1,512]{1,0:T(1,128)S(1)} %get-tuple-element.65), channel_id=1, source_target_pairs={{8,0},{16,8},{24,16},{32,24},{40,32},{48,40},{56,48},{64,56},{72,6... | collective-permute-start | bytes 6152 | tf_op jit(solution)/shard_map/ppermute | solution.py:52
  234.0 4.5 collective-permute-start.8
  235.1 9.8 %copy-start.20 = (pred[512]{0:T(512)(128)(4,1)S(1)}, pred[512]{0:T(512)(128)(4,1)}, u32[]{:S(2)}) copy-start(pred[512]{0:T(512)(128)(4,1)} %get-tuple-element.82) | copy-start | bytes 1540
  235.1 9.8 %copy-start.23 = (pred[512]{0:T(512)(128)(4,1)S(1)}, pred[512]{0:T(512)(128)(4,1)}, u32[]{:S(2)}) copy-start(pred[512]{0:T(512)(128)(4,1)} %get-tuple-element.83) | copy-start | bytes 1540
  235.1 93.2 %copy-start.5 = (f32[32,512]{1,0:T(8,128)S(1)}, f32[32,512]{1,0:T(8,128)}, u32[]{:S(2)}) copy-start(f32[32,512]{1,0:T(8,128)} %get-tuple-element.6) | copy-start | bytes 196612
  238.5 166.4 %copy-start = (f32[19,32,512]{2,1,0:T(8,128)S(1)}, f32[19,32,512]{2,1,0:T(8,128)}, u32[]{:S(2)}) copy-start(f32[19,32,512]{2,1,0:T(8,128)} %gather_fusion) | copy-start | bytes 3735556
  238.6 5.5 %collective-permute-start.11 = (f32[34,16]{1,0:T(8,128)S(1)}, f32[34,16]{1,0:T(8,128)S(1)}, u32[]{:S(2)}, u32[]{:S(2)}) collective-permute-start(f32[34,16]{1,0:T(8,128)S(1)} %get-tuple-element.57), channel_id=1, source_target_pairs={{1,0},{2,1},{3,2},{4,3},{5,4},{6,5},{7,6},{9,8},{10,9},{11,10},{12... | collective-permute-start | bytes 6536 | tf_op jit(solution)/shard_map/ppermute | solution.py:52
  240.0 4.9 collective-permute-start.10
  403.1 5.2 %collective-permute-start.13 = (f32[1,512]{1,0:T(1,128)S(1)}, f32[1,512]{1,0:T(1,128)S(1)}, u32[]{:S(2)}, u32[]{:S(2)}) collective-permute-start(f32[1,512]{1,0:T(1,128)S(1)} %get-tuple-element.63), channel_id=1, source_target_pairs={{8,0},{16,8},{24,16},{32,24},{40,32},{48,40},{56,48},{64,56},{72,6... | collective-permute-start | bytes 6152 | tf_op jit(solution)/shard_map/ppermute | solution.py:52
  403.9 4.5 collective-permute-start.12
  405.0 9.7 %copy-start.21 = (pred[512]{0:T(512)(128)(4,1)S(1)}, pred[512]{0:T(512)(128)(4,1)}, u32[]{:S(2)}) copy-start(pred[512]{0:T(512)(128)(4,1)} %get-tuple-element.82) | copy-start | bytes 1540
  405.0 9.7 %copy-start.24 = (pred[512]{0:T(512)(128)(4,1)S(1)}, pred[512]{0:T(512)(128)(4,1)}, u32[]{:S(2)}) copy-start(pred[512]{0:T(512)(128)(4,1)} %get-tuple-element.83) | copy-start | bytes 1540
  408.5 5.4 %collective-permute-start.15 = (f32[34,16]{1,0:T(8,128)S(1)}, f32[34,16]{1,0:T(8,128)S(1)}, u32[]{:S(2)}, u32[]{:S(2)}) collective-permute-start(f32[34,16]{1,0:T(8,128)S(1)} %get-tuple-element.55), channel_id=1, source_target_pairs={{1,0},{2,1},{3,2},{4,3},{5,4},{6,5},{7,6},{9,8},{10,9},{11,10},{12... | collective-permute-start | bytes 6536 | tf_op jit(solution)/shard_map/ppermute | solution.py:52
  409.7 4.9 collective-permute-start.14
  (11 other events, 24.0 us)
where the time goes:
time: 502 us; the launch traced here: 500 us
  blocking collectives  394 us (78%)
  starting transfers between devices  35.3 us (7%)
  matrix products  18.8 us (4%)
  local copies, waits for them, and re-layouts  18.2 us (4%)
  other arithmetic  16.3 us (3%)
  waiting for transfers between devices  9.7 us (2%)
  between operations  7.57 us (2%)
    psum x3, blocking collectives, squares(): return lax.psum(jnp.sum(residual * residual), ('gx', 'gy'))  233 us
    psum x2, blocking collectives, curvature_sum(): return lax.psum(jnp.sum(product), ('gx', 'gy'))  162 us
    ppermute x8, starting transfers between devices, padded_2(): lax.ppermute(tail, axis, [(i, (i + 1) % count) for i in range(ends)])  20.2 us
    ppermute x8, starting transfers between devices, padded_2(): lax.ppermute(head, axis, [((i + 1) % count, i) for i in range(ends)])  15.1 us
  transfers between devices with their start and end apart: 16, of which 7 were waited for; matrix products, arithmetic and copies ran while one was open for 4% of the time, Pallas kernels for 0%

commit v1 on v0

--- a/solution.py
+++ b/solution.py
@@ -107,66 +107,97 @@
     return jnp.stack(pulled)
 
 
-def stencil_core(padded_field):
-    rows, width = padded_field.shape
-    inner_width = width - 2 * NZ
-    center = padded_field[1:-1, NZ : NZ + inner_width]
-    beside = padded_field[:-2, NZ : NZ + inner_width] + padded_field[2:, NZ : NZ + inner_width]
-    beside = beside + padded_field[1:-1, :inner_width] + padded_field[1:-1, 2 * NZ :]
-    depth_index = jnp.arange(inner_width) % NZ
-    above = jnp.where(depth_index < NZ - 1, jnp.pad(center[:, 1:], ((0, 0), (0, 1))), 0.0)
-    below = jnp.where(depth_index > 0, jnp.pad(center[:, :-1], ((0, 0), (1, 0))), 0.0)
-    return (1.0 + 6.0 * radius_sq) * center - radius_sq * (beside + above + below)
-
-
-def helmholtz(values):
-    wide = padded_2(values, (("gx", 0),), 1, True)
-    padded = padded_2(wide, (("gy", 1),), NZ, False)
-    return stencil_core(padded)
-
-
-def squares(residual):
-    return lax.psum(jnp.sum(residual * residual), ("gx", "gy"))
-
-
-def curvature_sum(product):
-    return lax.psum(jnp.sum(product), ("gx", "gy"))
-
-
-def solve_filter(sensitivity, apply_op, trim, inner):
-    depth = ITERS
-    filtered = jnp.zeros_like(sensitivity)
-    residual = sensitivity
-    direction = sensitivity
-    norm_now = squares(inner(residual, depth))
+def laplace(field, depth_index, inside):
+    left = jnp.where(depth_index > 0, jnp.pad(field[:, :-1], ((0, 0), (1, 0))), 0.0)
+    right = jnp.where(depth_index < NZ - 1, jnp.pad(field[:, 1:], ((0, 0), (0, 1))), 0.0)
+    center = field[1:-1, NZ:-NZ]
+    total = field[:-2, NZ:-NZ] + field[2:, NZ:-NZ]
+    total = total + field[1:-1, : -2 * NZ] + field[1:-1, 2 * NZ :]
+    total = total + left[1:-1, NZ:-NZ] + right[1:-1, NZ:-NZ]
+    return jnp.where(inside, center - total * (1.0 / 6.0), 0.0)
+
+
+def total_over_devices(row):
+    size = lax.axis_size("gx") * lax.axis_size("gy")
+    copies = jnp.broadcast_to(row[None], (size,) + row.shape)
+    return jnp.sum(lax.all_to_all(copies, ("gx", "gy"), 0, 0), axis=0)
+
+
+def times_h(poly):
+    top = 1.0 + 6.0 * radius_sq - 1.0
+    out = list(poly) + [0.0]
+    for power, entry in enumerate(poly):
+        out[power + 1] = out[power + 1] + top * entry
+    return out
+
+
+def dot_poly(p, q, moments):
+    total = 0.0
+    for i, left in enumerate(p):
+        for j, right in enumerate(q):
+            total = total + left * right * moments[i + j]
+    return total
+
+
+def combination(moments):
+    upper = 1.0 + 12.0 * radius_sq
+    growth = (upper - 1.0) ** 2 / (4.0 * upper) * 1.001
+    zero, one = jnp.zeros_like(moments[0]), jnp.ones_like(moments[0])
+    solved, residual, direction = [zero], [one], [one]
+    norm_now = moments[0]
     for iteration in range(ITERS):
-        applied = apply_op(direction, depth)
-        depth = depth - 1
-        direction, residual, filtered = (trim(direction), trim(residual), trim(filtered))
-        step_size = norm_now / curvature_sum(inner(direction * applied, depth))
-        filtered = filtered + step_size * direction
-        residual = residual - step_size * applied
-        norm_next = squares(inner(residual, depth))
-        direction = residual + norm_next / norm_now * direction
-        norm_now = norm_next
-    return filtered
+        image = times_h(direction)
+        step = norm_now / dot_poly(direction, image, moments)
+        step = jnp.clip(step, 1.0 / upper, 1.0)
+        solved = [
+            (solved[k] if k < len(solved) else 0.0) + step * direction[k]
+            for k in range(len(direction))
+        ]
+        if iteration == ITERS - 1:
+            break
+        residual = [
+            (residual[k] if k < len(residual) else 0.0) - step * image[k] for k in range(len(image))
+        ]
+        norm_next = dot_poly(residual, residual, moments)
+        ratio = jnp.clip(norm_next / norm_now, 0.0, growth)
+        direction = [
+            residual[k] + (ratio * direction[k] if k < len(direction) else 0.0)
+            for k in range(len(residual))
+        ]
+        norm_now = jnp.maximum(norm_next, 0.0)
+    return solved
+
+
+def solve_filter(sensitivity):
+    layers, columns = sensitivity.shape
+    wide = padded_2(sensitivity, (("gx", 0),), ITERS, True)
+    wide = padded_2(wide, (("gy", 1),), ITERS * NZ, False)
+    place = lax.axis_index("gy")
+    vectors = [wide]
+    for power in range(ITERS):
+        margin = (ITERS - power) * NZ
+        column = jnp.arange(columns + 2 * margin)
+        depth_index = column % NZ
+        inner = column[NZ:-NZ] - margin + place * columns
+        inside = (inner >= 0) & (inner < columns * lax.axis_size("gy"))
+        vectors.append(laplace(vectors[-1], depth_index, inside))
+    cores = []
+    for power, field in enumerate(vectors):
+        margin = ITERS - power
+        cores.append(field[margin : margin + layers, margin * NZ : margin * NZ + columns])
+    pairs = [(0, 0), (0, 1), (1, 1), (1, 2), (2, 2), (2, 3)]
+    local = jnp.stack([jnp.sum(cores[i] * cores[j]) for i, j in pairs])
+    row = jnp.pad(local, (0, 128 - len(pairs)))[None]
+    moments = total_over_devices(row)[0]
+    weights = combination([moments[k] for k in range(len(pairs))])
+    return sum(weight * core for weight, core in zip(weights, cores))
 
 
 def shards(forward, adjoint, design, node_type):
     populations, layers, columns = adjoint.shape
     read = pull_bordered(gather_faces(adjoint), layers, columns)
     adjoint_new, sensitivity = adjoint_cell(read, forward, design, node_type)
-
-    def apply_plain(field, depth):
-        return helmholtz(field)
-
-    def keep(field):
-        return field
-
-    def whole(field, depth):
-        return field
-
-    filtered = solve_filter(sensitivity, apply_plain, keep, whole)
+    filtered = solve_filter(sensitivity)
     return (adjoint_new, filtered)
 
 

time: 502 us -> 132 us (0.26)
  blocking collectives: 394 us -> 0 us
  between operations: 7.57 us -> 20.8 us
  local copies, waits for them, and re-layouts: 18.2 us -> 23.8 us
    psum x5 -> x0, blocking collectives: 394 us -> none  [the longest x3 233 us: squares(): return lax.psum(jnp.sum(residual * residual), ('gx', 'gy'))]
    all_to_all x0 -> x1, starting transfers between devices: none -> 19.4 us  [total_over_devices(): return jnp.sum(lax.all_to_all(copies, ('gx', 'gy'), 0, 0), axis=0)]
    ppermute x8 -> x4, starting transfers between devices: 20.2 us -> 10 us  [padded_2(): lax.ppermute(tail, axis, [(i, (i + 1) % count) for i in range(ends)])]
    all_to_all x0 -> x1, waiting for transfers between devices: none -> 7.57 us  [total_over_devices(): return jnp.sum(lax.all_to_all(copies, ('gx', 'gy'), 0, 0), axis=0)]
    ppermute x8 -> x4, starting transfers between devices: 15.1 us -> 10.6 us  [padded_2(): lax.ppermute(head, axis, [((i + 1) % count, i) for i in range(ends)])]
  transfers between devices with their start and end apart: 16 -> 9, of which waited for: 7 -> 4; matrix products, arithmetic and copies ran while one was open for 4% -> 14% of each run, Pallas kernels for 0% -> 0%
where the time goes in v1:
time: 132 us; the launch traced here: 131 us
  starting transfers between devices  40 us (30%)
  local copies, waits for them, and re-layouts  23.8 us (18%)
  between operations  20.8 us (16%)
  matrix products  18 us (14%)
  other arithmetic  15.1 us (11%)
  waiting for transfers between devices  13.7 us (10%)
    all_to_all x1, starting transfers between devices, total_over_devices(): return jnp.sum(lax.all_to_all(copies, ('gx', 'gy'), 0, 0), axis=0)  19.4 us
    ppermute x4, starting transfers between devices, padded_2(): lax.ppermute(head, axis, [((i + 1) % count, i) for i in range(ends)])  10.6 us
    ppermute x4, starting transfers between devices, padded_2(): lax.ppermute(tail, axis, [(i, (i + 1) % count) for i in range(ends)])  10 us
    all_to_all x1, waiting for transfers between devices, total_over_devices(): return jnp.sum(lax.all_to_all(copies, ('gx', 'gy'), 0, 0), axis=0)  7.57 us
    dot_general x1, matrix products, adjoint_cell(): projected = jnp.einsum('qk,kxw->qxw', table, velocity, precision=highest)  6.95 us
    unnamed x58, local copies, waits for them, and re-layouts  5.74 us
    ppermute x4, waiting for transfers between devices, padded_2(): lax.ppermute(head, axis, [((i + 1) % count, i) for i in range(ends)])  3.85 us
    another operation x1, local copies, waits for them, and re-layouts, solve_filter(): local = jnp.stack([jnp.sum(cores[i] * cores[j]) for i, j in pairs])  3.72 us
  transfers between devices with their start and end apart: 9, of which 4 were waited for; matrix products, arithmetic and copies ran while one was open for 14% of the time, Pallas kernels for 0%

profile of v1, /device:TPU:1, one launch (start us, length us, event | category | flops | bytes accessed | tf_op | source)
XLA Modules:
  0.0 131.4 jit_solution(7343149692818010933)
XLA Ops:
  0.7 2.1 %copy.83 = f32[19,32,512]{2,0,1:T(8,128)S(1)} copy(f32[19,32,512]{2,1,0:T(8,128)} %param.11) | data formatting | bytes 2490368 | tf_op args[1]
  3.5 3.0 %collective-permute-start.1 = (f32[19,1,512]{2,0,1:T(8,128)}, f32[19,1,512]{2,0,1:T(8,128)}, u32[]{:S(2)}, u32[]{:S(2)}) collective-permute-start(f32[19,1,512]{2,0,1:T(8,128)} %get-tuple-element.42), channel_id=1, source_target_pairs={{0,8},{8,16},{16,24},{24,32},{32,40},{40,48},{48,56},{56,64},{64,7... | collective-permute-start | bytes 116744 | tf_op jit(solution)/shard_map/ppermute | solution.py:50
  6.7 0.8 fusion.79
  7.8 1.4 %reduce_sum.111 = f32[32,512]{1,0:T(8,128)S(1)} reduce(f32[19,32,512]{2,1,0:T(8,128)} %param.10, f32[]{:T(128)} %constant.42.clone.1), dimensions={0}, to_apply=%region_1.2 | reduce | flops 294912 | bytes 1310724 | tf_op jit(solution)/shard_map/reduce_sum | solution.py:63
  9.3 3.0 %multiply_reduce_fusion.2 = (f32[32,512]{1,0:T(8,128)S(1)}, f32[3,32,512]{2,0,1:T(4,128)S(1)}) fusion(f32[32,512]{1,0:T(8,128)S(1)} %reduce_sum.111, f32[19,3,1]{0,1,2:T(4,128)S(1)} %copy-done.24, f32[19,32,512]{2,1,0:T(8,128)} %param.10), kind=kOutput, calls=%fused_computation.41 | convolution fusion | flops 11337728 | bytes 1573092 | tf_op jit(solution)/shard_map/qk,qxw->kxw/dot_general | solution.py:64
  14.1 0.8 constant_dynamic-update-slice_fusion.1
  15.7 0.8 constant_dynamic-update-slice_fusion
  16.7 3.0 %collective-permute-start.3 = (f32[19,34,16]{2,0,1:T(8,128)S(1)}, f32[19,34,16]{2,0,1:T(8,128)S(1)}, u32[]{:S(2)}, u32[]{:S(2)}) collective-permute-start(f32[19,34,16]{2,0,1:T(8,128)S(1)} %get-tuple-element.37), channel_id=1, source_target_pairs={{0,1},{1,2},{2,3},{3,4},{4,5},{5,6},{6,7},{8,9},{9,10},{10,11},{11... | collective-permute-start | bytes 124040 | tf_op jit(solution)/shard_map/ppermute | solution.py:50
  19.7 1.5 %collective-permute-start.2 = (f32[19,34,16]{2,0,1:T(8,128)S(1)}, f32[19,34,16]{2,0,1:T(8,128)S(1)}, u32[]{:S(2)}, u32[]{:S(2)}) collective-permute-start(f32[19,34,16]{2,0,1:T(8,128)S(1)} %get-tuple-element.38), channel_id=1, source_target_pairs={{1,0},{2,1},{3,2},{4,3},{5,4},{6,5},{7,6},{9,8},{10,9},{11,10},{12... | collective-permute-start | bytes 124040 | tf_op jit(solution)/shard_map/ppermute | solution.py:52
  21.2 1.5 %pad_maximum_fusion.9 = (f32[1,32,512]{2,0,1:T(1,128)S(1)}, f32[1,32,512]{2,0,1:T(1,128)}) fusion(f32[19,32,512]{2,0,1:T(8,128)S(1)} %copy.83, f32[19,1,512]{2,0,1:T(8,128)} %collective-permute-done.1, f32[19,1,512]{2,0,1:T(8,128)} %collective-permute-done), kind=kLoop, calls=%fused_computation.94 | loop fusion | flops 32768 | bytes 1454080 | tf_op jit(solution)/shard_map/concatenate | solution.py:48
  22.6 2.0 %collective-permute-done.3 = f32[19,34,16]{2,0,1:T(8,128)S(1)} collective-permute-done((f32[19,34,16]{2,0,1:T(8,128)S(1)}, f32[19,34,16]{2,0,1:T(8,128)S(1)}, u32[]{:S(2)}, u32[]{:S(2)}) %collective-permute-start.3) | collective-permute-done | bytes 41376 | tf_op jit(solution)/shard_map/ppermute | solution.py:50
  24.6 3.8 %collective-permute-done.2 = f32[19,34,16]{2,0,1:T(8,128)S(1)} collective-permute-done((f32[19,34,16]{2,0,1:T(8,128)S(1)}, f32[19,34,16]{2,0,1:T(8,128)S(1)}, u32[]{:S(2)}, u32[]{:S(2)}) %collective-permute-start.2) | collective-permute-done | bytes 41376 | tf_op jit(solution)/shard_map/ppermute | solution.py:52
  28.5 0.9 select_maximum_fusion
  30.4 1.2 broadcast_select_fusion.7
  31.6 1.1 broadcast_select_fusion.2
  32.7 2.0 %stack.16 = f32[19,32,512]{2,0,1:T(8,128)S(1)} concatenate(f32[1,32,512]{2,0,1:T(1,128)S(1)} %copy-done.17, f32[1,32,512]{2,0,1:T(1,128)S(1)} %copy-done.12, f32[1,32,512]{2,0,1:T(1,128)S(1)} %get-tuple-element.40, f32[1,32,512]{2,0,1:T(1,128)S(1)} %get-tuple-element.36, f32[1,32,512]{2,0,1:T(1,128)S(1)} %get-tuple-element.35, f32[1,32,512]{2,0,1:T(1,128)S(1)} %get-tuple-element.23, ...), dimensions={0} | concatenate | bytes 2490368 | tf_op jit(solution)/shard_map/stack | solution.py:107
  35.5 1.7 %gather_fusion = f32[19,32,512]{2,1,0:T(8,128)} fusion(f32[19,32,512]{2,1,0:T(8,128)S(1)} %copy.98, s32[1024]{0:T(1024)S(1)} %pad_clamp_fusion), kind=kCustom, calls=%fused_computation | custom fusion | bytes 2490444 | tf_op jit(solution)/shard_map/gather | solution.py:74
  37.1 6.9 %multiply_reduce_fusion = (f32[32,512]{1,0:T(8,128)}, f32[32,512]{1,0:T(8,128)S(1)}, f32[19,32,512]{2,0,1:T(8,128)S(1)}, f32[19,32,512]{2,0,1:T(8,128)S(1)}, f32[19,32,512]{2,0,1:T(8,128)}) fusion(f32[19]{0:T(128)S(1)} %copy-done.25, f32[19,32,512]{2,1,0:T(8,128)} %gather_fusion, f32[32,512]{1,0:T(8,128)} %param.12, f32[19,32,512]{2,0,1:T(8,128)S(1)} %stack.16, ...), kind=kOutput, calls=%fused_computation.26 | convolution fusion | flops 17088512 | bytes 8061232 | tf_op jit(solution)/shard_map/qk,kxw->qxw/dot_general | solution.py:66
  44.1 2.3 %fusion.33 = f32[32,512,3]{1,2,0:T(4,128)} fusion(f32[19,3,1]{0,1,2:T(4,128)S(1)} %copy-done.24, f32[19,32,512]{2,0,1:T(8,128)S(1)} %get-tuple-element.20, f32[19]{0:T(128)S(1)} %copy-done.25), kind=kOutput, calls=%fused_computation.38 | convolution fusion | flops 11567104 | bytes 1442096 | tf_op jit(solution)/shard_map/qk,qxw->kxw/dot_general | solution.py:77
  47.1 1.8 %copy.104 = f32[19,32,512]{2,1,0:T(8,128)} copy(f32[19,32,512]{2,0,1:T(8,128)S(1)} %get-tuple-element.39) | data formatting | bytes 2490368 | tf_op jit(solution)/shard_map/sub | solution.py:71
  48.9 3.0 %gather_fusion.1 = f32[19,32,512]{2,1,0:T(8,128)} fusion(f32[19,32,512]{2,1,0:T(8,128)} %copy.104, s32[1024]{0:T(1024)S(1)} %pad_clamp_fusion), kind=kCustom, calls=%fused_computation.1 | custom fusion | bytes 2490444 | tf_op jit(solution)/shard_map/gather | solution.py:73
  51.9 3.1 %fusion.12 = f32[32,512]{1,0:T(8,128)S(1)} fusion(f32[19,32,512]{2,0,1:T(8,128)S(1)} %stack.16, f32[19,32,512]{2,0,1:T(8,128)} %copy-done.1, f32[19,32,512]{2,1,0:T(8,128)} %gather_fusion.1), kind=kLoop, calls=%fused_computation.25 | loop fusion | flops 917504 | bytes 3801088 | tf_op jit(solution)/shard_map/reduce_sum | solution.py:73
  55.6 7.7 %collective-permute-start.5 = (f32[3,512]{1,0:T(4,128)S(1)}, f32[3,512]{1,0:T(4,128)S(1)}, u32[]{:S(2)}, u32[]{:S(2)}) collective-permute-start(f32[3,512]{1,0:T(4,128)S(1)} %get-tuple-element.64), channel_id=1, source_target_pairs={{8,0},{16,8},{24,16},{32,24},{40,32},{48,40},{56,48},{64,56},{72,6... | collective-permute-start | bytes 18440 | tf_op jit(solution)/shard_map/ppermute | solution.py:52
  63.3 2.4 %fusion.30 = f32[3,32,512]{2,0,1:T(4,128)} fusion(f32[32,512,3]{1,2,0:T(4,128)S(1)} %copy-done.5, f32[19,3,1]{0,1,2:T(4,128)S(1)} %copy-done.24, f32[19,32,512]{2,0,1:T(8,128)S(1)} %copy-done.3, f32[19,32,512]{2,0,1:T(8,128)S(1)} %get-tuple-element.20, f32[19]{0:T(128)S(1)} %copy-done.25, f32[3,32,512]{2,0,1:T(4,128)S(1)} %get-tuple-element.75, ...), kind=kOutput, calls=%fused_computation.37 | convolution fusion | flops 12025856 | bytes 3146032 | tf_op jit(solution)/shard_map/qk,qxw->kxw/dot_general | solution.py:78
  65.8 1.3 collective-permute-start.7
  67.1 4.0 %collective-permute-start.6 = (f32[38,48]{1,0:T(8,128)S(1)}, f32[38,48]{1,0:T(8,128)S(1)}, u32[]{:S(2)}, u32[]{:S(2)}) collective-permute-start(f32[38,48]{1,0:T(8,128)S(1)} %get-tuple-element.61), channel_id=1, source_target_pairs={{0,1},{1,2},{2,3},{3,4},{4,5},{5,6},{6,7},{8,9},{9,10},{10,11},{11... | collective-permute-start | bytes 21896 | tf_op jit(solution)/shard_map/ppermute | solution.py:50
  72.9 0.9 fusion.53
  73.7 3.7 %stack.41 = f32[6]{0:T(128)S(1)} concatenate(f32[1]{0:T(128)} %bitcast.3, f32[1]{0:T(128)} %bitcast.4, f32[1]{0:T(128)} %bitcast.5, f32[1]{0:T(128)} %bitcast.6, f32[1]{0:T(128)} %bitcast.7, f32[1]{0:T(128)} %bitcast.8), dimensions={0} | concatenate | bytes 48 | tf_op jit(solution)/shard_map/stack | solution.py:189
  78.2 19.4 %all-to-all-start = ((f32[256,1,128]{2,1,0:T(1,128)}), f32[256,1,128]{2,1,0:T(1,128)S(1)}, u32[]{:S(2)}, u32[]{:S(2)}) async-start(f32[256,1,128]{2,1,0:T(1,128)} %broadcast_in_dim.133), calls=%async_computation | async-start | bytes 262144 | tf_op jit(solution)/shard_map/all_to_all | solution.py:123
  97.6 3.4 %copy_select_fusion = f32[19,32,512]{2,0,1:T(8,128)S(1)} fusion(f32[19,32,512]{2,1,0:T(8,128)S(1)} %copy-done, f32[19,32,512]{2,0,1:T(8,128)S(1)} %get-tuple-element.20, f32[3,32,512]{2,0,1:T(4,128)S(1)} %copy-done.4, f32[19,3,1]{0,1,2:T(4,128)S(1)} %copy-done.24, f32[32,512]{1,0:T(8,128)} %get-tuple-element.65, f32[32,512]{1,0:T(8,128)} %get-tuple-element.66, ...), kind=kOutput, calls=%fused_computation.12 | convolution fusion | flops 13697024 | bytes 4210916 | tf_op jit(solution)/shard_map/qk,kxw->qxw/dot_general | solution.py:81
  100.9 1.8 %copy.107 = f32[19,32,512]{2,1,0:T(8,128)} copy(f32[19,32,512]{2,0,1:T(8,128)S(1)} %copy_select_fusion) | data formatting | bytes 2490368
  102.7 7.6 %all-to-all-done = f32[256,1,128]{2,1,0:T(1,128)S(1)} async-done(((f32[256,1,128]{2,1,0:T(1,128)}), f32[256,1,128]{2,1,0:T(1,128)S(1)}, u32[]{:S(2)}, u32[]{:S(2)}) %all-to-all-start) | async-done | bytes 131104 | tf_op jit(solution)/shard_map/all_to_all | solution.py:123
  (106 shorter events, 10.9 us)
Async XLA Ops:
  0.6 6.9 %copy-start.26 = (s32[19]{0:T(128)S(1)}, s32[19]{0:T(128)}, u32[]{:S(2)}) copy-start(s32[19]{0:T(128)} %constant.139) | copy-start | bytes 232
  0.6 6.1 %copy-start.2 = (f32[19,32,512]{2,1,0:T(8,128)S(1)}, f32[19,32,512]{2,1,0:T(8,128)}, u32[]{:S(2)}) copy-start(f32[19,32,512]{2,1,0:T(8,128)} %param.11) | copy-start | bytes 3735556
  2.8 6.4 %copy-start.24 = (f32[19,3,1]{0,1,2:T(4,128)S(1)}, f32[19,3,1]{0,1,2:T(4,128)}, u32[]{:S(2)}) copy-start(f32[19,3,1]{0,1,2:T(4,128)} %constant.141) | copy-start | bytes 688
  3.5 10.7 %collective-permute-start.1 = (f32[19,1,512]{2,0,1:T(8,128)}, f32[19,1,512]{2,0,1:T(8,128)}, u32[]{:S(2)}, u32[]{:S(2)}) collective-permute-start(f32[19,1,512]{2,0,1:T(8,128)} %get-tuple-element.42), channel_id=1, source_target_pairs={{0,8},{8,16},{16,24},{24,32},{32,40},{40,48},{48,56},{56,64},{64,7... | collective-permute-start | bytes 116744 | tf_op jit(solution)/shard_map/ppermute | solution.py:50
  6.5 9.2 %collective-permute-start = (f32[19,1,512]{2,0,1:T(8,128)}, f32[19,1,512]{2,0,1:T(8,128)}, u32[]{:S(2)}, u32[]{:S(2)}) collective-permute-start(f32[19,1,512]{2,0,1:T(8,128)} %get-tuple-element.43), channel_id=1, source_target_pairs={{8,0},{16,8},{24,16},{32,24},{40,32},{48,40},{56,48},{64,56},{72,6... | collective-permute-start | bytes 116744 | tf_op jit(solution)/shard_map/ppermute | solution.py:52
  7.8 4.5 %copy-start.10 = (f32[32,512]{1,0:T(8,128)S(1)}, f32[32,512]{1,0:T(8,128)}, u32[]{:S(2)}) copy-start(f32[32,512]{1,0:T(8,128)} %param.12) | copy-start | bytes 196612
  9.2 6.4 %copy-start.8 = (f32[32,512]{1,0:T(8,128)}, f32[32,512]{1,0:T(8,128)S(1)}, u32[]{:S(2)}) copy-start(f32[32,512]{1,0:T(8,128)S(1)} %reduce_sum.111) | copy-start | bytes 196612
  9.2 3.7 %copy-start.18 = (f32[1,32,512]{2,1,0:T(8,128)S(1)}, f32[1,32,512]{2,1,0:T(8,128)}, u32[]{:S(2)}) copy-start(f32[1,32,512]{2,1,0:T(8,128)} %get-tuple-element.53) | copy-start | bytes 196612
  12.3 3.4 %copy-start.21 = (f32[32,512]{1,0:T(8,128)}, f32[32,512]{1,0:T(8,128)S(1)}, u32[]{:S(2)}) copy-start(f32[32,512]{1,0:T(8,128)S(1)} %get-tuple-element.74) | copy-start | bytes 196612
  16.7 8.0 %collective-permute-start.3 = (f32[19,34,16]{2,0,1:T(8,128)S(1)}, f32[19,34,16]{2,0,1:T(8,128)S(1)}, u32[]{:S(2)}, u32[]{:S(2)}) collective-permute-start(f32[19,34,16]{2,0,1:T(8,128)S(1)} %get-tuple-element.37), channel_id=1, source_target_pairs={{0,1},{1,2},{2,3},{3,4},{4,5},{5,6},{6,7},{8,9},{9,10},{10,11},{11... | collective-permute-start | bytes 124040 | tf_op jit(solution)/shard_map/ppermute | solution.py:50
  19.7 8.8 %collective-permute-start.2 = (f32[19,34,16]{2,0,1:T(8,128)S(1)}, f32[19,34,16]{2,0,1:T(8,128)S(1)}, u32[]{:S(2)}, u32[]{:S(2)}) collective-permute-start(f32[19,34,16]{2,0,1:T(8,128)S(1)} %get-tuple-element.38), channel_id=1, source_target_pairs={{1,0},{2,1},{3,2},{4,3},{5,4},{6,5},{7,6},{9,8},{10,9},{11,10},{12... | collective-permute-start | bytes 124040 | tf_op jit(solution)/shard_map/ppermute | solution.py:52
  22.6 6.8 %copy-start.19 = (f32[1,32,512]{2,1,0:T(8,128)S(1)}, f32[1,32,512]{2,1,0:T(8,128)}, u32[]{:S(2)}) copy-start(f32[1,32,512]{2,1,0:T(8,128)} %get-tuple-element.51) | copy-start | bytes 196612
  22.6 6.8 %copy-start.20 = (f32[1,32,512]{2,1,0:T(8,128)S(1)}, f32[1,32,512]{2,1,0:T(8,128)}, u32[]{:S(2)}) copy-start(f32[1,32,512]{2,1,0:T(8,128)} %get-tuple-element.52) | copy-start | bytes 196612
  31.6 1.1 copy-start.12
  31.6 1.1 copy-start.17
  35.5 1.7 %copy-start.25 = (f32[19]{0:T(128)S(1)}, f32[19]{0:T(128)}, u32[]{:S(2)}) copy-start(f32[19]{0:T(128)} %constant.119.clone) | copy-start | bytes 232
  44.1 3.0 %copy-start.1 = (f32[19,32,512]{2,0,1:T(8,128)}, f32[19,32,512]{2,0,1:T(8,128)S(1)}, u32[]{:S(2)}) copy-start(f32[19,32,512]{2,0,1:T(8,128)S(1)} %get-tuple-element.39) | copy-start | bytes 3735556
  44.1 4.8 %copy-start.6 = (f32[32,512]{1,0:T(8,128)}, f32[32,512]{1,0:T(8,128)S(1)}, u32[]{:S(2)}) copy-start(f32[32,512]{1,0:T(8,128)S(1)} %get-tuple-element.11) | copy-start | bytes 196612
  44.1 2.3 %copy-start.22 = (f32[32,512]{1,0:T(8,128)S(1)}, f32[32,512]{1,0:T(8,128)}, u32[]{:S(2)}) copy-start(f32[32,512]{1,0:T(8,128)} %copy-done.21) | copy-start | bytes 196612
  51.8 3.1 %copy-start.23 = (s32[32,512]{1,0:T(8,128)S(1)}, s32[32,512]{1,0:T(8,128)}, u32[]{:S(2)}) copy-start(s32[32,512]{1,0:T(8,128)} %param.13) | copy-start | bytes 196612
  51.8 11.5 %copy-start.3 = (f32[19,32,512]{2,0,1:T(8,128)S(1)}, f32[19,32,512]{2,0,1:T(8,128)}, u32[]{:S(2)}) copy-start(f32[19,32,512]{2,0,1:T(8,128)} %get-tuple-element.76) | copy-start | bytes 3735556
  51.8 11.5 %copy-start.5 = (f32[32,512,3]{1,2,0:T(4,128)S(1)}, f32[32,512,3]{1,2,0:T(4,128)}, u32[]{:S(2)}) copy-start(f32[32,512,3]{1,2,0:T(4,128)} %fusion.33) | copy-start | bytes 589828
  51.8 11.5 %copy-start.11 = (f32[32,512]{1,0:T(8,128)S(1)}, f32[32,512]{1,0:T(8,128)}, u32[]{:S(2)}) copy-start(f32[32,512]{1,0:T(8,128)} %get-tuple-element.67) | copy-start | bytes 196612
  55.6 10.1 %collective-permute-start.5 = (f32[3,512]{1,0:T(4,128)S(1)}, f32[3,512]{1,0:T(4,128)S(1)}, u32[]{:S(2)}, u32[]{:S(2)}) collective-permute-start(f32[3,512]{1,0:T(4,128)S(1)} %get-tuple-element.64), channel_id=1, source_target_pairs={{8,0},{16,8},{24,16},{32,24},{40,32},{48,40},{56,48},{64,56},{72,6... | collective-permute-start | bytes 18440 | tf_op jit(solution)/shard_map/ppermute | solution.py:52
  63.3 2.4 %collective-permute-start.4 = (f32[3,512]{1,0:T(4,128)S(1)}, f32[3,512]{1,0:T(4,128)S(1)}, u32[]{:S(2)}, u32[]{:S(2)}) collective-permute-start(f32[3,512]{1,0:T(4,128)S(1)} %get-tuple-element.63), channel_id=1, source_target_pairs={{0,8},{8,16},{16,24},{24,32},{32,40},{40,48},{48,56},{56,64},{64,7... | collective-permute-start | bytes 18440 | tf_op jit(solution)/shard_map/ppermute | solution.py:50
  63.3 7.7 %copy-start.9 = (f32[32,512]{1,0:T(8,128)S(1)}, f32[32,512]{1,0:T(8,128)}, u32[]{:S(2)}) copy-start(f32[32,512]{1,0:T(8,128)} %get-tuple-element.10) | copy-start | bytes 196612
  65.8 5.9 %collective-permute-start.7 = (f32[38,48]{1,0:T(8,128)S(1)}, f32[38,48]{1,0:T(8,128)S(1)}, u32[]{:S(2)}, u32[]{:S(2)}) collective-permute-start(f32[38,48]{1,0:T(8,128)S(1)} %get-tuple-element.62), channel_id=1, source_target_pairs={{1,0},{2,1},{3,2},{4,3},{5,4},{6,5},{7,6},{9,8},{10,9},{11,10},{12... | collective-permute-start | bytes 21896 | tf_op jit(solution)/shard_map/ppermute | solution.py:52
  67.1 4.9 %collective-permute-start.6 = (f32[38,48]{1,0:T(8,128)S(1)}, f32[38,48]{1,0:T(8,128)S(1)}, u32[]{:S(2)}, u32[]{:S(2)}) collective-permute-start(f32[38,48]{1,0:T(8,128)S(1)} %get-tuple-element.61), channel_id=1, source_target_pairs={{0,1},{1,2},{2,3},{3,4},{4,5},{5,6},{6,7},{8,9},{9,10},{10,11},{11... | collective-permute-start | bytes 21896 | tf_op jit(solution)/shard_map/ppermute | solution.py:50
  72.4 25.1 %copy-start = (f32[19,32,512]{2,1,0:T(8,128)S(1)}, f32[19,32,512]{2,1,0:T(8,128)}, u32[]{:S(2)}) copy-start(f32[19,32,512]{2,1,0:T(8,128)} %gather_fusion) | copy-start | bytes 3735556
  72.4 25.1 %copy-start.4 = (f32[3,32,512]{2,0,1:T(4,128)S(1)}, f32[3,32,512]{2,0,1:T(4,128)}, u32[]{:S(2)}) copy-start(f32[3,32,512]{2,0,1:T(4,128)} %fusion.30) | copy-start | bytes 589828
  72.4 25.1 %copy-start.7 = (f32[32,512]{1,0:T(8,128)S(1)}, f32[32,512]{1,0:T(8,128)}, u32[]{:S(2)}) copy-start(f32[32,512]{1,0:T(8,128)} %copy-done.6) | copy-start | bytes 196612
  78.2 32.1 %all-to-all-start = ((f32[256,1,128]{2,1,0:T(1,128)}), f32[256,1,128]{2,1,0:T(1,128)S(1)}, u32[]{:S(2)}, u32[]{:S(2)}) async-start(f32[256,1,128]{2,1,0:T(1,128)} %broadcast_in_dim.133), calls=%async_computation | async-start | bytes 262144 | tf_op jit(solution)/shard_map/all_to_all | solution.py:123
  (4 other events, 3.5 us)

commit v2 on v0

v2 whole, which is shorter than its diff:
```python
import jax
import jax.numpy as jnp
from jax import lax
from jax.experimental import pallas as pl
from jax.experimental.pallas import tpu as pltpu
from jax.sharding import PartitionSpec as P

NZ = 16
ITERS = 3
PAIRS = (
    (1, 0, 0),
    (0, 1, 0),
    (0, 0, 1),
    (1, 1, 0),
    (1, -1, 0),
    (1, 0, 1),
    (1, 0, -1),
    (0, 1, 1),
    (0, 1, -1),
)
WEIGHTS = (1.0 / 18.0,) * 3 + (1.0 / 36.0,) * 6
REST_WEIGHT = 1.0 / 3.0
X_PAIRS = (0, 3, 4, 5, 6)
Y_PAIRS = (1, 3, 4, 7, 8)
relax_rate = 1.25
radius_sq = 4.0
ROWS = 8
READS = 80
EDGE = 160


def iota(shape, axis):
    return lax.broadcasted_iota(jnp.int32, shape, axis)


def roll(value, shift, axis):
    shift = shift % value.shape[axis]
    return value if shift == 0 else pltpu.roll(value, shift, axis)


def signed_sum(terms):
    total = None
    for sign, value in terms:
        if total is None:
            total = value if sign > 0 else -value
        else:
            total = total + value if sign > 0 else total - value
    return total


def dot_velocity(velocity, vector):
    return signed_sum([(c, v) for c, v in zip(velocity, vector) if c != 0])


def momentum_of(differences):
    return [
        signed_sum([(PAIRS[k][axis], differences[k]) for k in range(9) if PAIRS[k][axis] != 0])
        for axis in range(3)
    ]


def member_of(k, sign):
    return 2 * k + 1 if sign > 0 else 2 * k + 2


def row_tile(ref, member, tile, step, above=None, below=None):
    start = tile * ROWS
    layers = ref.shape[1]
    if step == 0:
        return ref[member, start : start + ROWS, :]
    if 0 <= start + step and start + step + ROWS <= layers:
        return ref[member, start + step : start + step + ROWS, :]
    value = ref[member, start : start + ROWS, :]
    row = iota(value.shape, 0)
    if step > 0:
        return jnp.where(row < ROWS - 1, roll(value, ROWS - 1, 0), 0.0 if above is None else above)
    return jnp.where(row > 0, roll(value, 1, 0), 0.0 if below is None else below)


def slide(value, step_y, step_z):
    columns = value.shape[1]
    if step_y == 0 and step_z == 0:
        return value
    moved = roll(value, -(step_y * NZ + step_z), 1)
    column = iota(value.shape, 1)
    keep = None
    if step_y != 0:
        keep = column < columns - NZ if step_y > 0 else column >= NZ
    if step_z != 0:
        depth = column & (NZ - 1)
        inner = depth < NZ - 1 if step_z > 0 else depth > 0
        keep = inner if keep is None else keep & inner
    return jnp.where(keep, moved, 0.0)


def leaves_depth(shape, step_z):
    depth = iota(shape, 1) & (NZ - 1)
    return depth == NZ - 1 if step_z > 0 else depth == 0


def block_at(lane, start):
    return (lane >= start) & (lane < start + NZ)


def pack_edge(gains, populations, high):
    origin = 0 if not high else 128 - NZ
    shape = (ROWS, 128)
    lane = iota(shape, 1)
    halves = [jnp.zeros(shape, jnp.float32), jnp.zeros(shape, jnp.float32)]
    for place, value in enumerate(list(gains) + list(populations)):
        columns = value.shape[1]
        part = value[:, :128] if not high else value[:, columns - 128 :]
        half, start = divmod(place * NZ, 128)
        halves[half] = jnp.where(block_at(lane, start), roll(part, start - origin, 1), halves[half])
    return jnp.concatenate(halves, axis=1)


def collide_kernel(forward, adjoint, node_type, partial, edges, out_s, out_z):
    layers, columns = partial.shape
    tiles = layers // ROWS
    shape = (ROWS, columns)
    row = iota(shape, 0)
    packs = {}
    for tile in range(tiles):
        rows = slice(tile * ROWS, tile * ROWS + ROWS)
        differences = [forward[2 * k + 1, rows, :] - forward[2 * k + 2, rows, :] for k in range(9)]
        momentum = momentum_of(differences)
        fluid = node_type[rows, :] != 1
        gains = []
        total = None
        for k in range(9):
            gain = (relax_rate - 1.0) * differences[k]
            gain = gain - (6.0 * relax_rate * WEIGHTS[k]) * dot_velocity(PAIRS[k], momentum)
            gain = jnp.where(fluid, gain, 0.0)
            gains.append(gain)
            reads = []
            for sign in (1, -1):
                step = [sign * c for c in PAIRS[k]]
                read = row_tile(adjoint, member_of(k, sign), tile, step[0])
                read = slide(read, step[1], step[2])
                if step[2] != 0:
                    bounce = adjoint[member_of(k, -sign), rows, :]
                    read = jnp.where(leaves_depth(shape, step[2]), bounce, read)
                reads.append(read)
            term = (reads[0] - reads[1]) * gain
            total = term if total is None else total + term
        partial[rows, :] = total
        packed = []
        for high in (False, True):
            way = -1 if high else 1
            populations = [
                adjoint[member_of(k, way * PAIRS[k][1]), rows, :] for k in Y_PAIRS
            ]
            packed.append(pack_edge([gains[k] for k in Y_PAIRS], populations, high))
        edge = jnp.concatenate(packed, axis=1)
        edges[rows, :] = edge
        if tile == 0:
            top = total
            faces = jnp.zeros(shape, jnp.float32)
            for place, k in enumerate(X_PAIRS):
                top = jnp.where(row == 3 + place, gains[k][0:1, :], top)
                faces = jnp.where(row == place, adjoint[member_of(k, 1), 0:1, :], faces)
            packs["down"] = (top, edge, faces)
        if tile == tiles - 1:
            top = total
            faces = jnp.zeros(shape, jnp.float32)
            for place, k in enumerate(X_PAIRS):
                top = jnp.where(row == place, gains[k][ROWS - 1 :, :], top)
                last = adjoint[member_of(k, -1), layers - 1 : layers, :]
                faces = jnp.where(row == place, last, faces)
            packs["up"] = (top, edge, faces)
    even = (lax.axis_index("gx") & 1) == 0
    for part in range(3):
        rows = slice(part * ROWS, part * ROWS + ROWS)
        out_s[rows, :] = jnp.where(even, packs["up"][part], packs["down"][part])
        out_z[rows, :] = jnp.where(even, packs["down"][part], packs["up"][part])


def face_reads(faces, sign):
    row = iota(faces.shape, 0)
    result = faces
    for place, k in enumerate(X_PAIRS):
        step_y, step_z = sign * PAIRS[k][1], sign * PAIRS[k][2]
        if step_y or step_z:
            result = jnp.where(row == place, slide(faces, step_y, step_z), result)
    return result


def outgoing(edge, way):
    lane = iota(edge.shape, 1)
    result = edge
    for place, k in enumerate(Y_PAIRS):
        sign = way * PAIRS[k][1]
        step_x, step_z = sign * PAIRS[k][0], sign * PAIRS[k][2]
        start = READS + place * NZ
        if step_x:
            result = jnp.where(block_at(lane, start), roll(edge, -step_x, 0), result)
        if step_z:
            moved = jnp.where(leaves_depth(edge.shape, step_z), 0.0, roll(edge, -step_z, 1))
            result = jnp.where(block_at(lane, start), moved, result)
    return result


def faces_kernel(partial, edges, own_s, own_z, got_s, got_z, wide, out_s, out_z):
    layers, columns = partial.shape
    even = (lax.axis_index("gx") & 1) == 0

    def pick(first, second, part):
        rows = slice(part * ROWS, part * ROWS + ROWS)
        return jnp.where(even, first[rows, :], second[rows, :])

    up = [pick(own_s, own_z, part) for part in range(3)]
    down = [pick(own_z, own_s, part) for part in range(3)]
    above = [pick(got_s, got_z, part) for part in range(3)]
    below = [pick(got_z, got_s, part) for part in range(3)]
    row = iota((ROWS, columns), 0)

    def completion(reads, gains):
        return jnp.sum(reads * gains, axis=0, keepdims=True)

    own_last = completion(face_reads(above[2], 1), up[0])
    own_first = completion(face_reads(below[2], -1), roll(down[0], -3, 0))
    far_first = completion(face_reads(up[2], -1), roll(above[0], -3, 0))
    far_last = completion(face_reads(down[2], 1), below[0])
    last = ROWS - 1
    wide[:ROWS, :] = below[0] + jnp.where(row == last, far_last, 0.0)
    wide[ROWS : 2 * ROWS, :] = partial[:ROWS, :] - jnp.where(row == 0, own_first, 0.0)
    wide[2 * ROWS : layers, :] = partial[ROWS : layers - ROWS, :]
    wide[layers : layers + ROWS, :] = partial[layers - ROWS :, :] + jnp.where(
        row == last, own_last, 0.0
    )
    wide[layers + ROWS :, :] = above[0] - jnp.where(row == 0, far_first, 0.0)

    edge = jnp.concatenate([below[1], edges[...], above[1]], axis=0)
    half = edge.shape[1] // 2
    low = outgoing(edge[:, :half], 1)
    high = outgoing(edge[:, half:], -1)
    low_field = roll(wide[:, :128], EDGE - 128, 1)
    high_field = roll(wide[:, columns - 128 :], EDGE - 128 - (128 - 3 * NZ), 1)
    lane = iota(low_field.shape, 1)
    held = (lane >= EDGE - 128) & (lane < EDGE - 128 + 3 * NZ)
    to_left = [low[:, :128], jnp.where(held, low_field, low[:, 128:])]
    to_right = [high[:, :128], jnp.where(held, high_field, high[:, 128:])]
    even_y = (lax.axis_index("gy") & 1) == 0
    for part in range(2):
        lanes = slice(part * 128, part * 128 + 128)
        out_s[:, lanes] = jnp.where(even_y, to_right[part], to_left[part])
        out_z[:, lanes] = jnp.where(even_y, to_left[part], to_right[part])


def fold(reads, gains, way):
    moved = roll(reads, -READS, 1)[:, :128]
    gains = gains[:, :128]
    lane = iota(gains.shape, 1)
    product = moved * gains
    for place, k in enumerate(Y_PAIRS):
        if way * PAIRS[k][1] < 0:
            product = jnp.where(block_at(lane, place * NZ), -product, product)
    total = product
    for place in range(1, len(Y_PAIRS)):
        total = total + roll(product, -place * NZ, 1)
    return jnp.where(lane < NZ, total, 0.0)


def laplace(field, depth, inside):
    rows, lanes = field.shape
    total = roll(field, 1, 0) + roll(field, -1, 0)
    total = total + (roll(field, NZ, 1) + roll(field, -NZ, 1))
    total = total + jnp.where(depth > 0, roll(field, 1, 1), 0.0)
    total = total + jnp.where(depth < NZ - 1, roll(field, -1, 1), 0.0)
    result = field - total * (1.0 / 6.0)
    return result if inside is None else jnp.where(inside, result, 0.0)


def tree_sum(parts):
    while len(parts) > 1:
        half = (len(parts) + 1) // 2
        parts = [
            parts[i] + parts[i + half] if i + half < len(parts) else parts[i] for i in range(half)
        ]
    return parts[0]


def sum_all(value):
    rows, lanes = value.shape
    parts = [
        value[r : r + ROWS, c : c + 128] for r in range(0, rows, ROWS) for c in range(0, lanes, 128)
    ]
    folded = tree_sum(parts)
    return jnp.sum(jnp.sum(folded, axis=0, keepdims=True), axis=1, keepdims=True)


def krylov_kernel(wide, own_s, own_z, got_s, got_z, basis, shares):
    rows, columns = wide.shape
    place = lax.axis_index("gy")
    last_place = lax.axis_size("gy") - 1
    even = (place & 1) == 0

    def pick(first, second):
        return jnp.where(even, first[...], second[...])

    to_right = pick(own_s, own_z)
    to_left = pick(own_z, own_s)
    right = pick(got_s, got_z)
    left = pick(got_z, got_s)
    lane = iota((rows, 128), 1)
    field = wide[...]
    low_end = field[:, :128] + fold(left, to_left, -1)
    high_end = field[:, columns - 128 :] + roll(fold(right, to_right, 1), 128 - NZ, 1)
    right_halo = jnp.where(lane < 3 * NZ, roll(right[:, 128:], 128 - EDGE, 1), 0.0)
    right_halo = right_halo + fold(to_right, right, -1)
    left_halo = jnp.where(
        lane >= 128 - 3 * NZ, roll(left[:, 128:], 128 - 3 * NZ - (EDGE - 128), 1), 0.0
    )
    left_halo = left_halo + roll(fold(to_left, left, 1), 128 - NZ, 1)
    field = jnp.concatenate(
        [left_halo, low_end, field[:, 128 : columns - 128], high_end, right_halo], axis=1
    )
    column = iota(field.shape, 1)
    depth = column & (NZ - 1)
    inside = ((column >= 128) | (place > 0)) & ((column < 128 + columns) | (place < last_place))
    first = laplace(field, depth, inside)
    second = laplace(first, depth, inside)
    third = laplace(second, depth, None)
    cores = [v[ROWS : rows - ROWS, 128 : 128 + columns] for v in (field, first, second, third)]
    for power in range(ITERS):
        basis[power] = cores[power]
    row = jnp.zeros((1, 128), jnp.float32)
    lane = iota((1, 128), 1)
    for power in range(2 * ITERS):
        value = sum_all(cores[power // 2] * cores[(power + 1) // 2])
        row = jnp.where(lane == power, value, row)
    shares[...] = jnp.broadcast_to(row, shares.shape)


def times_h(poly):
    out = list(poly) + [0.0]
    for power, entry in enumerate(poly):
        out[power + 1] = out[power + 1] + (6.0 * radius_sq) * entry
    return out


def dot_poly(p, q, moments):
    total = 0.0
    for power in range(len(p) + len(q) - 1):
        terms = [p[i] * q[power - i] for i in range(len(p)) if 0 <= power - i < len(q)]
        total = total + tree_sum(terms) * moments[power]
    return total


def entry_of(poly, power):
    return poly[power] if power < len(poly) else 0.0


def combination(moments):
    upper = 1.0 + 12.0 * radius_sq
    growth = (upper - 1.0) ** 2 / (4.0 * upper) * 1.001
    one = jnp.ones_like(moments[0])
    solved, residual, direction = [], [one], [one]
    norm_now = moments[0]
    for iteration in range(ITERS):
        image = times_h(direction)
        step = norm_now / dot_poly(direction, image, moments)
        step = jnp.clip(step, 1.0 / upper, 1.0)
        solved = [entry_of(solved, k) + step * direction[k] for k in range(len(direction))]
        if iteration < ITERS - 1:
            residual = [entry_of(residual, k) - step * image[k] for k in range(len(image))]
            norm_next = jnp.maximum(dot_poly(residual, residual, moments), 0.0)
            ratio = jnp.clip(norm_next / norm_now, 0.0, growth)
            direction = [
                residual[k] + ratio * entry_of(direction, k) for k in range(len(residual))
            ]
            norm_now = norm_next
    return solved


def combine_kernel(shares, basis, filtered):
    count = shares.shape[0]
    total = tree_sum([shares[r : r + ROWS, :] for r in range(0, count, ROWS)])
    total = jnp.sum(total, axis=0, keepdims=True)
    lane = iota(total.shape, 1)
    moments = [
        jnp.sum(jnp.where(lane == power, total, 0.0), axis=1, keepdims=True)
        for power in range(2 * ITERS)
    ]
    weights = combination(moments)
    result = basis[0] * weights[0]
    for power in range(1, ITERS):
        result = result + basis[power] * weights[power]
    filtered[...] = result


def adjoint_kernel(
    forward, adjoint, design, node_type, got_s, got_z, side_s, side_z, adjoint_new
):
    layers, columns = design.shape
    tiles = layers // ROWS
    shape = (ROWS, columns)
    even = (lax.axis_index("gx") & 1) == 0
    even_y = (lax.axis_index("gy") & 1) == 0
    faces = slice(2 * ROWS, 3 * ROWS)
    above = jnp.where(even, got_s[faces, :], got_z[faces, :])
    below = jnp.where(even, got_z[faces, :], got_s[faces, :])
    column = iota(shape, 1)
    for tile in range(tiles):
        rows = slice(tile * ROWS, tile * ROWS + ROWS)
        wide_rows = slice(tile * ROWS + ROWS, tile * ROWS + 2 * ROWS)
        right = jnp.where(even_y, side_s[wide_rows, :], side_z[wide_rows, :])
        left = jnp.where(even_y, side_z[wide_rows, :], side_s[wide_rows, :])
        density = forward[0, rows, :]
        differences = []
        for k in range(9):
            one, other = forward[2 * k + 1, rows, :], forward[2 * k + 2, rows, :]
            density = density + (one + other)
            differences.append(one - other)
        inverse = 1.0 / density
        velocity = [part * inverse for part in momentum_of(differences)]
        speed_sq = velocity[0] * velocity[0] + velocity[1] * velocity[1]
        speed_sq = speed_sq + velocity[2] * velocity[2]
        kind = node_type[rows, :]
        wall = kind == 1
        source = jnp.where(kind == 2, 1.0, jnp.where(kind == 3, -1.0, 0.0))
        blend = 1.0 - 2.0 * design[rows, :]
        rest = adjoint[0, rows, :]
        zeroth = REST_WEIGHT * rest
        quadratic = None
        vector = [None, None, None]
        kept = []
        for k in range(9):
            reads = []
            for sign in (1, -1):
                step = [sign * c for c in PAIRS[k]]
                member = member_of(k, sign)
                place = X_PAIRS.index(k) if k in X_PAIRS else 0
                read = row_tile(
                    adjoint,
                    member,
                    tile,
                    step[0],
                    above[place : place + 1, :],
                    below[place : place + 1, :],
                )
                if step[1] or step[2]:
                    read = roll(read, -(step[1] * NZ + step[2]), 1)
                if step[1]:
                    start = READS + Y_PAIRS.index(k) * NZ
                    side = right if step[1] > 0 else left
                    target = columns - NZ if step[1] > 0 else 0
                    part = side[:, start // 128 * 128 : start // 128 * 128 + 128]
                    part = roll(part, target - start, 1)
                    border = column >= columns - NZ if step[1] > 0 else column < NZ
                    spread = jnp.concatenate([part] * (columns // 128), axis=1)
                    read = jnp.where(border, spread, read)
                if step[2]:
                    bounce = adjoint[member_of(k, -sign), rows, :]
                    read = jnp.where(leaves_depth(shape, step[2]), bounce, read)
                reads.append(read)
            both = reads[0] + reads[1]
            odd = blend * (reads[0] - reads[1])
            projected = dot_velocity(PAIRS[k], velocity)
            even_part = WEIGHTS[k] * both
            zeroth = zeroth + even_part
            moved = even_part * projected
            square = moved * projected
            quadratic = square if quadratic is None else quadratic + square
            pull = (3.0 * WEIGHTS[k]) * odd + 9.0 * moved
            for axis in range(3):
                if PAIRS[k][axis]:
                    vector[axis] = (
                        signed_sum([(PAIRS[k][axis], pull)])
                        if vector[axis] is None
                        else signed_sum([(1, vector[axis]), (PAIRS[k][axis], pull)])
                    )
            kept.append((reads[0], reads[1], both, odd))
        scaled = relax_rate * zeroth
        base = scaled * (1.0 + 1.5 * speed_sq) - (4.5 * relax_rate) * quadratic + source
        vector = [
            relax_rate * part - (3.0 * scaled) * speed for part, speed in zip(vector, velocity)
        ]
        keep = relax_rate - 1.0
        adjoint_new[0, rows, :] = jnp.where(wall, rest, base - keep * rest)
        for k in range(9):
            one, other, both, odd = kept[k]
            level = base - (0.5 * keep) * both
            slope = dot_velocity(PAIRS[k], vector) - (0.5 * keep) * odd
            adjoint_new[2 * k + 1, rows, :] = jnp.where(wall, other, level + slope)
            adjoint_new[2 * k + 2, rows, :] = jnp.where(wall, one, level - slope)


def run(kernel, outputs, *operands, flops=1_000_000):
    sizes = [jax.ShapeDtypeStruct(shape, jnp.float32) for shape in outputs]
    moved = 4 * sum(a.size for a in operands) + 4 * sum(s.size for s in sizes)
    result = pl.pallas_call(
        kernel,
        out_shape=sizes,
        in_specs=[pl.BlockSpec(memory_space=pltpu.VMEM) for _ in operands],
        out_specs=[pl.BlockSpec(memory_space=pltpu.VMEM) for _ in outputs],
        compiler_params=pltpu.CompilerParams(vmem_limit_bytes=32 * 1024 * 1024),
        cost_estimate=pl.CostEstimate(flops=flops, bytes_accessed=moved, transcendentals=0),
    )(*operands)
    return result


def swap(first, second, axis, closed):
    count = lax.axis_size(axis)
    near = [(i, i ^ 1) for i in range(count)]
    starts = range(1, count if closed else count - 1, 2)
    far = [(i, (i + 1) % count) for i in starts]
    far = far + [(b, a) for a, b in far]
    return lax.ppermute(first, axis, near), lax.ppermute(second, axis, far)


def shards(forward, adjoint, design, node_type):
    members, layers, columns = adjoint.shape
    sites = layers * columns
    devices = lax.axis_size("gx") * lax.axis_size("gy")
    plane = (layers, columns)
    face = (3 * ROWS, columns)
    side = (layers + 2 * ROWS, 256)
    partial, edges, own_s, own_z = run(
        collide_kernel, [plane, (layers, 512), face, face], forward, adjoint, node_type,
        flops=150 * sites,
    )
    got_s, got_z = swap(own_s, own_z, "gx", True)
    wide, out_s, out_z = run(
        faces_kernel,
        [(layers + 2 * ROWS, columns), side, side],
        partial, edges, own_s, own_z, got_s, got_z,
    )
    side_s, side_z = swap(out_s, out_z, "gy", False)
    basis, shares = run(
        krylov_kernel, [(ITERS,) + plane, (devices, 128)], wide, out_s, out_z, side_s, side_z,
        flops=60 * sites,
    )
    spread = lax.all_to_all(shares.reshape(devices, 1, 128), ("gx", "gy"), 0, 0)
    (adjoint_new,) = run(
        adjoint_kernel,
        [adjoint.shape],
        forward, adjoint, design, node_type, got_s, got_z, side_s, side_z,
        flops=400 * sites,
    )
    (filtered,) = run(combine_kernel, [plane], spread.reshape(devices, 128), basis)
    return (adjoint_new, filtered)


def solution(mesh):
    placed = (P(None, "gx", "gy"), P(None, "gx", "gy"), P("gx", "gy"), P("gx", "gy"))
    return jax.shard_map(
        shards,
        mesh=mesh,
        in_specs=placed,
        out_specs=(P(None, "gx", "gy"), P("gx", "gy")),
        check_vma=False,
    )
```

time: 502 us -> 49.7 us (0.10)
  blocking collectives: 394 us -> 0 us
  matrix products: 18.8 us -> 0 us
  other arithmetic: 16.3 us -> 0 us
  local copies, waits for them, and re-layouts: 18.2 us -> 3.43 us
  starting transfers between devices: 35.3 us -> 23.2 us
  waiting for transfers between devices: 9.7 us -> 16.9 us
  between operations: 7.57 us -> 0.72 us
  Pallas kernels: 0 us -> 5.17 us
    psum x5 -> x0, blocking collectives: 394 us -> none  [the longest x3 233 us: squares(): return lax.psum(jnp.sum(residual * residual), ('gx', 'gy'))]
    ppermute x16 -> x4, starting transfers between devices: 35.3 us -> 4.09 us  [swap(): return (lax.ppermute(first, axis, near), lax.ppermute(second, axis, far))]
    all_to_all x0 -> x1, starting transfers between devices: none -> 19.1 us  [shards(): spread = lax.all_to_all(shares.reshape(devices, 1, 128), ('gx', 'gy'), 0, 0)]
    dot_general x5 -> x0, matrix products: 18.8 us -> none  [the longest x1 6.69 us: adjoint_cell(): projected = jnp.einsum('qk,kxw->qxw', table, velocity, precision=highest)]
    all_to_all x0 -> x1, waiting for transfers between devices: none -> 10.8 us  [shards(): spread = lax.all_to_all(shares.reshape(devices, 1, 128), ('gx', 'gy'), 0, 0)]
    reduce_sum x7 -> x0, other arithmetic: 8.06 us -> none  [the longest x1 2.98 us: adjoint_cell(): jnp.sum(read * (collided[OPPOSITE] - collided), axis=0)]
    pallas_call x0 -> x5, Pallas kernels: none -> 5.17 us  [run(): pl.pallas_call(kernel, out_shape=sizes, in_specs=[pl.BlockSpec(memory_spa...]
  transfers between devices with their start and end apart: 16 -> 5, of which waited for: 7 -> 4; matrix products, arithmetic and copies ran while one was open for 4% -> 0% of each run, Pallas kernels for 0% -> 4%
where the time goes in v2:
time: 49.7 us; the launch traced here: 49.4 us
  starting transfers between devices  23.2 us (47%)
  waiting for transfers between devices  16.9 us (34%)
  Pallas kernels  5.17 us (10%)
  local copies, waits for them, and re-layouts  3.43 us (7%)
  between operations  0.72 us (1%)
    all_to_all x1, starting transfers between devices, shards(): spread = lax.all_to_all(shares.reshape(devices, 1, 128), ('gx', 'gy'), 0, 0)  19.1 us
    all_to_all x1, waiting for transfers between devices, shards(): spread = lax.all_to_all(shares.reshape(devices, 1, 128), ('gx', 'gy'), 0, 0)  10.8 us
    ppermute x4, waiting for transfers between devices, swap(): return (lax.ppermute(first, axis, near), lax.ppermute(second, axis, far))  6.06 us
    pallas_call x5, Pallas kernels, run(): pl.pallas_call(kernel, out_shape=sizes, in_specs=[pl.BlockSpec(memory_spa...  5.17 us
    ppermute x4, starting transfers between devices, swap(): return (lax.ppermute(first, axis, near), lax.ppermute(second, axis, far))  4.09 us
    unnamed x14, local copies, waits for them, and re-layouts  3.43 us
  transfers between devices with their start and end apart: 5, of which 4 were waited for; matrix products, arithmetic and copies ran while one was open for 0% of the time, Pallas kernels for 4%

profile of v2, /device:TPU:1, one launch (start us, length us, event | category | flops | bytes accessed | tf_op | source)
XLA Modules:
  0.0 49.4 jit_solution(15271430598284938708)
XLA Ops:
  0.6 0.0 copy-start
  0.6 1.3 %copy-done = f32[19,32,512]{2,1,0:T(8,128)S(1)} copy-done((f32[19,32,512]{2,1,0:T(8,128)S(1)}, f32[19,32,512]{2,1,0:T(8,128)}, u32[]{:S(2)}) %copy-start) | copy-done | bytes 1245208
  1.9 0.0 copy-start.2
  1.9 1.3 %copy-done.2 = f32[19,32,512]{2,1,0:T(8,128)S(1)} copy-done((f32[19,32,512]{2,1,0:T(8,128)S(1)}, f32[19,32,512]{2,1,0:T(8,128)}, u32[]{:S(2)}) %copy-start.2) | copy-done | bytes 1245208
  3.2 0.0 copy-start.4
  3.2 0.8 %copy-done.4 = s32[32,512]{1,0:T(8,128)S(1)} copy-done((s32[32,512]{1,0:T(8,128)S(1)}, s32[32,512]{1,0:T(8,128)}, u32[]{:S(2)}) %copy-start.4) | copy-done | bytes 65560
  4.1 0.0 copy-start.1
  4.1 0.0 copy-start.3
  4.1 0.0 copy-start.5
  4.1 0.0 copy-start.6
  4.1 0.5 %shard_map.59 = (f32[32,512]{1,0:T(8,128)S(1)}, f32[32,512]{1,0:T(8,128)S(1)}, f32[24,512]{1,0:T(8,128)S(1)}, f32[24,512]{1,0:T(8,128)S(1)}) custom-call(f32[19,32,512]{2,1,0:T(8,128)S(1)} %copy-done, f32[19,32,512]{2,1,0:T(8,128)S(1)} %copy-done.2, s32[32,512]{1,0:T(8,128)S(1)} %copy-done.4), custom_call_target="tpu_custom_call" | custom-call | flops 2457600 | bytes 2785280 | tf_op jit(solution)/shard_map/pallas_call | solution.py:493
  4.6 3.3 %collective-permute-start = (f32[24,512]{1,0:T(8,128)S(1)}, f32[24,512]{1,0:T(8,128)S(1)}, u32[]{:S(2)}, u32[]{:S(2)}) collective-permute-start(f32[24,512]{1,0:T(8,128)S(1)} %get-tuple-element.11.own_s), channel_id=1, source_target_pairs={{0,8},{8,0},{16,24},{24,16},{32,40},{40,32},{48,56},{56,48},{64,72... | collective-permute-start | bytes 147464 | tf_op jit(solution)/shard_map/ppermute | solution.py:510
  7.9 0.0 collective-permute-start.1
  7.9 0.9 %collective-permute-done.got_s = f32[24,512]{1,0:T(8,128)S(1)} collective-permute-done((f32[24,512]{1,0:T(8,128)S(1)}, f32[24,512]{1,0:T(8,128)S(1)}, u32[]{:S(2)}, u32[]{:S(2)}) %collective-permute-start) | collective-permute-done | bytes 49184 | tf_op jit(solution)/shard_map/ppermute | solution.py:510
  8.8 2.6 %collective-permute-done.1.got_z = f32[24,512]{1,0:T(8,128)S(1)} collective-permute-done((f32[24,512]{1,0:T(8,128)S(1)}, f32[24,512]{1,0:T(8,128)S(1)}, u32[]{:S(2)}, u32[]{:S(2)}) %collective-permute-start.1) | collective-permute-done | bytes 49184 | tf_op jit(solution)/shard_map/ppermute | solution.py:510
  11.4 0.2 shard_map.60
  11.7 0.1 collective-permute-start.2
  11.8 0.7 %collective-permute-start.3 = (f32[48,256]{1,0:T(8,128)S(1)}, f32[48,256]{1,0:T(8,128)S(1)}, u32[]{:S(2)}, u32[]{:S(2)}) collective-permute-start(f32[48,256]{1,0:T(8,128)S(1)} %get-tuple-element.16.own_z), channel_id=1, source_target_pairs={{1,2},{3,4},{5,6},{2,1},{4,3},{6,5},{9,10},{11,12},{13,14},{10,9},... | collective-permute-start | bytes 147464 | tf_op jit(solution)/shard_map/ppermute | solution.py:510
  12.4 2.5 %collective-permute-done.2.side_s.got_s = f32[48,256]{1,0:T(8,128)S(1)} collective-permute-done((f32[48,256]{1,0:T(8,128)S(1)}, f32[48,256]{1,0:T(8,128)S(1)}, u32[]{:S(2)}, u32[]{:S(2)}) %collective-permute-start.2) | collective-permute-done | bytes 49184 | tf_op jit(solution)/shard_map/ppermute | solution.py:510
  15.0 0.0 collective-permute-done.3.side_z.got_z
  15.0 1.7 %shard_map.62 = (f32[3,32,512]{2,1,0:T(8,128)S(1)}, f32[256,128]{1,0:T(8,128)}) custom-call(f32[48,512]{1,0:T(8,128)S(1)} %get-tuple-element.17.wide, f32[48,256]{1,0:T(8,128)S(1)} %get-tuple-element.15.own_s, f32[48,256]{1,0:T(8,128)S(1)} %get-tuple-element.16.own_z, f32[48,256]{1,0:T(8,128)S(1)} %collective-permute-done.2.side_s.got_s, ...), custom_call_target="tpu_custom_call" | custom-call | flops 983040 | bytes 622592 | tf_op jit(solution)/shard_map/pallas_call | solution.py:493
  16.7 19.1 %all-to-all-start = ((f32[256,1,128]{2,1,0:T(1,128)}), f32[256,1,128]{2,1,0:T(1,128)S(1)}, u32[]{:S(2)}, u32[]{:S(2)}) async-start(f32[256,1,128]{2,1,0:T(1,128)} %bitcast.1), calls=%async_computation | async-start | bytes 262144 | tf_op jit(solution)/shard_map/all_to_all | solution.py:535
  35.9 0.0 copy-done.1
  35.9 0.0 copy-done.3
  35.9 0.0 copy-done.5
  35.9 0.0 copy-done.6
  35.9 1.9 %shard_map.61 = f32[19,32,512]{2,1,0:T(8,128)} custom-call(f32[19,32,512]{2,1,0:T(8,128)S(1)} %copy-done.1, f32[19,32,512]{2,1,0:T(8,128)S(1)} %copy-done.3, f32[32,512]{1,0:T(8,128)S(1)} %copy-done.6, s32[32,512]{1,0:T(8,128)S(1)} %copy-done.5, f32[24,512]{1,0:T(8,128)S(1)} %collective-permute-done.got_s, f32[24,512]{1,0:T(8,128)S(1)} %collective-permute-done.1.got_z, ...), custom_call_target="tpu_custom_call" | custom-call | flops 6553600 | bytes 4063232 | tf_op jit(solution)/shard_map/pallas_call | solution.py:493
  37.8 10.8 %all-to-all-done = f32[256,1,128]{2,1,0:T(1,128)S(1)} async-done(((f32[256,1,128]{2,1,0:T(1,128)}), f32[256,1,128]{2,1,0:T(1,128)S(1)}, u32[]{:S(2)}, u32[]{:S(2)}) %all-to-all-start) | async-done | bytes 131104 | tf_op jit(solution)/shard_map/all_to_all | solution.py:535
  48.6 0.8 %shard_map.63 = f32[32,512]{1,0:T(8,128)} custom-call(f32[256,128]{1,0:T(8,128)S(1)} %bitcast.4, f32[3,32,512]{2,1,0:T(8,128)S(1)} %get-tuple-element.19.basis), custom_call_target="tpu_custom_call" | custom-call | flops 1000000 | bytes 393216 | tf_op jit(solution)/shard_map/pallas_call | solution.py:493
Async XLA Ops:
  0.6 1.3 %copy-start = (f32[19,32,512]{2,1,0:T(8,128)S(1)}, f32[19,32,512]{2,1,0:T(8,128)}, u32[]{:S(2)}) copy-start(f32[19,32,512]{2,1,0:T(8,128)} %forward.3) | copy-start | bytes 3735556
  1.9 1.3 %copy-start.2 = (f32[19,32,512]{2,1,0:T(8,128)S(1)}, f32[19,32,512]{2,1,0:T(8,128)}, u32[]{:S(2)}) copy-start(f32[19,32,512]{2,1,0:T(8,128)} %adjoint.3) | copy-start | bytes 3735556
  3.2 0.8 %copy-start.4 = (s32[32,512]{1,0:T(8,128)S(1)}, s32[32,512]{1,0:T(8,128)}, u32[]{:S(2)}) copy-start(s32[32,512]{1,0:T(8,128)} %node_type.3) | copy-start | bytes 196612
  4.1 31.8 %copy-start.1 = (f32[19,32,512]{2,1,0:T(8,128)S(1)}, f32[19,32,512]{2,1,0:T(8,128)}, u32[]{:S(2)}) copy-start(f32[19,32,512]{2,1,0:T(8,128)} %forward.3) | copy-start | bytes 3735556
  4.1 31.8 %copy-start.3 = (f32[19,32,512]{2,1,0:T(8,128)S(1)}, f32[19,32,512]{2,1,0:T(8,128)}, u32[]{:S(2)}) copy-start(f32[19,32,512]{2,1,0:T(8,128)} %adjoint.3) | copy-start | bytes 3735556
  4.1 31.8 %copy-start.5 = (s32[32,512]{1,0:T(8,128)S(1)}, s32[32,512]{1,0:T(8,128)}, u32[]{:S(2)}) copy-start(s32[32,512]{1,0:T(8,128)} %node_type.3) | copy-start | bytes 196612
  4.1 31.8 %copy-start.6 = (f32[32,512]{1,0:T(8,128)S(1)}, f32[32,512]{1,0:T(8,128)}, u32[]{:S(2)}) copy-start(f32[32,512]{1,0:T(8,128)} %design.1) | copy-start | bytes 196612
  4.6 4.2 %collective-permute-start = (f32[24,512]{1,0:T(8,128)S(1)}, f32[24,512]{1,0:T(8,128)S(1)}, u32[]{:S(2)}, u32[]{:S(2)}) collective-permute-start(f32[24,512]{1,0:T(8,128)S(1)} %get-tuple-element.11.own_s), channel_id=1, source_target_pairs={{0,8},{8,0},{16,24},{24,16},{32,40},{40,32},{48,56},{56,48},{64,72... | collective-permute-start | bytes 147464 | tf_op jit(solution)/shard_map/ppermute | solution.py:510
  7.9 3.5 %collective-permute-start.1 = (f32[24,512]{1,0:T(8,128)S(1)}, f32[24,512]{1,0:T(8,128)S(1)}, u32[]{:S(2)}, u32[]{:S(2)}) collective-permute-start(f32[24,512]{1,0:T(8,128)S(1)} %get-tuple-element.12.own_z), channel_id=1, source_target_pairs={{8,16},{24,32},{40,48},{56,64},{72,80},{88,96},{104,112},{120,128}... | collective-permute-start | bytes 147464 | tf_op jit(solution)/shard_map/ppermute | solution.py:510
  11.7 3.3 %collective-permute-start.2 = (f32[48,256]{1,0:T(8,128)S(1)}, f32[48,256]{1,0:T(8,128)S(1)}, u32[]{:S(2)}, u32[]{:S(2)}) collective-permute-start(f32[48,256]{1,0:T(8,128)S(1)} %get-tuple-element.15.own_s), channel_id=1, source_target_pairs={{0,1},{1,0},{2,3},{3,2},{4,5},{5,4},{6,7},{7,6},{8,9},{9,8},{10,11... | collective-permute-start | bytes 147464 | tf_op jit(solution)/shard_map/ppermute | solution.py:510
  11.8 3.2 %collective-permute-start.3 = (f32[48,256]{1,0:T(8,128)S(1)}, f32[48,256]{1,0:T(8,128)S(1)}, u32[]{:S(2)}, u32[]{:S(2)}) collective-permute-start(f32[48,256]{1,0:T(8,128)S(1)} %get-tuple-element.16.own_z), channel_id=1, source_target_pairs={{1,2},{3,4},{5,6},{2,1},{4,3},{6,5},{9,10},{11,12},{13,14},{10,9},... | collective-permute-start | bytes 147464 | tf_op jit(solution)/shard_map/ppermute | solution.py:510
  16.7 31.9 %all-to-all-start = ((f32[256,1,128]{2,1,0:T(1,128)}), f32[256,1,128]{2,1,0:T(1,128)S(1)}, u32[]{:S(2)}, u32[]{:S(2)}) async-start(f32[256,1,128]{2,1,0:T(1,128)} %bitcast.1), calls=%async_computation | async-start | bytes 262144 | tf_op jit(solution)/shard_map/all_to_all | solution.py:535

commit v3 on v2

--- a/solution.py
+++ b/solution.py
@@ -115,65 +115,126 @@
     return jnp.concatenate(halves, axis=1)
 
 
-def collide_kernel(forward, adjoint, node_type, partial, edges, out_s, out_z):
-    layers, columns = partial.shape
-    tiles = layers // ROWS
-    shape = (ROWS, columns)
-    row = iota(shape, 0)
-    packs = {}
-    for tile in range(tiles):
-        rows = slice(tile * ROWS, tile * ROWS + ROWS)
-        differences = [forward[2 * k + 1, rows, :] - forward[2 * k + 2, rows, :] for k in range(9)]
-        momentum = momentum_of(differences)
-        fluid = node_type[rows, :] != 1
-        gains = []
-        total = None
-        for k in range(9):
-            gain = (relax_rate - 1.0) * differences[k]
-            gain = gain - (6.0 * relax_rate * WEIGHTS[k]) * dot_velocity(PAIRS[k], momentum)
-            gain = jnp.where(fluid, gain, 0.0)
-            gains.append(gain)
-            reads = []
-            for sign in (1, -1):
-                step = [sign * c for c in PAIRS[k]]
-                read = row_tile(adjoint, member_of(k, sign), tile, step[0])
-                read = slide(read, step[1], step[2])
-                if step[2] != 0:
-                    bounce = adjoint[member_of(k, -sign), rows, :]
-                    read = jnp.where(leaves_depth(shape, step[2]), bounce, read)
-                reads.append(read)
-            term = (reads[0] - reads[1]) * gain
-            total = term if total is None else total + term
-        partial[rows, :] = total
-        packed = []
-        for high in (False, True):
-            way = -1 if high else 1
-            populations = [
-                adjoint[member_of(k, way * PAIRS[k][1]), rows, :] for k in Y_PAIRS
-            ]
-            packed.append(pack_edge([gains[k] for k in Y_PAIRS], populations, high))
-        edge = jnp.concatenate(packed, axis=1)
-        edges[rows, :] = edge
-        if tile == 0:
-            top = total
-            faces = jnp.zeros(shape, jnp.float32)
-            for place, k in enumerate(X_PAIRS):
-                top = jnp.where(row == 3 + place, gains[k][0:1, :], top)
-                faces = jnp.where(row == place, adjoint[member_of(k, 1), 0:1, :], faces)
-            packs["down"] = (top, edge, faces)
-        if tile == tiles - 1:
-            top = total
-            faces = jnp.zeros(shape, jnp.float32)
-            for place, k in enumerate(X_PAIRS):
-                top = jnp.where(row == place, gains[k][ROWS - 1 :, :], top)
-                last = adjoint[member_of(k, -1), layers - 1 : layers, :]
-                faces = jnp.where(row == place, last, faces)
-            packs["up"] = (top, edge, faces)
+def gains_of(forward, kinds):
+    differences = [forward(2 * k + 1) - forward(2 * k + 2) for k in range(9)]
+    momentum = momentum_of(differences)
+    fluid = kinds != 1
+    gains = []
+    for k in range(9):
+        gain = (relax_rate - 1.0) * differences[k]
+        gain = gain - (6.0 * relax_rate * WEIGHTS[k]) * dot_velocity(PAIRS[k], momentum)
+        gains.append(jnp.where(fluid, gain, 0.0))
+    return gains
+
+
+def inner_sensitivity(gains, rows_of):
+    total = None
+    for k in range(9):
+        reads = []
+        for sign in (1, -1):
+            step = [sign * c for c in PAIRS[k]]
+            read = slide(rows_of(member_of(k, sign), step[0]), step[1], step[2])
+            if step[2] != 0:
+                bounce = rows_of(member_of(k, -sign), 0)
+                read = jnp.where(leaves_depth(read.shape, step[2]), bounce, read)
+            reads.append(read)
+        term = (reads[0] - reads[1]) * gains[k]
+        total = term if total is None else total + term
+    return total
+
+
+def pack_edges(gains, adjoint):
+    packed = []
+    for high in (False, True):
+        way = -1 if high else 1
+        populations = [adjoint(member_of(k, way * PAIRS[k][1])) for k in Y_PAIRS]
+        packed.append(pack_edge([gains[k] for k in Y_PAIRS], populations, high))
+    return jnp.concatenate(packed, axis=1)
+
+
+def border_kernel(forward, adjoint, node_type, out_s, out_z, moving, carried, kinds, sems):
+    layers, columns = node_type.shape
+    copies = []
+    for place, start in enumerate((0, layers - ROWS)):
+        rows = pl.ds(start, ROWS)
+        copies.append(pltpu.make_async_copy(node_type.at[rows, :], kinds.at[place], sems.at[place]))
+    for source, target in ((forward, moving), (adjoint, carried)):
+        for place, start in enumerate((0, layers - ROWS)):
+            part = source.at[:, pl.ds(start, ROWS), :]
+            copies.append(pltpu.make_async_copy(part, target.at[place], sems.at[len(copies)]))
+    for copy in copies:
+        copy.start()
+    row = iota((ROWS, columns), 0)
+    for place in range(2):
+        copies[place].wait()
+    gains = []
+    for place in range(2):
+        copies[2 + place].wait()
+        gains.append(gains_of(lambda member: moving[place, member], kinds[place]))
+    packs = []
+    for place in range(2):
+        copies[4 + place].wait()
+
+        def rows_of(member, step):
+            value = carried[place, member]
+            if step == 0:
+                return value
+            if step > 0:
+                return jnp.where(row < ROWS - 1, roll(value, ROWS - 1, 0), 0.0)
+            return jnp.where(row > 0, roll(value, 1, 0), 0.0)
+
+        top = inner_sensitivity(gains[place], rows_of)
+        edge = pack_edges(gains[place], lambda member: carried[place, member])
+        faces = jnp.zeros((ROWS, columns), jnp.float32)
+        last = place * (ROWS - 1)
+        base = 3 * (1 - place)
+        for index, k in enumerate(X_PAIRS):
+            member = member_of(k, 1 - 2 * place)
+            top = jnp.where(row == base + index, gains[place][k][last : last + 1, :], top)
+            faces = jnp.where(row == index, carried[place, member, last : last + 1, :], faces)
+        packs.append((top, edge, faces))
     even = (lax.axis_index("gx") & 1) == 0
     for part in range(3):
         rows = slice(part * ROWS, part * ROWS + ROWS)
-        out_s[rows, :] = jnp.where(even, packs["up"][part], packs["down"][part])
-        out_z[rows, :] = jnp.where(even, packs["down"][part], packs["up"][part])
+        out_s[rows, :] = jnp.where(even, packs[1][part], packs[0][part])
+        out_z[rows, :] = jnp.where(even, packs[0][part], packs[1][part])
+
+
+def fetch_tiles(sources, targets, sems):
+    tiles = sources[-1].shape[-2] // ROWS
+    groups = []
+    for tile in range(tiles):
+        rows = pl.ds(tile * ROWS, ROWS)
+        group = []
+        for index, (source, target) in enumerate(zip(sources, targets)):
+            at = (slice(None), rows) if len(source.shape) == 3 else (rows,)
+            group.append(
+                pltpu.make_async_copy(source.at[at], target.at[at], sems.at[tile, index])
+            )
+        for copy in group:
+            copy.start()
+        groups.append(group)
+    return groups
+
+
+def take(groups, tile):
+    for ready in ((0, 1) if tile == 0 else (tile + 1,)):
+        if ready < len(groups):
+            for copy in groups[ready]:
+                copy.wait()
+
+
+def collide_kernel(forward, adjoint, node_type, partial, edges, moving, carried, kinds, sems):
+    layers, columns = partial.shape
+    groups = fetch_tiles((forward, adjoint, node_type), (moving, carried, kinds), sems)
+    for tile in range(layers // ROWS):
+        rows = slice(tile * ROWS, tile * ROWS + ROWS)
+        take(groups, tile)
+        gains = gains_of(lambda member: moving[member, rows, :], kinds[rows, :])
+        partial[rows, :] = inner_sensitivity(
+            gains, lambda member, step: row_tile(carried, member, tile, step)
+        )
+        edges[rows, :] = pack_edges(gains, lambda member: carried[member, rows, :])
 
 
 def face_reads(faces, sign):
@@ -391,9 +452,30 @@
 
 
 def adjoint_kernel(
-    forward, adjoint, design, node_type, got_s, got_z, side_s, side_z, adjoint_new
+    forward_far,
+    adjoint_far,
+    design_far,
+    node_far,
+    got_s,
+    got_z,
+    side_s,
+    side_z,
+    result,
+    forward,
+    adjoint,
+    design,
+    node_type,
+    adjoint_new,
+    sems,
+    out_sems,
 ):
     layers, columns = design.shape
+    groups = fetch_tiles(
+        (forward_far, adjoint_far, design_far, node_far),
+        (forward, adjoint, design, node_type),
+        sems,
+    )
+    sent = []
     tiles = layers // ROWS
     shape = (ROWS, columns)
     even = (lax.axis_index("gx") & 1) == 0
@@ -407,6 +489,7 @@
         wide_rows = slice(tile * ROWS + ROWS, tile * ROWS + 2 * ROWS)
         right = jnp.where(even_y, side_s[wide_rows, :], side_z[wide_rows, :])
         left = jnp.where(even_y, side_z[wide_rows, :], side_s[wide_rows, :])
+        take(groups, tile)
         density = forward[0, rows, :]
         differences = []
         for k in range(9):
@@ -485,20 +568,35 @@
             slope = dot_velocity(PAIRS[k], vector) - (0.5 * keep) * odd
             adjoint_new[2 * k + 1, rows, :] = jnp.where(wall, other, level + slope)
             adjoint_new[2 * k + 2, rows, :] = jnp.where(wall, one, level - slope)
-
-
-def run(kernel, outputs, *operands, flops=1_000_000):
+        part = pl.ds(tile * ROWS, ROWS)
+        sent.append(
+            pltpu.make_async_copy(
+                adjoint_new.at[:, part, :], result.at[:, part, :], out_sems.at[tile]
+            )
+        )
+        sent[-1].start()
+    for copy in sent:
+        copy.wait()
+
+
+def run(kernel, outputs, *operands, flops, far=0, far_out=False, scratch=(), vmem=32):
     sizes = [jax.ShapeDtypeStruct(shape, jnp.float32) for shape in outputs]
     moved = 4 * sum(a.size for a in operands) + 4 * sum(s.size for s in sizes)
-    result = pl.pallas_call(
+    operands = [
+        pltpu.with_memory_space_constraint(a, pltpu.HBM) if i < far else a
+        for i, a in enumerate(operands)
+    ]
+    near = pl.BlockSpec(memory_space=pltpu.VMEM)
+    away = pl.BlockSpec(memory_space=pl.ANY)
+    return pl.pallas_call(
         kernel,
         out_shape=sizes,
-        in_specs=[pl.BlockSpec(memory_space=pltpu.VMEM) for _ in operands],
-        out_specs=[pl.BlockSpec(memory_space=pltpu.VMEM) for _ in outputs],
-        compiler_params=pltpu.CompilerParams(vmem_limit_bytes=32 * 1024 * 1024),
+        in_specs=[away if i < far else near for i in range(len(operands))],
+        out_specs=[away if far_out else near for _ in outputs],
+        scratch_shapes=list(scratch),
+        compiler_params=pltpu.CompilerParams(vmem_limit_bytes=vmem * 1024 * 1024),
         cost_estimate=pl.CostEstimate(flops=flops, bytes_accessed=moved, transcendentals=0),
     )(*operands)
-    return result
 
 
 def swap(first, second, axis, closed):
@@ -517,29 +615,91 @@
     plane = (layers, columns)
     face = (3 * ROWS, columns)
     side = (layers + 2 * ROWS, 256)
-    partial, edges, own_s, own_z = run(
-        collide_kernel, [plane, (layers, 512), face, face], forward, adjoint, node_type,
+    tiles = layers // ROWS
+    field = pltpu.VMEM((members,) + plane, jnp.float32)
+    ends = pltpu.VMEM((2, members, ROWS, columns), jnp.float32)
+    own_s, own_z = run(
+        border_kernel,
+        [face, face],
+        forward,
+        adjoint,
+        node_type,
+        far=3,
+        scratch=[
+            ends,
+            ends,
+            pltpu.VMEM((2, ROWS, columns), jnp.int32),
+            pltpu.SemaphoreType.DMA((6,)),
+        ],
+        flops=80 * sites,
+    )
+    got_s, got_z = swap(own_s, own_z, "gx", True)
+    partial, edges = run(
+        collide_kernel,
+        [plane, (layers, 512)],
+        forward,
+        adjoint,
+        node_type,
+        far=3,
+        scratch=[
+            field,
+            field,
+            pltpu.VMEM(plane, jnp.int32),
+            pltpu.SemaphoreType.DMA((tiles, 3)),
+        ],
         flops=150 * sites,
     )
-    got_s, got_z = swap(own_s, own_z, "gx", True)
     wide, out_s, out_z = run(
         faces_kernel,
         [(layers + 2 * ROWS, columns), side, side],
-        partial, edges, own_s, own_z, got_s, got_z,
+        partial,
+        edges,
+        own_s,
+        own_z,
+        got_s,
+        got_z,
+        flops=10 * sites,
     )
     side_s, side_z = swap(out_s, out_z, "gy", False)
     basis, shares = run(
-        krylov_kernel, [(ITERS,) + plane, (devices, 128)], wide, out_s, out_z, side_s, side_z,
+        krylov_kernel,
+        [(ITERS,) + plane, (ROWS, 128)],
+        wide,
+        out_s,
+        out_z,
+        side_s,
+        side_z,
         flops=60 * sites,
     )
-    spread = lax.all_to_all(shares.reshape(devices, 1, 128), ("gx", "gy"), 0, 0)
+    copies = jnp.broadcast_to(shares[None, :1], (devices, 1, 128))
+    spread = lax.all_to_all(copies, ("gx", "gy"), 0, 0)
     (adjoint_new,) = run(
         adjoint_kernel,
         [adjoint.shape],
-        forward, adjoint, design, node_type, got_s, got_z, side_s, side_z,
+        forward,
+        adjoint,
+        design,
+        node_type,
+        got_s,
+        got_z,
+        side_s,
+        side_z,
+        far=4,
+        far_out=True,
+        scratch=[
+            field,
+            field,
+            pltpu.VMEM(plane, jnp.float32),
+            pltpu.VMEM(plane, jnp.int32),
+            field,
+            pltpu.SemaphoreType.DMA((tiles, 4)),
+            pltpu.SemaphoreType.DMA((tiles,)),
+        ],
         flops=400 * sites,
     )
-    (filtered,) = run(combine_kernel, [plane], spread.reshape(devices, 128), basis)
+    (filtered,) = run(
+        combine_kernel, [plane], spread.reshape(devices, 128), basis, flops=10 * sites
+    )
     return (adjoint_new, filtered)
 
 

time: 49.7 us -> 47.4 us (0.954)
  Pallas kernels: 5.17 us -> 8.8 us
  waiting for transfers between devices: 16.9 us -> 13.7 us
  local copies, waits for them, and re-layouts: 3.43 us -> 0.73 us
    pallas_call x5 -> x6, Pallas kernels: 5.17 us -> 8.8 us  [run(): pl.pallas_call(kernel, out_shape=sizes, in_specs=[away if i < far else ne...]
    unnamed x14 -> x0, local copies, waits for them, and re-layouts: 3.43 us -> none
    ppermute x4, waiting for transfers between devices: 6.06 us -> 4.02 us  [swap(): return (lax.ppermute(first, axis, near), lax.ppermute(second, axis, far))]
    all_to_all x1, waiting for transfers between devices: 10.8 us -> 9.66 us  [shards(): spread = lax.all_to_all(copies, ('gx', 'gy'), 0, 0)]
    broadcast_in_dim x0 -> x2, local copies, waits for them, and re-layouts: none -> 0.73 us  [shards(): copies = jnp.broadcast_to(shares[None, :1], (devices, 1, 128))]
  transfers between devices with their start and end apart: 5 -> 5, of which waited for: 4 -> 3; matrix products, arithmetic and copies ran while one was open for 0% -> 0% of each run, Pallas kernels for 4% -> 11%
where the time goes in v3:
time: 47.4 us; the launch traced here: 47.1 us
  starting transfers between devices  23.2 us (49%)
  waiting for transfers between devices  13.7 us (29%)
  Pallas kernels  8.8 us (19%)
  local copies, waits for them, and re-layouts  0.73 us (2%)
  between operations  0.7 us (1%)
    all_to_all x1, starting transfers between devices, shards(): spread = lax.all_to_all(copies, ('gx', 'gy'), 0, 0)  19.1 us
    all_to_all x1, waiting for transfers between devices, shards(): spread = lax.all_to_all(copies, ('gx', 'gy'), 0, 0)  9.66 us
    pallas_call x6, Pallas kernels, run(): pl.pallas_call(kernel, out_shape=sizes, in_specs=[away if i < far else ne...  8.8 us
    ppermute x4, starting transfers between devices, swap(): return (lax.ppermute(first, axis, near), lax.ppermute(second, axis, far))  4.09 us
    ppermute x4, waiting for transfers between devices, swap(): return (lax.ppermute(first, axis, near), lax.ppermute(second, axis, far))  4.02 us
  transfers between devices with their start and end apart: 5, of which 3 were waited for; matrix products, arithmetic and copies ran while one was open for 0% of the time, Pallas kernels for 11%

profile of v3, /device:TPU:1, one launch (start us, length us, event | category | flops | bytes accessed | tf_op | source)
XLA Modules:
  0.0 47.1 jit_solution(16210856516039569372)
XLA Ops:
  0.6 1.6 %shard_map.59 = (f32[24,512]{1,0:T(8,128)S(1)}, f32[24,512]{1,0:T(8,128)S(1)}) custom-call(f32[19,32,512]{2,1,0:T(8,128)} %forward_far.1, f32[19,32,512]{2,1,0:T(8,128)} %adjoint_far.1, s32[32,512]{1,0:T(8,128)} %node_far.1), custom_call_target="tpu_custom_call" | custom-call | flops 1310720 | bytes 2654208 | tf_op jit(solution)/shard_map/pallas_call | solution.py:591
  2.2 3.3 %collective-permute-start = (f32[24,512]{1,0:T(8,128)S(1)}, f32[24,512]{1,0:T(8,128)S(1)}, u32[]{:S(2)}, u32[]{:S(2)}) collective-permute-start(f32[24,512]{1,0:T(8,128)S(1)} %get-tuple-element.11.own_s), channel_id=1, source_target_pairs={{0,8},{8,0},{16,24},{24,16},{32,40},{40,32},{48,56},{56,48},{64,72... | collective-permute-start | bytes 147464 | tf_op jit(solution)/shard_map/ppermute | solution.py:608
  5.5 0.0 collective-permute-start.1
  5.5 2.0 %shard_map.60 = (f32[32,512]{1,0:T(8,128)S(1)}, f32[32,512]{1,0:T(8,128)S(1)}) custom-call(f32[19,32,512]{2,1,0:T(8,128)} %forward_far.1, f32[19,32,512]{2,1,0:T(8,128)} %adjoint_far.1, s32[32,512]{1,0:T(8,128)} %node_far.1), custom_call_target="tpu_custom_call" | custom-call | flops 2457600 | bytes 2686976 | tf_op jit(solution)/shard_map/pallas_call | solution.py:591
  7.6 0.0 collective-permute-done.got_s
  7.6 1.5 %collective-permute-done.1.got_z = f32[24,512]{1,0:T(8,128)S(1)} collective-permute-done((f32[24,512]{1,0:T(8,128)S(1)}, f32[24,512]{1,0:T(8,128)S(1)}, u32[]{:S(2)}, u32[]{:S(2)}) %collective-permute-start.1) | collective-permute-done | bytes 49184 | tf_op jit(solution)/shard_map/ppermute | solution.py:608
  9.0 0.2 shard_map.61
  9.3 0.1 collective-permute-start.2
  9.4 0.7 %collective-permute-start.3 = (f32[48,256]{1,0:T(8,128)S(1)}, f32[48,256]{1,0:T(8,128)S(1)}, u32[]{:S(2)}, u32[]{:S(2)}) collective-permute-start(f32[48,256]{1,0:T(8,128)S(1)} %get-tuple-element.16.own_z), channel_id=1, source_target_pairs={{1,2},{3,4},{5,6},{2,1},{4,3},{6,5},{9,10},{11,12},{13,14},{10,9},... | collective-permute-start | bytes 147464 | tf_op jit(solution)/shard_map/ppermute | solution.py:608
  10.0 2.5 %collective-permute-done.2.side_s.got_s = f32[48,256]{1,0:T(8,128)S(1)} collective-permute-done((f32[48,256]{1,0:T(8,128)S(1)}, f32[48,256]{1,0:T(8,128)S(1)}, u32[]{:S(2)}, u32[]{:S(2)}) %collective-permute-start.2) | collective-permute-done | bytes 49184 | tf_op jit(solution)/shard_map/ppermute | solution.py:608
  12.6 0.0 collective-permute-done.3.side_z.got_z
  12.6 1.1 %shard_map.63 = (f32[3,32,512]{2,1,0:T(8,128)S(1)}, f32[8,128]{1,0:T(8,128)S(1)}) custom-call(f32[48,512]{1,0:T(8,128)S(1)} %get-tuple-element.17.wide, f32[48,256]{1,0:T(8,128)S(1)} %get-tuple-element.15.own_s, f32[48,256]{1,0:T(8,128)S(1)} %get-tuple-element.16.own_z, f32[48,256]{1,0:T(8,128)S(1)} %collective-permute-done.2.side_s.got_s, ...), custom_call_target="tpu_custom_call" | custom-call | flops 983040 | bytes 495616 | tf_op jit(solution)/shard_map/pallas_call | solution.py:591
  13.7 0.7 %broadcast_in_dim.9 = f32[256,1,128]{2,1,0:T(1,128)} broadcast(f32[128]{0:T(128)S(1)} %slice_bitcast_fusion), dimensions={2} | broadcast | bytes 131584 | tf_op jit(solution)/shard_map/broadcast_in_dim | solution.py:674
  14.4 19.1 %all-to-all-start = ((f32[256,1,128]{2,1,0:T(1,128)}), f32[256,1,128]{2,1,0:T(1,128)S(1)}, u32[]{:S(2)}, u32[]{:S(2)}) async-start(f32[256,1,128]{2,1,0:T(1,128)} %broadcast_in_dim.9), calls=%async_computation | async-start | bytes 262144 | tf_op jit(solution)/shard_map/all_to_all | solution.py:675
  33.6 3.1 %shard_map.62 = f32[19,32,512]{2,1,0:T(8,128)} custom-call(f32[19,32,512]{2,1,0:T(8,128)} %forward_far.1, f32[19,32,512]{2,1,0:T(8,128)} %adjoint_far.1, f32[32,512]{1,0:T(8,128)} %design_far.1, s32[32,512]{1,0:T(8,128)} %node_far.1, f32[24,512]{1,0:T(8,128)S(1)} %collective-permute-done.got_s, f32[24,512]{1,0:T(8,128)S(1)} %collective-permute-done.1.got_z, ...), custom_call_target="tpu_custom_call" | custom-call | flops 6553600 | bytes 4063232 | tf_op jit(solution)/shard_map/pallas_call | solution.py:591
  36.6 9.7 %all-to-all-done = f32[256,1,128]{2,1,0:T(1,128)S(1)} async-done(((f32[256,1,128]{2,1,0:T(1,128)}), f32[256,1,128]{2,1,0:T(1,128)S(1)}, u32[]{:S(2)}, u32[]{:S(2)}) %all-to-all-start) | async-done | bytes 131104 | tf_op jit(solution)/shard_map/all_to_all | solution.py:675
  46.3 0.8 %shard_map.64 = f32[32,512]{1,0:T(8,128)} custom-call(f32[256,128]{1,0:T(8,128)S(1)} %bitcast.3, f32[3,32,512]{2,1,0:T(8,128)S(1)} %get-tuple-element.19.basis), custom_call_target="tpu_custom_call" | custom-call | flops 163840 | bytes 393216 | tf_op jit(solution)/shard_map/pallas_call | solution.py:591
  (1 shorter events, 0.0 us)
Async XLA Ops:
  2.2 5.4 %collective-permute-start = (f32[24,512]{1,0:T(8,128)S(1)}, f32[24,512]{1,0:T(8,128)S(1)}, u32[]{:S(2)}, u32[]{:S(2)}) collective-permute-start(f32[24,512]{1,0:T(8,128)S(1)} %get-tuple-element.11.own_s), channel_id=1, source_target_pairs={{0,8},{8,0},{16,24},{24,16},{32,40},{40,32},{48,56},{56,48},{64,72... | collective-permute-start | bytes 147464 | tf_op jit(solution)/shard_map/ppermute | solution.py:608
  5.5 3.5 %collective-permute-start.1 = (f32[24,512]{1,0:T(8,128)S(1)}, f32[24,512]{1,0:T(8,128)S(1)}, u32[]{:S(2)}, u32[]{:S(2)}) collective-permute-start(f32[24,512]{1,0:T(8,128)S(1)} %get-tuple-element.12.own_z), channel_id=1, source_target_pairs={{8,16},{24,32},{40,48},{56,64},{72,80},{88,96},{104,112},{120,128}... | collective-permute-start | bytes 147464 | tf_op jit(solution)/shard_map/ppermute | solution.py:608
  9.3 3.3 %collective-permute-start.2 = (f32[48,256]{1,0:T(8,128)S(1)}, f32[48,256]{1,0:T(8,128)S(1)}, u32[]{:S(2)}, u32[]{:S(2)}) collective-permute-start(f32[48,256]{1,0:T(8,128)S(1)} %get-tuple-element.15.own_s), channel_id=1, source_target_pairs={{0,1},{1,0},{2,3},{3,2},{4,5},{5,4},{6,7},{7,6},{8,9},{9,8},{10,11... | collective-permute-start | bytes 147464 | tf_op jit(solution)/shard_map/ppermute | solution.py:608
  9.4 3.2 %collective-permute-start.3 = (f32[48,256]{1,0:T(8,128)S(1)}, f32[48,256]{1,0:T(8,128)S(1)}, u32[]{:S(2)}, u32[]{:S(2)}) collective-permute-start(f32[48,256]{1,0:T(8,128)S(1)} %get-tuple-element.16.own_z), channel_id=1, source_target_pairs={{1,2},{3,4},{5,6},{2,1},{4,3},{6,5},{9,10},{11,12},{13,14},{10,9},... | collective-permute-start | bytes 147464 | tf_op jit(solution)/shard_map/ppermute | solution.py:608
  14.4 31.9 %all-to-all-start = ((f32[256,1,128]{2,1,0:T(1,128)}), f32[256,1,128]{2,1,0:T(1,128)S(1)}, u32[]{:S(2)}, u32[]{:S(2)}) async-start(f32[256,1,128]{2,1,0:T(1,128)} %broadcast_in_dim.9), calls=%async_computation | async-start | bytes 262144 | tf_op jit(solution)/shard_map/all_to_all | solution.py:675

commit v4 on v3

--- a/solution.py
+++ b/solution.py
@@ -1,3 +1,5 @@
+import functools
+
 import jax
 import jax.numpy as jnp
 from jax import lax
@@ -152,52 +154,52 @@
     return jnp.concatenate(packed, axis=1)
 
 
-def border_kernel(forward, adjoint, node_type, out_s, out_z, moving, carried, kinds, sems):
+def border_kernel(near, forward, adjoint, node_type, out, moving, carried, kinds, sems):
     layers, columns = node_type.shape
-    copies = []
-    for place, start in enumerate((0, layers - ROWS)):
-        rows = pl.ds(start, ROWS)
-        copies.append(pltpu.make_async_copy(node_type.at[rows, :], kinds.at[place], sems.at[place]))
+    odd = lax.axis_index("gx") & 1
+    up = 1 - odd if near else odd
+    rows = pl.ds(pl.multiple_of(up * (layers - ROWS), ROWS), ROWS)
+    half = forward.shape[0] // 2
+    copies = [pltpu.make_async_copy(node_type.at[rows, :], kinds, sems.at[0])]
     for source, target in ((forward, moving), (adjoint, carried)):
-        for place, start in enumerate((0, layers - ROWS)):
-            part = source.at[:, pl.ds(start, ROWS), :]
-            copies.append(pltpu.make_async_copy(part, target.at[place], sems.at[len(copies)]))
+        for members in (pl.ds(0, half), pl.ds(half, forward.shape[0] - half)):
+            copies.append(
+                pltpu.make_async_copy(
+                    source.at[members, rows, :], target.at[members], sems.at[len(copies)]
+                )
+            )
     for copy in copies:
         copy.start()
+    for copy in copies[:3]:
+        copy.wait()
+    gains = gains_of(lambda member: moving[member], kinds[...])
+    for copy in copies[3:]:
+        copy.wait()
     row = iota((ROWS, columns), 0)
-    for place in range(2):
-        copies[place].wait()
-    gains = []
-    for place in range(2):
-        copies[2 + place].wait()
-        gains.append(gains_of(lambda member: moving[place, member], kinds[place]))
-    packs = []
-    for place in range(2):
-        copies[4 + place].wait()
-
-        def rows_of(member, step):
-            value = carried[place, member]
-            if step == 0:
-                return value
-            if step > 0:
-                return jnp.where(row < ROWS - 1, roll(value, ROWS - 1, 0), 0.0)
-            return jnp.where(row > 0, roll(value, 1, 0), 0.0)
-
-        top = inner_sensitivity(gains[place], rows_of)
-        edge = pack_edges(gains[place], lambda member: carried[place, member])
-        faces = jnp.zeros((ROWS, columns), jnp.float32)
-        last = place * (ROWS - 1)
-        base = 3 * (1 - place)
-        for index, k in enumerate(X_PAIRS):
-            member = member_of(k, 1 - 2 * place)
-            top = jnp.where(row == base + index, gains[place][k][last : last + 1, :], top)
-            faces = jnp.where(row == index, carried[place, member, last : last + 1, :], faces)
-        packs.append((top, edge, faces))
-    even = (lax.axis_index("gx") & 1) == 0
-    for part in range(3):
-        rows = slice(part * ROWS, part * ROWS + ROWS)
-        out_s[rows, :] = jnp.where(even, packs[1][part], packs[0][part])
-        out_z[rows, :] = jnp.where(even, packs[0][part], packs[1][part])
+
+    def rows_of(member, step):
+        value = carried[member]
+        if step == 0:
+            return value
+        if step > 0:
+            return jnp.where(row < ROWS - 1, roll(value, ROWS - 1, 0), 0.0)
+        return jnp.where(row > 0, roll(value, 1, 0), 0.0)
+
+    def border(value):
+        return jnp.where(up == 1, value[ROWS - 1 :, :], value[:1, :])
+
+    top = inner_sensitivity(gains, rows_of)
+    faces = jnp.zeros((ROWS, columns), jnp.float32)
+    base = 3 * (1 - up)
+    for index, k in enumerate(X_PAIRS):
+        top = jnp.where(row == base + index, border(gains[k]), top)
+        outward = jnp.where(
+            up == 1, carried[2 * k + 2, ROWS - 1 :, :], carried[2 * k + 1, :1, :]
+        )
+        faces = jnp.where(row == index, outward, faces)
+    out[:ROWS, :] = top
+    out[ROWS : 2 * ROWS, :] = pack_edges(gains, lambda member: carried[member])
+    out[2 * ROWS :, :] = faces
 
 
 def fetch_tiles(sources, targets, sems):
@@ -284,15 +286,17 @@
     far_first = completion(face_reads(up[2], -1), roll(above[0], -3, 0))
     far_last = completion(face_reads(down[2], 1), below[0])
     last = ROWS - 1
-    wide[:ROWS, :] = below[0] + jnp.where(row == last, far_last, 0.0)
-    wide[ROWS : 2 * ROWS, :] = partial[:ROWS, :] - jnp.where(row == 0, own_first, 0.0)
-    wide[2 * ROWS : layers, :] = partial[ROWS : layers - ROWS, :]
-    wide[layers : layers + ROWS, :] = partial[layers - ROWS :, :] + jnp.where(
+    wide[:ROWS, :] = partial[:ROWS, :] - jnp.where(row == 0, own_first, 0.0)
+    wide[ROWS : layers - ROWS, :] = partial[ROWS : layers - ROWS, :]
+    wide[layers - ROWS : layers, :] = partial[layers - ROWS :, :] + jnp.where(
         row == last, own_last, 0.0
     )
-    wide[layers + ROWS :, :] = above[0] - jnp.where(row == 0, far_first, 0.0)
-
-    edge = jnp.concatenate([below[1], edges[...], above[1]], axis=0)
+    halo = jnp.where(row < ROWS // 2, above[0], below[0])
+    halo = halo - jnp.where(row == 0, far_first, 0.0) + jnp.where(row == last, far_last, 0.0)
+    wide[layers:, :] = halo
+
+    halo = jnp.where(row < ROWS // 2, above[1], below[1])
+    edge = jnp.concatenate([edges[...], halo], axis=0)
     half = edge.shape[1] // 2
     low = outgoing(edge[:, :half], 1)
     high = outgoing(edge[:, half:], -1)
@@ -309,6 +313,10 @@
         out_z[:, lanes] = jnp.where(even_y, to_left[part], to_right[part])
 
 
+def hand_on_kernel(first, second, out):
+    out[...] = first[...]
+
+
 def fold(reads, gains, way):
     moved = roll(reads, -READS, 1)[:, :128]
     gains = gains[:, :128]
@@ -369,21 +377,21 @@
     low_end = field[:, :128] + fold(left, to_left, -1)
     high_end = field[:, columns - 128 :] + roll(fold(right, to_right, 1), 128 - NZ, 1)
     right_halo = jnp.where(lane < 3 * NZ, roll(right[:, 128:], 128 - EDGE, 1), 0.0)
-    right_halo = right_halo + fold(to_right, right, -1)
     left_halo = jnp.where(
         lane >= 128 - 3 * NZ, roll(left[:, 128:], 128 - 3 * NZ - (EDGE - 128), 1), 0.0
     )
-    left_halo = left_halo + roll(fold(to_left, left, 1), 128 - NZ, 1)
-    field = jnp.concatenate(
-        [left_halo, low_end, field[:, 128 : columns - 128], high_end, right_halo], axis=1
-    )
+    halo = right_halo + fold(to_right, right, -1)
+    halo = halo + (left_halo + roll(fold(to_left, left, 1), 128 - NZ, 1))
+    field = jnp.concatenate([low_end, field[:, 128 : columns - 128], high_end, halo], axis=1)
     column = iota(field.shape, 1)
     depth = column & (NZ - 1)
-    inside = ((column >= 128) | (place > 0)) & ((column < 128 + columns) | (place < last_place))
+    on_right = (column < columns + 64) & (place < last_place)
+    on_left = (column >= columns + 64) & (place > 0)
+    inside = (column < columns) | on_right | on_left
     first = laplace(field, depth, inside)
     second = laplace(first, depth, inside)
     third = laplace(second, depth, None)
-    cores = [v[ROWS : rows - ROWS, 128 : 128 + columns] for v in (field, first, second, third)]
+    cores = [v[: basis.shape[1], :columns] for v in (field, first, second, third)]
     for power in range(ITERS):
         basis[power] = cores[power]
     row = jnp.zeros((1, 128), jnp.float32)
@@ -486,9 +494,8 @@
     column = iota(shape, 1)
     for tile in range(tiles):
         rows = slice(tile * ROWS, tile * ROWS + ROWS)
-        wide_rows = slice(tile * ROWS + ROWS, tile * ROWS + 2 * ROWS)
-        right = jnp.where(even_y, side_s[wide_rows, :], side_z[wide_rows, :])
-        left = jnp.where(even_y, side_z[wide_rows, :], side_s[wide_rows, :])
+        right = jnp.where(even_y, side_s[rows, :], side_z[rows, :])
+        left = jnp.where(even_y, side_z[rows, :], side_s[rows, :])
         take(groups, tile)
         density = forward[0, rows, :]
         differences = []
@@ -601,11 +608,11 @@
 
 def swap(first, second, axis, closed):
     count = lax.axis_size(axis)
-    near = [(i, i ^ 1) for i in range(count)]
     starts = range(1, count if closed else count - 1, 2)
     far = [(i, (i + 1) % count) for i in starts]
     far = far + [(b, a) for a, b in far]
-    return lax.ppermute(first, axis, near), lax.ppermute(second, axis, far)
+    near = [(i, i ^ 1) for i in range(count)]
+    return lax.ppermute(first, axis, far), lax.ppermute(second, axis, near)
 
 
 def shards(forward, adjoint, design, node_type):
@@ -614,26 +621,33 @@
     devices = lax.axis_size("gx") * lax.axis_size("gy")
     plane = (layers, columns)
     face = (3 * ROWS, columns)
-    side = (layers + 2 * ROWS, 256)
+    side = (layers + ROWS, 256)
     tiles = layers // ROWS
     field = pltpu.VMEM((members,) + plane, jnp.float32)
-    ends = pltpu.VMEM((2, members, ROWS, columns), jnp.float32)
-    own_s, own_z = run(
-        border_kernel,
-        [face, face],
-        forward,
-        adjoint,
-        node_type,
-        far=3,
-        scratch=[
-            ends,
-            ends,
-            pltpu.VMEM((2, ROWS, columns), jnp.int32),
-            pltpu.SemaphoreType.DMA((6,)),
-        ],
-        flops=80 * sites,
-    )
-    got_s, got_z = swap(own_s, own_z, "gx", True)
+    end = pltpu.VMEM((members, ROWS, columns), jnp.float32)
+
+    def border(near):
+        (message,) = run(
+            functools.partial(border_kernel, near),
+            [face],
+            forward,
+            adjoint,
+            node_type,
+            far=3,
+            scratch=[
+                end,
+                end,
+                pltpu.VMEM((ROWS, columns), jnp.int32),
+                pltpu.SemaphoreType.DMA((5,)),
+            ],
+            flops=40 * sites,
+        )
+        return message
+
+    own_z = border(False)
+    own_s = border(True)
+    got_z, got_s = swap(own_z, own_s, "gx", True)
+    got_z = lax.optimization_barrier(got_z)
     partial, edges = run(
         collide_kernel,
         [plane, (layers, 512)],
@@ -651,7 +665,7 @@
     )
     wide, out_s, out_z = run(
         faces_kernel,
-        [(layers + 2 * ROWS, columns), side, side],
+        [(layers + ROWS, columns), side, side],
         partial,
         edges,
         own_s,
@@ -660,7 +674,8 @@
         got_z,
         flops=10 * sites,
     )
-    side_s, side_z = swap(out_s, out_z, "gy", False)
+    side_z, side_s = swap(out_z, out_s, "gy", False)
+    side_z = lax.optimization_barrier(side_z)
     basis, shares = run(
         krylov_kernel,
         [(ITERS,) + plane, (ROWS, 128)],

time: 47.4 us -> 46.1 us (0.973)
  waiting for transfers between devices: 13.7 us -> 11.1 us
  Pallas kernels: 8.8 us -> 9.76 us
    ppermute x4, starting transfers between devices: 4.09 us -> 14 us  [swap(): return (lax.ppermute(first, axis, far), lax.ppermute(second, axis, near))]
    all_to_all x1, starting transfers between devices: 19.1 us -> 9.45 us  [shards(): spread = lax.all_to_all(copies, ('gx', 'gy'), 0, 0)]
    ppermute x4, waiting for transfers between devices: 4.02 us -> 1.4 us  [swap(): return (lax.ppermute(first, axis, far), lax.ppermute(second, axis, near))]
    pallas_call x6 -> x7, Pallas kernels: 8.8 us -> 9.76 us  [run(): pl.pallas_call(kernel, out_shape=sizes, in_specs=[away if i < far else ne...]
  transfers between devices with their start and end apart: 5 -> 5, of which waited for: 3 -> 2; matrix products, arithmetic and copies ran while one was open for 0% -> 0% of each run, Pallas kernels for 11% -> 14%
where the time goes in v4:
time: 46.1 us; the launch traced here: 45.7 us
  starting transfers between devices  23.5 us (51%)
  waiting for transfers between devices  11.1 us (24%)
  Pallas kernels  9.76 us (21%)
  local copies, waits for them, and re-layouts  0.73 us (2%)
  between operations  0.7 us (2%)
    ppermute x4, starting transfers between devices, swap(): return (lax.ppermute(first, axis, far), lax.ppermute(second, axis, near))  14 us
    pallas_call x7, Pallas kernels, run(): pl.pallas_call(kernel, out_shape=sizes, in_specs=[away if i < far else ne...  9.76 us
    all_to_all x1, waiting for transfers between devices, shards(): spread = lax.all_to_all(copies, ('gx', 'gy'), 0, 0)  9.67 us
    all_to_all x1, starting transfers between devices, shards(): spread = lax.all_to_all(copies, ('gx', 'gy'), 0, 0)  9.45 us
    ppermute x4, waiting for transfers between devices, swap(): return (lax.ppermute(first, axis, far), lax.ppermute(second, axis, near))  1.4 us
  transfers between devices with their start and end apart: 5, of which 2 were waited for; matrix products, arithmetic and copies ran while one was open for 0% of the time, Pallas kernels for 14%

profile of v4, /device:TPU:1, one launch (start us, length us, event | category | flops | bytes accessed | tf_op | source)
XLA Modules:
  0.0 45.7 jit_solution(4936669946989246308)
XLA Ops:
  0.6 1.4 %shard_map.60.own_z = f32[24,512]{1,0:T(8,128)S(1)} custom-call(f32[19,32,512]{2,1,0:T(8,128)} %forward_far.1, f32[19,32,512]{2,1,0:T(8,128)} %adjoint_far.1, s32[32,512]{1,0:T(8,128)} %node_far.1), custom_call_target="tpu_custom_call" | custom-call | flops 655360 | bytes 2605056 | tf_op jit(solution)/shard_map/pallas_call | solution.py:598
  2.0 3.1 %collective-permute-start.1 = (f32[24,512]{1,0:T(8,128)S(1)}, f32[24,512]{1,0:T(8,128)S(1)}, u32[]{:S(2)}, u32[]{:S(2)}) collective-permute-start(f32[24,512]{1,0:T(8,128)S(1)} %shard_map.60.own_z), channel_id=1, source_target_pairs={{8,16},{24,32},{40,48},{56,64},{72,80},{88,96},{104,112},{120,128}... | collective-permute-start | bytes 147464 | tf_op jit(solution)/shard_map/ppermute | solution.py:615
  5.1 1.4 %shard_map.59.own_s = f32[24,512]{1,0:T(8,128)S(1)} custom-call(f32[19,32,512]{2,1,0:T(8,128)} %forward_far.1, f32[19,32,512]{2,1,0:T(8,128)} %adjoint_far.1, s32[32,512]{1,0:T(8,128)} %node_far.1), custom_call_target="tpu_custom_call" | custom-call | flops 655360 | bytes 2605056 | tf_op jit(solution)/shard_map/pallas_call | solution.py:598
  6.5 6.3 %collective-permute-start = (f32[24,512]{1,0:T(8,128)S(1)}, f32[24,512]{1,0:T(8,128)S(1)}, u32[]{:S(2)}, u32[]{:S(2)}) collective-permute-start(f32[24,512]{1,0:T(8,128)S(1)} %shard_map.59.own_s), channel_id=1, source_target_pairs={{0,8},{8,0},{16,24},{24,16},{32,40},{40,32},{48,56},{56,48},{64,72... | collective-permute-start | bytes 147464 | tf_op jit(solution)/shard_map/ppermute | solution.py:615
  12.8 2.0 %shard_map.61 = (f32[32,512]{1,0:T(8,128)S(1)}, f32[32,512]{1,0:T(8,128)S(1)}) custom-call(f32[19,32,512]{2,1,0:T(8,128)} %forward_far.1, f32[19,32,512]{2,1,0:T(8,128)} %adjoint_far.1, s32[32,512]{1,0:T(8,128)} %node_far.1), custom_call_target="tpu_custom_call" | custom-call | flops 2457600 | bytes 2686976 | tf_op jit(solution)/shard_map/pallas_call | solution.py:598
  14.8 0.0 collective-permute-done.1.got_z
  14.8 0.0 collective-permute-done.got_s
  14.9 0.2 shard_map.62
  15.1 0.7 %collective-permute-start.3 = (f32[40,256]{1,0:T(8,128)S(1)}, f32[40,256]{1,0:T(8,128)S(1)}, u32[]{:S(2)}, u32[]{:S(2)}) collective-permute-start(f32[40,256]{1,0:T(8,128)S(1)} %get-tuple-element.12.own_z), channel_id=1, source_target_pairs={{1,2},{3,4},{5,6},{2,1},{4,3},{6,5},{9,10},{11,12},{13,14},{10,9},... | collective-permute-start | bytes 122888 | tf_op jit(solution)/shard_map/ppermute | solution.py:615
  15.7 3.9 %collective-permute-start.2 = (f32[40,256]{1,0:T(8,128)S(1)}, f32[40,256]{1,0:T(8,128)S(1)}, u32[]{:S(2)}, u32[]{:S(2)}) collective-permute-start(f32[40,256]{1,0:T(8,128)S(1)} %get-tuple-element.11.own_s), channel_id=1, source_target_pairs={{0,1},{1,0},{2,3},{3,2},{4,5},{5,4},{6,7},{7,6},{8,9},{9,8},{10,11... | collective-permute-start | bytes 122888 | tf_op jit(solution)/shard_map/ppermute | solution.py:615
  19.7 0.0 collective-permute-done.3.side_z.got_z
  19.7 1.4 %collective-permute-done.2.side_s.got_s = f32[40,256]{1,0:T(8,128)S(1)} collective-permute-done((f32[40,256]{1,0:T(8,128)S(1)}, f32[40,256]{1,0:T(8,128)S(1)}, u32[]{:S(2)}, u32[]{:S(2)}) %collective-permute-start.2) | collective-permute-done | bytes 40992 | tf_op jit(solution)/shard_map/ppermute | solution.py:615
  21.1 0.9 %shard_map.64 = (f32[3,32,512]{2,1,0:T(8,128)S(1)}, f32[8,128]{1,0:T(8,128)S(1)}) custom-call(f32[40,512]{1,0:T(8,128)S(1)} %get-tuple-element.13.wide, f32[40,256]{1,0:T(8,128)S(1)} %get-tuple-element.11.own_s, f32[40,256]{1,0:T(8,128)S(1)} %get-tuple-element.12.own_z, f32[40,256]{1,0:T(8,128)S(1)} %collective-permute-done.2.side_s.got_s, ...), custom_call_target="tpu_custom_call" | custom-call | flops 983040 | bytes 446464 | tf_op jit(solution)/shard_map/pallas_call | solution.py:598
  22.0 0.7 %broadcast_in_dim.9 = f32[256,1,128]{2,1,0:T(1,128)} broadcast(f32[128]{0:T(128)S(1)} %slice_bitcast_fusion), dimensions={2} | broadcast | bytes 131584 | tf_op jit(solution)/shard_map/broadcast_in_dim | solution.py:689
  22.7 9.5 %all-to-all-start = ((f32[256,1,128]{2,1,0:T(1,128)}), f32[256,1,128]{2,1,0:T(1,128)S(1)}, u32[]{:S(2)}, u32[]{:S(2)}) async-start(f32[256,1,128]{2,1,0:T(1,128)} %broadcast_in_dim.9), calls=%async_computation | async-start | bytes 262144 | tf_op jit(solution)/shard_map/all_to_all | solution.py:690
  32.1 3.1 %shard_map.63 = f32[19,32,512]{2,1,0:T(8,128)} custom-call(f32[19,32,512]{2,1,0:T(8,128)} %forward_far.1, f32[19,32,512]{2,1,0:T(8,128)} %adjoint_far.1, f32[32,512]{1,0:T(8,128)} %design_far.1, s32[32,512]{1,0:T(8,128)} %node_far.1, f32[24,512]{1,0:T(8,128)S(1)} %collective-permute-done.got_s, f32[24,512]{1,0:T(8,128)S(1)} %collective-permute-done.1.got_z, ...), custom_call_target="tpu_custom_call" | custom-call | flops 6553600 | bytes 4046848 | tf_op jit(solution)/shard_map/pallas_call | solution.py:598
  35.2 9.7 %all-to-all-done = f32[256,1,128]{2,1,0:T(1,128)S(1)} async-done(((f32[256,1,128]{2,1,0:T(1,128)}), f32[256,1,128]{2,1,0:T(1,128)S(1)}, u32[]{:S(2)}, u32[]{:S(2)}) %all-to-all-start) | async-done | bytes 131104 | tf_op jit(solution)/shard_map/all_to_all | solution.py:690
  44.9 0.8 %shard_map.65 = f32[32,512]{1,0:T(8,128)} custom-call(f32[256,128]{1,0:T(8,128)S(1)} %bitcast.3, f32[3,32,512]{2,1,0:T(8,128)S(1)} %get-tuple-element.15.basis), custom_call_target="tpu_custom_call" | custom-call | flops 163840 | bytes 393216 | tf_op jit(solution)/shard_map/pallas_call | solution.py:598
  (1 shorter events, 0.0 us)
Async XLA Ops:
  2.0 12.8 %collective-permute-start.1 = (f32[24,512]{1,0:T(8,128)S(1)}, f32[24,512]{1,0:T(8,128)S(1)}, u32[]{:S(2)}, u32[]{:S(2)}) collective-permute-start(f32[24,512]{1,0:T(8,128)S(1)} %shard_map.60.own_z), channel_id=1, source_target_pairs={{8,16},{24,32},{40,48},{56,64},{72,80},{88,96},{104,112},{120,128}... | collective-permute-start | bytes 147464 | tf_op jit(solution)/shard_map/ppermute | solution.py:615
  6.5 8.4 %collective-permute-start = (f32[24,512]{1,0:T(8,128)S(1)}, f32[24,512]{1,0:T(8,128)S(1)}, u32[]{:S(2)}, u32[]{:S(2)}) collective-permute-start(f32[24,512]{1,0:T(8,128)S(1)} %shard_map.59.own_s), channel_id=1, source_target_pairs={{0,8},{8,0},{16,24},{24,16},{32,40},{40,32},{48,56},{56,48},{64,72... | collective-permute-start | bytes 147464 | tf_op jit(solution)/shard_map/ppermute | solution.py:615
  15.1 4.6 %collective-permute-start.3 = (f32[40,256]{1,0:T(8,128)S(1)}, f32[40,256]{1,0:T(8,128)S(1)}, u32[]{:S(2)}, u32[]{:S(2)}) collective-permute-start(f32[40,256]{1,0:T(8,128)S(1)} %get-tuple-element.12.own_z), channel_id=1, source_target_pairs={{1,2},{3,4},{5,6},{2,1},{4,3},{6,5},{9,10},{11,12},{13,14},{10,9},... | collective-permute-start | bytes 122888 | tf_op jit(solution)/shard_map/ppermute | solution.py:615
  15.7 5.3 %collective-permute-start.2 = (f32[40,256]{1,0:T(8,128)S(1)}, f32[40,256]{1,0:T(8,128)S(1)}, u32[]{:S(2)}, u32[]{:S(2)}) collective-permute-start(f32[40,256]{1,0:T(8,128)S(1)} %get-tuple-element.11.own_s), channel_id=1, source_target_pairs={{0,1},{1,0},{2,3},{3,2},{4,5},{5,4},{6,7},{7,6},{8,9},{9,8},{10,11... | collective-permute-start | bytes 122888 | tf_op jit(solution)/shard_map/ppermute | solution.py:615
  22.7 22.2 %all-to-all-start = ((f32[256,1,128]{2,1,0:T(1,128)}), f32[256,1,128]{2,1,0:T(1,128)S(1)}, u32[]{:S(2)}, u32[]{:S(2)}) async-start(f32[256,1,128]{2,1,0:T(1,128)} %broadcast_in_dim.9), calls=%async_computation | async-start | bytes 262144 | tf_op jit(solution)/shard_map/all_to_all | solution.py:690

commit v5 on v4

--- a/solution.py
+++ b/solution.py
@@ -27,8 +27,9 @@
 relax_rate = 1.25
 radius_sq = 4.0
 ROWS = 8
-READS = 80
-EDGE = 160
+READS = 128
+EDGE = 208
+SPARE = 80
 
 
 def iota(shape, axis):
@@ -109,11 +110,12 @@
     shape = (ROWS, 128)
     lane = iota(shape, 1)
     halves = [jnp.zeros(shape, jnp.float32), jnp.zeros(shape, jnp.float32)]
-    for place, value in enumerate(list(gains) + list(populations)):
-        columns = value.shape[1]
-        part = value[:, :128] if not high else value[:, columns - 128 :]
-        half, start = divmod(place * NZ, 128)
-        halves[half] = jnp.where(block_at(lane, start), roll(part, start - origin, 1), halves[half])
+    for half, values in enumerate((gains, populations)):
+        for place, value in enumerate(values):
+            columns = value.shape[1]
+            part = value[:, :128] if not high else value[:, columns - 128 :]
+            moved = roll(part, place * NZ - origin, 1)
+            halves[half] = jnp.where(block_at(lane, place * NZ), moved, halves[half])
     return jnp.concatenate(halves, axis=1)
 
 
@@ -154,15 +156,49 @@
     return jnp.concatenate(packed, axis=1)
 
 
+def fourth(up, high):
+    place = 1 if up == high else 2
+    return READS + place * NZ
+
+
+def stow(edge, up):
+    half = edge.shape[1] // 2
+    lane = iota((ROWS, half), 1)
+    sides = []
+    for high in (False, True):
+        part = edge[:, half : 2 * half] if high else edge[:, :half]
+        below = roll(roll(part, 1, 0), SPARE - fourth(True, high), 1)
+        above = roll(roll(part, -1, 0), SPARE - fourth(False, high), 1)
+        sides.append(jnp.where(block_at(lane, SPARE), jnp.where(up, below, above), part))
+    return jnp.concatenate(sides, axis=1)
+
+
+def unstow(halo):
+    half = halo.shape[1] // 2
+    lane = iota((ROWS, half), 1)
+    row = iota((ROWS, half), 0)
+    sides = []
+    for high in (False, True):
+        part = halo[:, half : 2 * half] if high else halo[:, :half]
+        result = part
+        for up, at, step in ((False, 3, 1), (True, 4, -1)):
+            start = fourth(up, high)
+            moved = roll(roll(part, step, 0), start - SPARE, 1)
+            result = jnp.where((row == at) & block_at(lane, start), moved, result)
+        sides.append(result)
+    return jnp.concatenate(sides, axis=1)
+
+
 def border_kernel(near, forward, adjoint, node_type, out, moving, carried, kinds, sems):
     layers, columns = node_type.shape
     odd = lax.axis_index("gx") & 1
     up = 1 - odd if near else odd
     rows = pl.ds(pl.multiple_of(up * (layers - ROWS), ROWS), ROWS)
-    half = forward.shape[0] // 2
+    cuts = (1, 10, 19)
     copies = [pltpu.make_async_copy(node_type.at[rows, :], kinds, sems.at[0])]
     for source, target in ((forward, moving), (adjoint, carried)):
-        for members in (pl.ds(0, half), pl.ds(half, forward.shape[0] - half)):
+        for low, high in zip(cuts, cuts[1:]):
+            members = pl.ds(low, high - low)
             copies.append(
                 pltpu.make_async_copy(
                     source.at[members, rows, :], target.at[members], sems.at[len(copies)]
@@ -189,17 +225,16 @@
         return jnp.where(up == 1, value[ROWS - 1 :, :], value[:1, :])
 
     top = inner_sensitivity(gains, rows_of)
-    faces = jnp.zeros((ROWS, columns), jnp.float32)
+    edge = stow(pack_edges(gains, lambda member: carried[member]), up == 1)
     base = 3 * (1 - up)
     for index, k in enumerate(X_PAIRS):
         top = jnp.where(row == base + index, border(gains[k]), top)
         outward = jnp.where(
             up == 1, carried[2 * k + 2, ROWS - 1 :, :], carried[2 * k + 1, :1, :]
         )
-        faces = jnp.where(row == index, outward, faces)
+        edge = jnp.where(row == base + index, outward, edge)
     out[:ROWS, :] = top
-    out[ROWS : 2 * ROWS, :] = pack_edges(gains, lambda member: carried[member])
-    out[2 * ROWS :, :] = faces
+    out[ROWS:, :] = edge
 
 
 def fetch_tiles(sources, targets, sems):
@@ -272,19 +307,20 @@
         rows = slice(part * ROWS, part * ROWS + ROWS)
         return jnp.where(even, first[rows, :], second[rows, :])
 
-    up = [pick(own_s, own_z, part) for part in range(3)]
-    down = [pick(own_z, own_s, part) for part in range(3)]
-    above = [pick(got_s, got_z, part) for part in range(3)]
-    below = [pick(got_z, got_s, part) for part in range(3)]
+    up = [pick(own_s, own_z, part) for part in range(2)]
+    down = [pick(own_z, own_s, part) for part in range(2)]
+    above = [pick(got_s, got_z, part) for part in range(2)]
+    below = [pick(got_z, got_s, part) for part in range(2)]
     row = iota((ROWS, columns), 0)
 
     def completion(reads, gains):
-        return jnp.sum(reads * gains, axis=0, keepdims=True)
-
-    own_last = completion(face_reads(above[2], 1), up[0])
-    own_first = completion(face_reads(below[2], -1), roll(down[0], -3, 0))
-    far_first = completion(face_reads(up[2], -1), roll(above[0], -3, 0))
-    far_last = completion(face_reads(down[2], 1), below[0])
+        product = jnp.where(row < len(X_PAIRS), reads * gains, 0.0)
+        return jnp.sum(product, axis=0, keepdims=True)
+
+    own_last = completion(face_reads(roll(above[1], -3, 0), 1), up[0])
+    own_first = completion(face_reads(below[1], -1), roll(down[0], -3, 0))
+    far_first = completion(face_reads(up[1], -1), roll(above[0], -3, 0))
+    far_last = completion(face_reads(roll(down[1], -3, 0), 1), below[0])
     last = ROWS - 1
     wide[:ROWS, :] = partial[:ROWS, :] - jnp.where(row == 0, own_first, 0.0)
     wide[ROWS : layers - ROWS, :] = partial[ROWS : layers - ROWS, :]
@@ -295,7 +331,7 @@
     halo = halo - jnp.where(row == 0, far_first, 0.0) + jnp.where(row == last, far_last, 0.0)
     wide[layers:, :] = halo
 
-    halo = jnp.where(row < ROWS // 2, above[1], below[1])
+    halo = unstow(jnp.where(row < ROWS // 2, above[1], below[1]))
     edge = jnp.concatenate([edges[...], halo], axis=0)
     half = edge.shape[1] // 2
     low = outgoing(edge[:, :half], 1)
@@ -317,18 +353,23 @@
     out[...] = first[...]
 
 
-def fold(reads, gains, way):
-    moved = roll(reads, -READS, 1)[:, :128]
-    gains = gains[:, :128]
-    lane = iota(gains.shape, 1)
-    product = moved * gains
+def signed_products(reads, gains, way):
+    product = reads[:, READS:] * gains[:, :128]
+    lane = iota(product.shape, 1)
     for place, k in enumerate(Y_PAIRS):
         if way * PAIRS[k][1] < 0:
             product = jnp.where(block_at(lane, place * NZ), -product, product)
-    total = product
-    for place in range(1, len(Y_PAIRS)):
-        total = total + roll(product, -place * NZ, 1)
-    return jnp.where(lane < NZ, total, 0.0)
+    return product
+
+
+def fold(first, second):
+    lane = iota(first.shape, 1)
+    total = jnp.where(lane < 64, first, roll(second, 64, 1))
+    total = total + roll(total, -NZ, 1)
+    total = total + roll(total, -2 * NZ, 1)
+    total = total + jnp.where(lane < 64, roll(first, 64, 1), second)
+    low = jnp.where(lane < NZ, total, 0.0)
+    return low, jnp.where(lane >= 128 - NZ, roll(total, 64 - NZ, 1), 0.0)
 
 
 def laplace(field, depth, inside):
@@ -337,8 +378,7 @@
     total = total + (roll(field, NZ, 1) + roll(field, -NZ, 1))
     total = total + jnp.where(depth > 0, roll(field, 1, 1), 0.0)
     total = total + jnp.where(depth < NZ - 1, roll(field, -1, 1), 0.0)
-    result = field - total * (1.0 / 6.0)
-    return result if inside is None else jnp.where(inside, result, 0.0)
+    return jnp.where(inside, field - total * (1.0 / 6.0), 0.0)
 
 
 def tree_sum(parts):
@@ -374,14 +414,15 @@
     left = pick(got_z, got_s)
     lane = iota((rows, 128), 1)
     field = wide[...]
-    low_end = field[:, :128] + fold(left, to_left, -1)
-    high_end = field[:, columns - 128 :] + roll(fold(right, to_right, 1), 128 - NZ, 1)
+    low, high = fold(signed_products(left, to_left, -1), signed_products(right, to_right, 1))
+    low_end = field[:, :128] + low
+    high_end = field[:, columns - 128 :] + high
     right_halo = jnp.where(lane < 3 * NZ, roll(right[:, 128:], 128 - EDGE, 1), 0.0)
     left_halo = jnp.where(
         lane >= 128 - 3 * NZ, roll(left[:, 128:], 128 - 3 * NZ - (EDGE - 128), 1), 0.0
     )
-    halo = right_halo + fold(to_right, right, -1)
-    halo = halo + (left_halo + roll(fold(to_left, left, 1), 128 - NZ, 1))
+    low, high = fold(signed_products(to_right, right, -1), signed_products(to_left, left, 1))
+    halo = (right_halo + low) + (left_halo + high)
     field = jnp.concatenate([low_end, field[:, 128 : columns - 128], high_end, halo], axis=1)
     column = iota(field.shape, 1)
     depth = column & (NZ - 1)
@@ -390,7 +431,9 @@
     inside = (column < columns) | on_right | on_left
     first = laplace(field, depth, inside)
     second = laplace(first, depth, inside)
-    third = laplace(second, depth, None)
+    ahead = roll(second, -1, 0) + roll(second, -NZ, 1)
+    ahead = ahead + jnp.where(depth < NZ - 1, roll(second, -1, 1), 0.0)
+    third = second - ahead * (1.0 / 3.0)
     cores = [v[: basis.shape[1], :columns] for v in (field, first, second, third)]
     for power in range(ITERS):
         basis[power] = cores[power]
@@ -488,7 +531,7 @@
     shape = (ROWS, columns)
     even = (lax.axis_index("gx") & 1) == 0
     even_y = (lax.axis_index("gy") & 1) == 0
-    faces = slice(2 * ROWS, 3 * ROWS)
+    faces = slice(ROWS, 2 * ROWS)
     above = jnp.where(even, got_s[faces, :], got_z[faces, :])
     below = jnp.where(even, got_z[faces, :], got_s[faces, :])
     column = iota(shape, 1)
@@ -527,7 +570,7 @@
                     member,
                     tile,
                     step[0],
-                    above[place : place + 1, :],
+                    above[3 + place : 4 + place, :],
                     below[place : place + 1, :],
                 )
                 if step[1] or step[2]:
@@ -620,7 +663,7 @@
     sites = layers * columns
     devices = lax.axis_size("gx") * lax.axis_size("gy")
     plane = (layers, columns)
-    face = (3 * ROWS, columns)
+    face = (2 * ROWS, columns)
     side = (layers + ROWS, 256)
     tiles = layers // ROWS
     field = pltpu.VMEM((members,) + plane, jnp.float32)
@@ -678,7 +721,7 @@
     side_z = lax.optimization_barrier(side_z)
     basis, shares = run(
         krylov_kernel,
-        [(ITERS,) + plane, (ROWS, 128)],
+        [(ITERS,) + plane, (devices, 128)],
         wide,
         out_s,
         out_z,
@@ -686,8 +729,7 @@
         side_z,
         flops=60 * sites,
     )
-    copies = jnp.broadcast_to(shares[None, :1], (devices, 1, 128))
-    spread = lax.all_to_all(copies, ("gx", "gy"), 0, 0)
+    spread = lax.all_to_all(shares.reshape(devices, 1, 128), ("gx", "gy"), 0, 0)
     (adjoint_new,) = run(
         adjoint_kernel,
         [adjoint.shape],

time: 46.1 us -> 45.8 us (level)
  local copies, waits for them, and re-layouts: 0.73 us -> 0 us
  Pallas kernels: 9.76 us -> 10.3 us
    broadcast_in_dim x2 -> x0, local copies, waits for them, and re-layouts: 0.73 us -> none  [shards(): copies = jnp.broadcast_to(shares[None, :1], (devices, 1, 128))]
    pallas_call x7, Pallas kernels: 9.76 us -> 10.3 us  [run(): pl.pallas_call(kernel, out_shape=sizes, in_specs=[away if i < far else ne...]
where the time goes in v5:
time: 45.8 us; the launch traced here: 45.5 us
  starting transfers between devices  23.4 us (51%)
  waiting for transfers between devices  11.1 us (24%)
  Pallas kernels  10.3 us (22%)
  between operations  0.7 us (2%)
    ppermute x4, starting transfers between devices, swap(): return (lax.ppermute(first, axis, far), lax.ppermute(second, axis, near))  14 us
    pallas_call x7, Pallas kernels, run(): pl.pallas_call(kernel, out_shape=sizes, in_specs=[away if i < far else ne...  10.3 us
    all_to_all x1, waiting for transfers between devices, shards(): spread = lax.all_to_all(shares.reshape(devices, 1, 128), ('gx', 'gy'), 0, 0)  9.69 us
    all_to_all x1, starting transfers between devices, shards(): spread = lax.all_to_all(shares.reshape(devices, 1, 128), ('gx', 'gy'), 0, 0)  9.37 us
    ppermute x4, waiting for transfers between devices, swap(): return (lax.ppermute(first, axis, far), lax.ppermute(second, axis, near))  1.4 us
  transfers between devices with their start and end apart: 5, of which 2 were waited for; matrix products, arithmetic and copies ran while one was open for 0% of the time, Pallas kernels for 14%

profile of v5, /device:TPU:1, one launch (start us, length us, event | category | flops | bytes accessed | tf_op | source)
XLA Modules:
  0.0 45.5 jit_solution(14952044180873092745)
XLA Ops:
  0.6 1.4 %shard_map.60.own_z = f32[16,512]{1,0:T(8,128)S(1)} custom-call(f32[19,32,512]{2,1,0:T(8,128)} %forward_far.1, f32[19,32,512]{2,1,0:T(8,128)} %adjoint_far.1, s32[32,512]{1,0:T(8,128)} %node_far.1), custom_call_target="tpu_custom_call" | custom-call | flops 655360 | bytes 2588672 | tf_op jit(solution)/shard_map/pallas_call | solution.py:641
  2.0 3.1 %collective-permute-start.1 = (f32[16,512]{1,0:T(8,128)S(1)}, f32[16,512]{1,0:T(8,128)S(1)}, u32[]{:S(2)}, u32[]{:S(2)}) collective-permute-start(f32[16,512]{1,0:T(8,128)S(1)} %shard_map.60.own_z), channel_id=1, source_target_pairs={{8,16},{24,32},{40,48},{56,64},{72,80},{88,96},{104,112},{120,128}... | collective-permute-start | bytes 98312 | tf_op jit(solution)/shard_map/ppermute | solution.py:658
  5.1 1.4 %shard_map.59.own_s = f32[16,512]{1,0:T(8,128)S(1)} custom-call(f32[19,32,512]{2,1,0:T(8,128)} %forward_far.1, f32[19,32,512]{2,1,0:T(8,128)} %adjoint_far.1, s32[32,512]{1,0:T(8,128)} %node_far.1), custom_call_target="tpu_custom_call" | custom-call | flops 655360 | bytes 2588672 | tf_op jit(solution)/shard_map/pallas_call | solution.py:641
  6.5 6.3 %collective-permute-start = (f32[16,512]{1,0:T(8,128)S(1)}, f32[16,512]{1,0:T(8,128)S(1)}, u32[]{:S(2)}, u32[]{:S(2)}) collective-permute-start(f32[16,512]{1,0:T(8,128)S(1)} %shard_map.59.own_s), channel_id=1, source_target_pairs={{0,8},{8,0},{16,24},{24,16},{32,40},{40,32},{48,56},{56,48},{64,72... | collective-permute-start | bytes 98312 | tf_op jit(solution)/shard_map/ppermute | solution.py:658
  12.8 2.0 %shard_map.61 = (f32[32,512]{1,0:T(8,128)S(1)}, f32[32,512]{1,0:T(8,128)S(1)}) custom-call(f32[19,32,512]{2,1,0:T(8,128)} %forward_far.1, f32[19,32,512]{2,1,0:T(8,128)} %adjoint_far.1, s32[32,512]{1,0:T(8,128)} %node_far.1), custom_call_target="tpu_custom_call" | custom-call | flops 2457600 | bytes 2686976 | tf_op jit(solution)/shard_map/pallas_call | solution.py:641
  14.9 0.0 collective-permute-done.1.got_z
  14.9 0.0 collective-permute-done.got_s
  14.9 0.2 shard_map.62
  15.1 0.7 %collective-permute-start.3 = (f32[40,256]{1,0:T(8,128)S(1)}, f32[40,256]{1,0:T(8,128)S(1)}, u32[]{:S(2)}, u32[]{:S(2)}) collective-permute-start(f32[40,256]{1,0:T(8,128)S(1)} %get-tuple-element.12.own_z), channel_id=1, source_target_pairs={{1,2},{3,4},{5,6},{2,1},{4,3},{6,5},{9,10},{11,12},{13,14},{10,9},... | collective-permute-start | bytes 122888 | tf_op jit(solution)/shard_map/ppermute | solution.py:658
  15.8 3.9 %collective-permute-start.2 = (f32[40,256]{1,0:T(8,128)S(1)}, f32[40,256]{1,0:T(8,128)S(1)}, u32[]{:S(2)}, u32[]{:S(2)}) collective-permute-start(f32[40,256]{1,0:T(8,128)S(1)} %get-tuple-element.11.own_s), channel_id=1, source_target_pairs={{0,1},{1,0},{2,3},{3,2},{4,5},{5,4},{6,7},{7,6},{8,9},{9,8},{10,11... | collective-permute-start | bytes 122888 | tf_op jit(solution)/shard_map/ppermute | solution.py:658
  19.7 0.0 collective-permute-done.3.side_z.got_z
  19.7 1.4 %collective-permute-done.2.side_s.got_s = f32[40,256]{1,0:T(8,128)S(1)} collective-permute-done((f32[40,256]{1,0:T(8,128)S(1)}, f32[40,256]{1,0:T(8,128)S(1)}, u32[]{:S(2)}, u32[]{:S(2)}) %collective-permute-start.2) | collective-permute-done | bytes 40992 | tf_op jit(solution)/shard_map/ppermute | solution.py:658
  21.1 1.4 %shard_map.64 = (f32[3,32,512]{2,1,0:T(8,128)S(1)}, f32[256,128]{1,0:T(8,128)}) custom-call(f32[40,512]{1,0:T(8,128)S(1)} %get-tuple-element.13.wide, f32[40,256]{1,0:T(8,128)S(1)} %get-tuple-element.11.own_s, f32[40,256]{1,0:T(8,128)S(1)} %get-tuple-element.12.own_z, f32[40,256]{1,0:T(8,128)S(1)} %collective-permute-done.2.side_s.got_s, ...), custom_call_target="tpu_custom_call" | custom-call | flops 983040 | bytes 573440 | tf_op jit(solution)/shard_map/pallas_call | solution.py:641
  22.5 9.4 %all-to-all-start = ((f32[256,1,128]{2,1,0:T(1,128)}), f32[256,1,128]{2,1,0:T(1,128)S(1)}, u32[]{:S(2)}, u32[]{:S(2)}) async-start(f32[256,1,128]{2,1,0:T(1,128)} %bitcast.1), calls=%async_computation | async-start | bytes 262144 | tf_op jit(solution)/shard_map/all_to_all | solution.py:732
  31.9 3.1 %shard_map.63 = f32[19,32,512]{2,1,0:T(8,128)} custom-call(f32[19,32,512]{2,1,0:T(8,128)} %forward_far.1, f32[19,32,512]{2,1,0:T(8,128)} %adjoint_far.1, f32[32,512]{1,0:T(8,128)} %design_far.1, s32[32,512]{1,0:T(8,128)} %node_far.1, f32[16,512]{1,0:T(8,128)S(1)} %collective-permute-done.got_s, f32[16,512]{1,0:T(8,128)S(1)} %collective-permute-done.1.got_z, ...), custom_call_target="tpu_custom_call" | custom-call | flops 6553600 | bytes 4014080 | tf_op jit(solution)/shard_map/pallas_call | solution.py:641
  35.0 9.7 %all-to-all-done = f32[256,1,128]{2,1,0:T(1,128)S(1)} async-done(((f32[256,1,128]{2,1,0:T(1,128)}), f32[256,1,128]{2,1,0:T(1,128)S(1)}, u32[]{:S(2)}, u32[]{:S(2)}) %all-to-all-start) | async-done | bytes 131104 | tf_op jit(solution)/shard_map/all_to_all | solution.py:732
  44.6 0.8 %shard_map.65 = f32[32,512]{1,0:T(8,128)} custom-call(f32[256,128]{1,0:T(8,128)S(1)} %bitcast.4, f32[3,32,512]{2,1,0:T(8,128)S(1)} %get-tuple-element.15.basis), custom_call_target="tpu_custom_call" | custom-call | flops 163840 | bytes 393216 | tf_op jit(solution)/shard_map/pallas_call | solution.py:641
Async XLA Ops:
  2.0 12.8 %collective-permute-start.1 = (f32[16,512]{1,0:T(8,128)S(1)}, f32[16,512]{1,0:T(8,128)S(1)}, u32[]{:S(2)}, u32[]{:S(2)}) collective-permute-start(f32[16,512]{1,0:T(8,128)S(1)} %shard_map.60.own_z), channel_id=1, source_target_pairs={{8,16},{24,32},{40,48},{56,64},{72,80},{88,96},{104,112},{120,128}... | collective-permute-start | bytes 98312 | tf_op jit(solution)/shard_map/ppermute | solution.py:658
  6.5 8.4 %collective-permute-start = (f32[16,512]{1,0:T(8,128)S(1)}, f32[16,512]{1,0:T(8,128)S(1)}, u32[]{:S(2)}, u32[]{:S(2)}) collective-permute-start(f32[16,512]{1,0:T(8,128)S(1)} %shard_map.59.own_s), channel_id=1, source_target_pairs={{0,8},{8,0},{16,24},{24,16},{32,40},{40,32},{48,56},{56,48},{64,72... | collective-permute-start | bytes 98312 | tf_op jit(solution)/shard_map/ppermute | solution.py:658
  15.1 4.6 %collective-permute-start.3 = (f32[40,256]{1,0:T(8,128)S(1)}, f32[40,256]{1,0:T(8,128)S(1)}, u32[]{:S(2)}, u32[]{:S(2)}) collective-permute-start(f32[40,256]{1,0:T(8,128)S(1)} %get-tuple-element.12.own_z), channel_id=1, source_target_pairs={{1,2},{3,4},{5,6},{2,1},{4,3},{6,5},{9,10},{11,12},{13,14},{10,9},... | collective-permute-start | bytes 122888 | tf_op jit(solution)/shard_map/ppermute | solution.py:658
  15.8 5.3 %collective-permute-start.2 = (f32[40,256]{1,0:T(8,128)S(1)}, f32[40,256]{1,0:T(8,128)S(1)}, u32[]{:S(2)}, u32[]{:S(2)}) collective-permute-start(f32[40,256]{1,0:T(8,128)S(1)} %get-tuple-element.11.own_s), channel_id=1, source_target_pairs={{0,1},{1,0},{2,3},{3,2},{4,5},{5,4},{6,7},{7,6},{8,9},{9,8},{10,11... | collective-permute-start | bytes 122888 | tf_op jit(solution)/shard_map/ppermute | solution.py:658
  22.5 22.1 %all-to-all-start = ((f32[256,1,128]{2,1,0:T(1,128)}), f32[256,1,128]{2,1,0:T(1,128)S(1)}, u32[]{:S(2)}, u32[]{:S(2)}) async-start(f32[256,1,128]{2,1,0:T(1,128)} %bitcast.1), calls=%async_computation | async-start | bytes 262144 | tf_op jit(solution)/shard_map/all_to_all | solution.py:732

commit v6 on v5

--- a/solution.py
+++ b/solution.py
@@ -193,23 +193,25 @@
     layers, columns = node_type.shape
     odd = lax.axis_index("gx") & 1
     up = 1 - odd if near else odd
-    rows = pl.ds(pl.multiple_of(up * (layers - ROWS), ROWS), ROWS)
-    cuts = (1, 10, 19)
-    copies = [pltpu.make_async_copy(node_type.at[rows, :], kinds, sems.at[0])]
+    half = ROWS // 2
+    rows = pl.ds(pl.multiple_of(up * (layers - half), half), half)
+    held = pl.ds(pl.multiple_of(up * half, half), half)
+    cuts = (1, 7, 13, 19)
+    copies = [pltpu.make_async_copy(node_type.at[rows, :], kinds.at[held, :], sems.at[0])]
     for source, target in ((forward, moving), (adjoint, carried)):
         for low, high in zip(cuts, cuts[1:]):
             members = pl.ds(low, high - low)
             copies.append(
                 pltpu.make_async_copy(
-                    source.at[members, rows, :], target.at[members], sems.at[len(copies)]
+                    source.at[members, rows, :], target.at[members, held, :], sems.at[len(copies)]
                 )
             )
     for copy in copies:
         copy.start()
-    for copy in copies[:3]:
+    for copy in copies[:4]:
         copy.wait()
     gains = gains_of(lambda member: moving[member], kinds[...])
-    for copy in copies[3:]:
+    for copy in copies[4:]:
         copy.wait()
     row = iota((ROWS, columns), 0)
 
@@ -681,7 +683,7 @@
                 end,
                 end,
                 pltpu.VMEM((ROWS, columns), jnp.int32),
-                pltpu.SemaphoreType.DMA((5,)),
+                pltpu.SemaphoreType.DMA((7,)),
             ],
             flops=40 * sites,
         )

time: 45.8 us -> 45.5 us (level)
  no operation moved by 1% of the time
where the time goes in v6:
time: 45.5 us; the launch traced here: 45.2 us
  starting transfers between devices  23.5 us (52%)
  waiting for transfers between devices  11.1 us (24%)
  Pallas kernels  9.9 us (22%)
  between operations  0.7 us (2%)
    ppermute x4, starting transfers between devices, swap(): return (lax.ppermute(first, axis, far), lax.ppermute(second, axis, near))  14 us
    pallas_call x7, Pallas kernels, run(): pl.pallas_call(kernel, out_shape=sizes, in_specs=[away if i < far else ne...  9.9 us
    all_to_all x1, waiting for transfers between devices, shards(): spread = lax.all_to_all(shares.reshape(devices, 1, 128), ('gx', 'gy'), 0, 0)  9.69 us
    all_to_all x1, starting transfers between devices, shards(): spread = lax.all_to_all(shares.reshape(devices, 1, 128), ('gx', 'gy'), 0, 0)  9.46 us
    ppermute x4, waiting for transfers between devices, swap(): return (lax.ppermute(first, axis, far), lax.ppermute(second, axis, near))  1.4 us
  transfers between devices with their start and end apart: 5, of which 2 were waited for; matrix products, arithmetic and copies ran while one was open for 0% of the time, Pallas kernels for 14%

profile of v6, /device:TPU:1, one launch (start us, length us, event | category | flops | bytes accessed | tf_op | source)
XLA Modules:
  0.0 45.2 jit_solution(14092755028476602110)
XLA Ops:
  0.6 1.2 %shard_map.60.own_z = f32[16,512]{1,0:T(8,128)S(1)} custom-call(f32[19,32,512]{2,1,0:T(8,128)} %forward_far.1, f32[19,32,512]{2,1,0:T(8,128)} %adjoint_far.1, s32[32,512]{1,0:T(8,128)} %node_far.1), custom_call_target="tpu_custom_call" | custom-call | flops 655360 | bytes 2588672 | tf_op jit(solution)/shard_map/pallas_call | solution.py:643
  1.8 3.1 %collective-permute-start.1 = (f32[16,512]{1,0:T(8,128)S(1)}, f32[16,512]{1,0:T(8,128)S(1)}, u32[]{:S(2)}, u32[]{:S(2)}) collective-permute-start(f32[16,512]{1,0:T(8,128)S(1)} %shard_map.60.own_z), channel_id=1, source_target_pairs={{8,16},{24,32},{40,48},{56,64},{72,80},{88,96},{104,112},{120,128}... | collective-permute-start | bytes 98312 | tf_op jit(solution)/shard_map/ppermute | solution.py:660
  4.9 1.2 %shard_map.59.own_s = f32[16,512]{1,0:T(8,128)S(1)} custom-call(f32[19,32,512]{2,1,0:T(8,128)} %forward_far.1, f32[19,32,512]{2,1,0:T(8,128)} %adjoint_far.1, s32[32,512]{1,0:T(8,128)} %node_far.1), custom_call_target="tpu_custom_call" | custom-call | flops 655360 | bytes 2588672 | tf_op jit(solution)/shard_map/pallas_call | solution.py:643
  6.1 6.3 %collective-permute-start = (f32[16,512]{1,0:T(8,128)S(1)}, f32[16,512]{1,0:T(8,128)S(1)}, u32[]{:S(2)}, u32[]{:S(2)}) collective-permute-start(f32[16,512]{1,0:T(8,128)S(1)} %shard_map.59.own_s), channel_id=1, source_target_pairs={{0,8},{8,0},{16,24},{24,16},{32,40},{40,32},{48,56},{56,48},{64,72... | collective-permute-start | bytes 98312 | tf_op jit(solution)/shard_map/ppermute | solution.py:660
  12.4 2.0 %shard_map.61 = (f32[32,512]{1,0:T(8,128)S(1)}, f32[32,512]{1,0:T(8,128)S(1)}) custom-call(f32[19,32,512]{2,1,0:T(8,128)} %forward_far.1, f32[19,32,512]{2,1,0:T(8,128)} %adjoint_far.1, s32[32,512]{1,0:T(8,128)} %node_far.1), custom_call_target="tpu_custom_call" | custom-call | flops 2457600 | bytes 2686976 | tf_op jit(solution)/shard_map/pallas_call | solution.py:643
  14.5 0.0 collective-permute-done.1.got_z
  14.5 0.0 collective-permute-done.got_s
  14.5 0.2 shard_map.62
  14.8 0.7 %collective-permute-start.3 = (f32[40,256]{1,0:T(8,128)S(1)}, f32[40,256]{1,0:T(8,128)S(1)}, u32[]{:S(2)}, u32[]{:S(2)}) collective-permute-start(f32[40,256]{1,0:T(8,128)S(1)} %get-tuple-element.12.own_z), channel_id=1, source_target_pairs={{1,2},{3,4},{5,6},{2,1},{4,3},{6,5},{9,10},{11,12},{13,14},{10,9},... | collective-permute-start | bytes 122888 | tf_op jit(solution)/shard_map/ppermute | solution.py:660
  15.4 3.9 %collective-permute-start.2 = (f32[40,256]{1,0:T(8,128)S(1)}, f32[40,256]{1,0:T(8,128)S(1)}, u32[]{:S(2)}, u32[]{:S(2)}) collective-permute-start(f32[40,256]{1,0:T(8,128)S(1)} %get-tuple-element.11.own_s), channel_id=1, source_target_pairs={{0,1},{1,0},{2,3},{3,2},{4,5},{5,4},{6,7},{7,6},{8,9},{9,8},{10,11... | collective-permute-start | bytes 122888 | tf_op jit(solution)/shard_map/ppermute | solution.py:660
  19.4 0.0 collective-permute-done.3.side_z.got_z
  19.4 1.4 %collective-permute-done.2.side_s.got_s = f32[40,256]{1,0:T(8,128)S(1)} collective-permute-done((f32[40,256]{1,0:T(8,128)S(1)}, f32[40,256]{1,0:T(8,128)S(1)}, u32[]{:S(2)}, u32[]{:S(2)}) %collective-permute-start.2) | collective-permute-done | bytes 40992 | tf_op jit(solution)/shard_map/ppermute | solution.py:660
  20.7 1.4 %shard_map.64 = (f32[3,32,512]{2,1,0:T(8,128)S(1)}, f32[256,128]{1,0:T(8,128)}) custom-call(f32[40,512]{1,0:T(8,128)S(1)} %get-tuple-element.13.wide, f32[40,256]{1,0:T(8,128)S(1)} %get-tuple-element.11.own_s, f32[40,256]{1,0:T(8,128)S(1)} %get-tuple-element.12.own_z, f32[40,256]{1,0:T(8,128)S(1)} %collective-permute-done.2.side_s.got_s, ...), custom_call_target="tpu_custom_call" | custom-call | flops 983040 | bytes 573440 | tf_op jit(solution)/shard_map/pallas_call | solution.py:643
  22.1 9.5 %all-to-all-start = ((f32[256,1,128]{2,1,0:T(1,128)}), f32[256,1,128]{2,1,0:T(1,128)S(1)}, u32[]{:S(2)}, u32[]{:S(2)}) async-start(f32[256,1,128]{2,1,0:T(1,128)} %bitcast.1), calls=%async_computation | async-start | bytes 262144 | tf_op jit(solution)/shard_map/all_to_all | solution.py:734
  31.6 3.1 %shard_map.63 = f32[19,32,512]{2,1,0:T(8,128)} custom-call(f32[19,32,512]{2,1,0:T(8,128)} %forward_far.1, f32[19,32,512]{2,1,0:T(8,128)} %adjoint_far.1, f32[32,512]{1,0:T(8,128)} %design_far.1, s32[32,512]{1,0:T(8,128)} %node_far.1, f32[16,512]{1,0:T(8,128)S(1)} %collective-permute-done.got_s, f32[16,512]{1,0:T(8,128)S(1)} %collective-permute-done.1.got_z, ...), custom_call_target="tpu_custom_call" | custom-call | flops 6553600 | bytes 4014080 | tf_op jit(solution)/shard_map/pallas_call | solution.py:643
  34.7 9.7 %all-to-all-done = f32[256,1,128]{2,1,0:T(1,128)S(1)} async-done(((f32[256,1,128]{2,1,0:T(1,128)}), f32[256,1,128]{2,1,0:T(1,128)S(1)}, u32[]{:S(2)}, u32[]{:S(2)}) %all-to-all-start) | async-done | bytes 131104 | tf_op jit(solution)/shard_map/all_to_all | solution.py:734
  44.3 0.8 %shard_map.65 = f32[32,512]{1,0:T(8,128)} custom-call(f32[256,128]{1,0:T(8,128)S(1)} %bitcast.4, f32[3,32,512]{2,1,0:T(8,128)S(1)} %get-tuple-element.15.basis), custom_call_target="tpu_custom_call" | custom-call | flops 163840 | bytes 393216 | tf_op jit(solution)/shard_map/pallas_call | solution.py:643
Async XLA Ops:
  1.8 12.7 %collective-permute-start.1 = (f32[16,512]{1,0:T(8,128)S(1)}, f32[16,512]{1,0:T(8,128)S(1)}, u32[]{:S(2)}, u32[]{:S(2)}) collective-permute-start(f32[16,512]{1,0:T(8,128)S(1)} %shard_map.60.own_z), channel_id=1, source_target_pairs={{8,16},{24,32},{40,48},{56,64},{72,80},{88,96},{104,112},{120,128}... | collective-permute-start | bytes 98312 | tf_op jit(solution)/shard_map/ppermute | solution.py:660
  6.1 8.4 %collective-permute-start = (f32[16,512]{1,0:T(8,128)S(1)}, f32[16,512]{1,0:T(8,128)S(1)}, u32[]{:S(2)}, u32[]{:S(2)}) collective-permute-start(f32[16,512]{1,0:T(8,128)S(1)} %shard_map.59.own_s), channel_id=1, source_target_pairs={{0,8},{8,0},{16,24},{24,16},{32,40},{40,32},{48,56},{56,48},{64,72... | collective-permute-start | bytes 98312 | tf_op jit(solution)/shard_map/ppermute | solution.py:660
  14.8 4.6 %collective-permute-start.3 = (f32[40,256]{1,0:T(8,128)S(1)}, f32[40,256]{1,0:T(8,128)S(1)}, u32[]{:S(2)}, u32[]{:S(2)}) collective-permute-start(f32[40,256]{1,0:T(8,128)S(1)} %get-tuple-element.12.own_z), channel_id=1, source_target_pairs={{1,2},{3,4},{5,6},{2,1},{4,3},{6,5},{9,10},{11,12},{13,14},{10,9},... | collective-permute-start | bytes 122888 | tf_op jit(solution)/shard_map/ppermute | solution.py:660
  15.4 5.3 %collective-permute-start.2 = (f32[40,256]{1,0:T(8,128)S(1)}, f32[40,256]{1,0:T(8,128)S(1)}, u32[]{:S(2)}, u32[]{:S(2)}) collective-permute-start(f32[40,256]{1,0:T(8,128)S(1)} %get-tuple-element.11.own_s), channel_id=1, source_target_pairs={{0,1},{1,0},{2,3},{3,2},{4,5},{5,4},{6,7},{7,6},{8,9},{9,8},{10,11... | collective-permute-start | bytes 122888 | tf_op jit(solution)/shard_map/ppermute | solution.py:660
  22.1 22.2 %all-to-all-start = ((f32[256,1,128]{2,1,0:T(1,128)}), f32[256,1,128]{2,1,0:T(1,128)S(1)}, u32[]{:S(2)}, u32[]{:S(2)}) async-start(f32[256,1,128]{2,1,0:T(1,128)} %bitcast.1), calls=%async_computation | async-start | bytes 262144 | tf_op jit(solution)/shard_map/all_to_all | solution.py:734

commit v7 on v6

--- a/solution.py
+++ b/solution.py
@@ -30,6 +30,7 @@
 READS = 128
 EDGE = 208
 SPARE = 80
+CENTRES = (0.0, 1.0, 2.0)
 
 
 def iota(shape, axis):
@@ -433,22 +434,33 @@
     inside = (column < columns) | on_right | on_left
     first = laplace(field, depth, inside)
     second = laplace(first, depth, inside)
-    ahead = roll(second, -1, 0) + roll(second, -NZ, 1)
-    ahead = ahead + jnp.where(depth < NZ - 1, roll(second, -1, 1), 0.0)
-    third = second - ahead * (1.0 / 3.0)
+    third = laplace(second, depth, inside)
     cores = [v[: basis.shape[1], :columns] for v in (field, first, second, third)]
     for power in range(ITERS):
         basis[power] = cores[power]
     row = jnp.zeros((1, 128), jnp.float32)
     lane = iota((1, 128), 1)
-    for power in range(2 * ITERS):
-        value = sum_all(cores[power // 2] * cores[(power + 1) // 2])
-        row = jnp.where(lane == power, value, row)
+    for index, centre in enumerate(CENTRES):
+        vectors = about(cores, centre)
+        for power in range(2 * ITERS):
+            value = sum_all(vectors[power // 2] * vectors[(power + 1) // 2])
+            row = jnp.where(lane == index * 2 * ITERS + power, value, row)
     shares[...] = jnp.broadcast_to(row, shares.shape)
 
 
-def times_h(poly):
-    out = list(poly) + [0.0]
+def about(vectors, centre):
+    if isinstance(centre, float) and centre == 0.0:
+        return list(vectors)
+    result = [vectors[0]]
+    level = list(vectors)
+    while len(level) > 1:
+        level = [level[k + 1] - centre * level[k] for k in range(len(level) - 1)]
+        result.append(level[0])
+    return result
+
+
+def times_h(poly, centre):
+    out = [entry * (1.0 + 6.0 * radius_sq * centre) for entry in poly] + [0.0]
     for power, entry in enumerate(poly):
         out[power + 1] = out[power + 1] + (6.0 * radius_sq) * entry
     return out
@@ -466,14 +478,14 @@
     return poly[power] if power < len(poly) else 0.0
 
 
-def combination(moments):
+def combination(moments, centre):
     upper = 1.0 + 12.0 * radius_sq
     growth = (upper - 1.0) ** 2 / (4.0 * upper) * 1.001
     one = jnp.ones_like(moments[0])
     solved, residual, direction = [], [one], [one]
     norm_now = moments[0]
     for iteration in range(ITERS):
-        image = times_h(direction)
+        image = times_h(direction, centre)
         step = norm_now / dot_poly(direction, image, moments)
         step = jnp.clip(step, 1.0 / upper, 1.0)
         solved = [entry_of(solved, k) + step * direction[k] for k in range(len(direction))]
@@ -494,13 +506,23 @@
     total = jnp.sum(total, axis=0, keepdims=True)
     lane = iota(total.shape, 1)
     moments = [
-        jnp.sum(jnp.where(lane == power, total, 0.0), axis=1, keepdims=True)
-        for power in range(2 * ITERS)
+        jnp.sum(jnp.where(lane == place, total, 0.0), axis=1, keepdims=True)
+        for place in range(2 * ITERS * len(CENTRES))
     ]
-    weights = combination(moments)
-    result = basis[0] * weights[0]
+    chosen = moments[: 2 * ITERS]
+    centre = jnp.zeros_like(moments[0]) + CENTRES[0]
+    for index in range(1, len(CENTRES)):
+        border = 0.5 * (CENTRES[index - 1] + CENTRES[index])
+        beyond = moments[1] > border * moments[0]
+        centre = jnp.where(beyond, CENTRES[index], centre)
+        for power in range(2 * ITERS):
+            other = moments[index * 2 * ITERS + power]
+            chosen[power] = jnp.where(beyond, other, chosen[power])
+    weights = combination(chosen, centre)
+    vectors = about([basis[power] for power in range(ITERS)], centre)
+    result = vectors[0] * weights[0]
     for power in range(1, ITERS):
-        result = result + basis[power] * weights[power]
+        result = result + vectors[power] * weights[power]
     filtered[...] = result
 
 

time: 45.5 us -> 45.6 us (level)
  no operation moved by 1% of the time
where the time goes in v7:
time: 45.6 us; the launch traced here: 45.2 us
  starting transfers between devices  23.5 us (52%)
  waiting for transfers between devices  11.1 us (24%)
  Pallas kernels  9.97 us (22%)
  between operations  0.7 us (2%)
    ppermute x4, starting transfers between devices, swap(): return (lax.ppermute(first, axis, far), lax.ppermute(second, axis, near))  14 us
    pallas_call x7, Pallas kernels, run(): pl.pallas_call(kernel, out_shape=sizes, in_specs=[away if i < far else ne...  9.97 us
    all_to_all x1, waiting for transfers between devices, shards(): spread = lax.all_to_all(shares.reshape(devices, 1, 128), ('gx', 'gy'), 0, 0)  9.69 us
    all_to_all x1, starting transfers between devices, shards(): spread = lax.all_to_all(shares.reshape(devices, 1, 128), ('gx', 'gy'), 0, 0)  9.46 us
    ppermute x4, waiting for transfers between devices, swap(): return (lax.ppermute(first, axis, far), lax.ppermute(second, axis, near))  1.4 us
  transfers between devices with their start and end apart: 5, of which 2 were waited for; matrix products, arithmetic and copies ran while one was open for 0% of the time, Pallas kernels for 14%

profile of v7, /device:TPU:1, one launch (start us, length us, event | category | flops | bytes accessed | tf_op | source)
XLA Modules:
  0.0 45.2 jit_solution(13937024044173623148)
XLA Ops:
  0.6 1.2 %shard_map.60.own_z = f32[16,512]{1,0:T(8,128)S(1)} custom-call(f32[19,32,512]{2,1,0:T(8,128)} %forward_far.1, f32[19,32,512]{2,1,0:T(8,128)} %adjoint_far.1, s32[32,512]{1,0:T(8,128)} %node_far.1), custom_call_target="tpu_custom_call" | custom-call | flops 655360 | bytes 2588672 | tf_op jit(solution)/shard_map/pallas_call | solution.py:665
  1.8 3.1 %collective-permute-start.1 = (f32[16,512]{1,0:T(8,128)S(1)}, f32[16,512]{1,0:T(8,128)S(1)}, u32[]{:S(2)}, u32[]{:S(2)}) collective-permute-start(f32[16,512]{1,0:T(8,128)S(1)} %shard_map.60.own_z), channel_id=1, source_target_pairs={{8,16},{24,32},{40,48},{56,64},{72,80},{88,96},{104,112},{120,128}... | collective-permute-start | bytes 98312 | tf_op jit(solution)/shard_map/ppermute | solution.py:682
  4.9 1.2 %shard_map.59.own_s = f32[16,512]{1,0:T(8,128)S(1)} custom-call(f32[19,32,512]{2,1,0:T(8,128)} %forward_far.1, f32[19,32,512]{2,1,0:T(8,128)} %adjoint_far.1, s32[32,512]{1,0:T(8,128)} %node_far.1), custom_call_target="tpu_custom_call" | custom-call | flops 655360 | bytes 2588672 | tf_op jit(solution)/shard_map/pallas_call | solution.py:665
  6.1 6.3 %collective-permute-start = (f32[16,512]{1,0:T(8,128)S(1)}, f32[16,512]{1,0:T(8,128)S(1)}, u32[]{:S(2)}, u32[]{:S(2)}) collective-permute-start(f32[16,512]{1,0:T(8,128)S(1)} %shard_map.59.own_s), channel_id=1, source_target_pairs={{0,8},{8,0},{16,24},{24,16},{32,40},{40,32},{48,56},{56,48},{64,72... | collective-permute-start | bytes 98312 | tf_op jit(solution)/shard_map/ppermute | solution.py:682
  12.4 2.0 %shard_map.61 = (f32[32,512]{1,0:T(8,128)S(1)}, f32[32,512]{1,0:T(8,128)S(1)}) custom-call(f32[19,32,512]{2,1,0:T(8,128)} %forward_far.1, f32[19,32,512]{2,1,0:T(8,128)} %adjoint_far.1, s32[32,512]{1,0:T(8,128)} %node_far.1), custom_call_target="tpu_custom_call" | custom-call | flops 2457600 | bytes 2686976 | tf_op jit(solution)/shard_map/pallas_call | solution.py:665
  14.5 0.0 collective-permute-done.1.got_z
  14.5 0.0 collective-permute-done.got_s
  14.5 0.2 shard_map.62
  14.8 0.7 %collective-permute-start.3 = (f32[40,256]{1,0:T(8,128)S(1)}, f32[40,256]{1,0:T(8,128)S(1)}, u32[]{:S(2)}, u32[]{:S(2)}) collective-permute-start(f32[40,256]{1,0:T(8,128)S(1)} %get-tuple-element.12.own_z), channel_id=1, source_target_pairs={{1,2},{3,4},{5,6},{2,1},{4,3},{6,5},{9,10},{11,12},{13,14},{10,9},... | collective-permute-start | bytes 122888 | tf_op jit(solution)/shard_map/ppermute | solution.py:682
  15.4 3.9 %collective-permute-start.2 = (f32[40,256]{1,0:T(8,128)S(1)}, f32[40,256]{1,0:T(8,128)S(1)}, u32[]{:S(2)}, u32[]{:S(2)}) collective-permute-start(f32[40,256]{1,0:T(8,128)S(1)} %get-tuple-element.11.own_s), channel_id=1, source_target_pairs={{0,1},{1,0},{2,3},{3,2},{4,5},{5,4},{6,7},{7,6},{8,9},{9,8},{10,11... | collective-permute-start | bytes 122888 | tf_op jit(solution)/shard_map/ppermute | solution.py:682
  19.4 0.0 collective-permute-done.3.side_z.got_z
  19.4 1.4 %collective-permute-done.2.side_s.got_s = f32[40,256]{1,0:T(8,128)S(1)} collective-permute-done((f32[40,256]{1,0:T(8,128)S(1)}, f32[40,256]{1,0:T(8,128)S(1)}, u32[]{:S(2)}, u32[]{:S(2)}) %collective-permute-start.2) | collective-permute-done | bytes 40992 | tf_op jit(solution)/shard_map/ppermute | solution.py:682
  20.7 1.4 %shard_map.64 = (f32[3,32,512]{2,1,0:T(8,128)S(1)}, f32[256,128]{1,0:T(8,128)}) custom-call(f32[40,512]{1,0:T(8,128)S(1)} %get-tuple-element.13.wide, f32[40,256]{1,0:T(8,128)S(1)} %get-tuple-element.11.own_s, f32[40,256]{1,0:T(8,128)S(1)} %get-tuple-element.12.own_z, f32[40,256]{1,0:T(8,128)S(1)} %collective-permute-done.2.side_s.got_s, ...), custom_call_target="tpu_custom_call" | custom-call | flops 983040 | bytes 573440 | tf_op jit(solution)/shard_map/pallas_call | solution.py:665
  22.2 9.5 %all-to-all-start = ((f32[256,1,128]{2,1,0:T(1,128)}), f32[256,1,128]{2,1,0:T(1,128)S(1)}, u32[]{:S(2)}, u32[]{:S(2)}) async-start(f32[256,1,128]{2,1,0:T(1,128)} %bitcast.1), calls=%async_computation | async-start | bytes 262144 | tf_op jit(solution)/shard_map/all_to_all | solution.py:756
  31.6 3.1 %shard_map.63 = f32[19,32,512]{2,1,0:T(8,128)} custom-call(f32[19,32,512]{2,1,0:T(8,128)} %forward_far.1, f32[19,32,512]{2,1,0:T(8,128)} %adjoint_far.1, f32[32,512]{1,0:T(8,128)} %design_far.1, s32[32,512]{1,0:T(8,128)} %node_far.1, f32[16,512]{1,0:T(8,128)S(1)} %collective-permute-done.got_s, f32[16,512]{1,0:T(8,128)S(1)} %collective-permute-done.1.got_z, ...), custom_call_target="tpu_custom_call" | custom-call | flops 6553600 | bytes 4014080 | tf_op jit(solution)/shard_map/pallas_call | solution.py:665
  34.7 9.7 %all-to-all-done = f32[256,1,128]{2,1,0:T(1,128)S(1)} async-done(((f32[256,1,128]{2,1,0:T(1,128)}), f32[256,1,128]{2,1,0:T(1,128)S(1)}, u32[]{:S(2)}, u32[]{:S(2)}) %all-to-all-start) | async-done | bytes 131104 | tf_op jit(solution)/shard_map/all_to_all | solution.py:756
  44.4 0.8 %shard_map.65 = f32[32,512]{1,0:T(8,128)} custom-call(f32[256,128]{1,0:T(8,128)S(1)} %bitcast.4, f32[3,32,512]{2,1,0:T(8,128)S(1)} %get-tuple-element.15.basis), custom_call_target="tpu_custom_call" | custom-call | flops 163840 | bytes 393216 | tf_op jit(solution)/shard_map/pallas_call | solution.py:665
Async XLA Ops:
  1.8 12.7 %collective-permute-start.1 = (f32[16,512]{1,0:T(8,128)S(1)}, f32[16,512]{1,0:T(8,128)S(1)}, u32[]{:S(2)}, u32[]{:S(2)}) collective-permute-start(f32[16,512]{1,0:T(8,128)S(1)} %shard_map.60.own_z), channel_id=1, source_target_pairs={{8,16},{24,32},{40,48},{56,64},{72,80},{88,96},{104,112},{120,128}... | collective-permute-start | bytes 98312 | tf_op jit(solution)/shard_map/ppermute | solution.py:682
  6.1 8.4 %collective-permute-start = (f32[16,512]{1,0:T(8,128)S(1)}, f32[16,512]{1,0:T(8,128)S(1)}, u32[]{:S(2)}, u32[]{:S(2)}) collective-permute-start(f32[16,512]{1,0:T(8,128)S(1)} %shard_map.59.own_s), channel_id=1, source_target_pairs={{0,8},{8,0},{16,24},{24,16},{32,40},{40,32},{48,56},{56,48},{64,72... | collective-permute-start | bytes 98312 | tf_op jit(solution)/shard_map/ppermute | solution.py:682
  14.8 4.6 %collective-permute-start.3 = (f32[40,256]{1,0:T(8,128)S(1)}, f32[40,256]{1,0:T(8,128)S(1)}, u32[]{:S(2)}, u32[]{:S(2)}) collective-permute-start(f32[40,256]{1,0:T(8,128)S(1)} %get-tuple-element.12.own_z), channel_id=1, source_target_pairs={{1,2},{3,4},{5,6},{2,1},{4,3},{6,5},{9,10},{11,12},{13,14},{10,9},... | collective-permute-start | bytes 122888 | tf_op jit(solution)/shard_map/ppermute | solution.py:682
  15.4 5.3 %collective-permute-start.2 = (f32[40,256]{1,0:T(8,128)S(1)}, f32[40,256]{1,0:T(8,128)S(1)}, u32[]{:S(2)}, u32[]{:S(2)}) collective-permute-start(f32[40,256]{1,0:T(8,128)S(1)} %get-tuple-element.11.own_s), channel_id=1, source_target_pairs={{0,1},{1,0},{2,3},{3,2},{4,5},{5,4},{6,7},{7,6},{8,9},{9,8},{10,11... | collective-permute-start | bytes 122888 | tf_op jit(solution)/shard_map/ppermute | solution.py:682
  22.2 22.2 %all-to-all-start = ((f32[256,1,128]{2,1,0:T(1,128)}), f32[256,1,128]{2,1,0:T(1,128)S(1)}, u32[]{:S(2)}, u32[]{:S(2)}) async-start(f32[256,1,128]{2,1,0:T(1,128)} %bitcast.1), calls=%async_computation | async-start | bytes 262144 | tf_op jit(solution)/shard_map/all_to_all | solution.py:756

commit v8 on v7

--- a/solution.py
+++ b/solution.py
@@ -302,7 +302,7 @@
     return result
 
 
-def faces_kernel(partial, edges, own_s, own_z, got_s, got_z, wide, out_s, out_z):
+def faces_kernel(near, partial, edges, own_s, own_z, got_s, got_z, out, wide):
     layers, columns = partial.shape
     even = (lax.axis_index("gx") & 1) == 0
 
@@ -325,14 +325,17 @@
     far_first = completion(face_reads(up[1], -1), roll(above[0], -3, 0))
     far_last = completion(face_reads(roll(down[1], -3, 0), 1), below[0])
     last = ROWS - 1
-    wide[:ROWS, :] = partial[:ROWS, :] - jnp.where(row == 0, own_first, 0.0)
-    wide[ROWS : layers - ROWS, :] = partial[ROWS : layers - ROWS, :]
-    wide[layers - ROWS : layers, :] = partial[layers - ROWS :, :] + jnp.where(
-        row == last, own_last, 0.0
-    )
+    top = partial[:ROWS, :] - jnp.where(row == 0, own_first, 0.0)
+    bottom = partial[layers - ROWS :, :] + jnp.where(row == last, own_last, 0.0)
     halo = jnp.where(row < ROWS // 2, above[0], below[0])
     halo = halo - jnp.where(row == 0, far_first, 0.0) + jnp.where(row == last, far_last, 0.0)
-    wide[layers:, :] = halo
+    for start in range(0, columns, 128):
+        if near or start in (0, columns - 128):
+            lanes = slice(start, start + 128)
+            wide[:ROWS, lanes] = top[:, lanes]
+            wide[ROWS : layers - ROWS, lanes] = partial[ROWS : layers - ROWS, lanes]
+            wide[layers - ROWS : layers, lanes] = bottom[:, lanes]
+            wide[layers:, lanes] = halo[:, lanes]
 
     halo = unstow(jnp.where(row < ROWS // 2, above[1], below[1]))
     edge = jnp.concatenate([edges[...], halo], axis=0)
@@ -348,8 +351,7 @@
     even_y = (lax.axis_index("gy") & 1) == 0
     for part in range(2):
         lanes = slice(part * 128, part * 128 + 128)
-        out_s[:, lanes] = jnp.where(even_y, to_right[part], to_left[part])
-        out_z[:, lanes] = jnp.where(even_y, to_left[part], to_right[part])
+        out[:, lanes] = jnp.where(even_y == near, to_right[part], to_left[part])
 
 
 def hand_on_kernel(first, second, out):
@@ -375,13 +377,13 @@
     return low, jnp.where(lane >= 128 - NZ, roll(total, 64 - NZ, 1), 0.0)
 
 
-def laplace(field, depth, inside):
+def laplace(field, depth):
     rows, lanes = field.shape
     total = roll(field, 1, 0) + roll(field, -1, 0)
     total = total + (roll(field, NZ, 1) + roll(field, -NZ, 1))
     total = total + jnp.where(depth > 0, roll(field, 1, 1), 0.0)
     total = total + jnp.where(depth < NZ - 1, roll(field, -1, 1), 0.0)
-    return jnp.where(inside, field - total * (1.0 / 6.0), 0.0)
+    return field - total * (1.0 / 6.0)
 
 
 def tree_sum(parts):
@@ -427,14 +429,16 @@
     low, high = fold(signed_products(to_right, right, -1), signed_products(to_left, left, 1))
     halo = (right_halo + low) + (left_halo + high)
     field = jnp.concatenate([low_end, field[:, 128 : columns - 128], high_end, halo], axis=1)
-    column = iota(field.shape, 1)
-    depth = column & (NZ - 1)
-    on_right = (column < columns + 64) & (place < last_place)
-    on_left = (column >= columns + 64) & (place > 0)
-    inside = (column < columns) | on_right | on_left
-    first = laplace(field, depth, inside)
-    second = laplace(first, depth, inside)
-    third = laplace(second, depth, inside)
+    depth = iota(field.shape, 1) & (NZ - 1)
+    inside = ((lane < 64) & (place < last_place)) | ((lane >= 64) & (place > 0))
+
+    def within(value):
+        halo = jnp.where(inside, value[:, columns:], 0.0)
+        return jnp.concatenate([value[:, :columns], halo], axis=1)
+
+    first = within(laplace(field, depth))
+    second = within(laplace(first, depth))
+    third = laplace(second, depth)
     cores = [v[: basis.shape[1], :columns] for v in (field, first, second, third)]
     for power in range(ITERS):
         basis[power] = cores[power]
@@ -730,16 +734,17 @@
         ],
         flops=150 * sites,
     )
-    wide, out_s, out_z = run(
-        faces_kernel,
-        [(layers + ROWS, columns), side, side],
-        partial,
-        edges,
-        own_s,
-        own_z,
-        got_s,
-        got_z,
+    given = (partial, edges, own_s, own_z, got_s, got_z)
+    across = (layers + ROWS, columns)
+    (out_z,) = run(
+        functools.partial(faces_kernel, False),
+        [side],
+        *given,
+        scratch=[pltpu.VMEM(across, jnp.float32)],
         flops=10 * sites,
+    )
+    out_s, wide = run(
+        functools.partial(faces_kernel, True), [side, across], *given, flops=10 * sites
     )
     side_z, side_s = swap(out_z, out_s, "gy", False)
     side_z = lax.optimization_barrier(side_z)

time: 45.6 us -> 45.5 us (level)
    pallas_call x7 -> x8, Pallas kernels: 9.97 us -> 10.2 us  [run(): pl.pallas_call(kernel, out_shape=sizes, in_specs=[away if i < far else ne...]
where the time goes in v8:
time: 45.5 us; the launch traced here: 45.2 us
  starting transfers between devices  23.2 us (51%)
  waiting for transfers between devices  11.1 us (24%)
  Pallas kernels  10.2 us (22%)
  between operations  0.71 us (2%)
    ppermute x4, starting transfers between devices, swap(): return (lax.ppermute(first, axis, far), lax.ppermute(second, axis, near))  14 us
    pallas_call x8, Pallas kernels, run(): pl.pallas_call(kernel, out_shape=sizes, in_specs=[away if i < far else ne...  10.2 us
    all_to_all x1, waiting for transfers between devices, shards(): spread = lax.all_to_all(shares.reshape(devices, 1, 128), ('gx', 'gy'), 0, 0)  9.69 us
    all_to_all x1, starting transfers between devices, shards(): spread = lax.all_to_all(shares.reshape(devices, 1, 128), ('gx', 'gy'), 0, 0)  9.21 us
    ppermute x4, waiting for transfers between devices, swap(): return (lax.ppermute(first, axis, far), lax.ppermute(second, axis, near))  1.4 us
  transfers between devices with their start and end apart: 5, of which 2 were waited for; matrix products, arithmetic and copies ran while one was open for 0% of the time, Pallas kernels for 14%

profile of v8, /device:TPU:1, one launch (start us, length us, event | category | flops | bytes accessed | tf_op | source)
XLA Modules:
  0.0 45.2 jit_solution(1668692431956776045)
XLA Ops:
  0.6 1.2 %shard_map.60.own_z = f32[16,512]{1,0:T(8,128)S(1)} custom-call(f32[19,32,512]{2,1,0:T(8,128)} %forward_far.1, f32[19,32,512]{2,1,0:T(8,128)} %adjoint_far.1, s32[32,512]{1,0:T(8,128)} %node_far.1), custom_call_target="tpu_custom_call" | custom-call | flops 655360 | bytes 2588672 | tf_op jit(solution)/shard_map/pallas_call | solution.py:669
  1.8 3.1 %collective-permute-start.1 = (f32[16,512]{1,0:T(8,128)S(1)}, f32[16,512]{1,0:T(8,128)S(1)}, u32[]{:S(2)}, u32[]{:S(2)}) collective-permute-start(f32[16,512]{1,0:T(8,128)S(1)} %shard_map.60.own_z), channel_id=1, source_target_pairs={{8,16},{24,32},{40,48},{56,64},{72,80},{88,96},{104,112},{120,128}... | collective-permute-start | bytes 98312 | tf_op jit(solution)/shard_map/ppermute | solution.py:686
  4.9 1.2 %shard_map.59.own_s = f32[16,512]{1,0:T(8,128)S(1)} custom-call(f32[19,32,512]{2,1,0:T(8,128)} %forward_far.1, f32[19,32,512]{2,1,0:T(8,128)} %adjoint_far.1, s32[32,512]{1,0:T(8,128)} %node_far.1), custom_call_target="tpu_custom_call" | custom-call | flops 655360 | bytes 2588672 | tf_op jit(solution)/shard_map/pallas_call | solution.py:669
  6.1 6.3 %collective-permute-start = (f32[16,512]{1,0:T(8,128)S(1)}, f32[16,512]{1,0:T(8,128)S(1)}, u32[]{:S(2)}, u32[]{:S(2)}) collective-permute-start(f32[16,512]{1,0:T(8,128)S(1)} %shard_map.59.own_s), channel_id=1, source_target_pairs={{0,8},{8,0},{16,24},{24,16},{32,40},{40,32},{48,56},{56,48},{64,72... | collective-permute-start | bytes 98312 | tf_op jit(solution)/shard_map/ppermute | solution.py:686
  12.4 2.0 %shard_map.61 = (f32[32,512]{1,0:T(8,128)S(1)}, f32[32,512]{1,0:T(8,128)S(1)}) custom-call(f32[19,32,512]{2,1,0:T(8,128)} %forward_far.1, f32[19,32,512]{2,1,0:T(8,128)} %adjoint_far.1, s32[32,512]{1,0:T(8,128)} %node_far.1), custom_call_target="tpu_custom_call" | custom-call | flops 2457600 | bytes 2686976 | tf_op jit(solution)/shard_map/pallas_call | solution.py:669
  14.5 0.0 collective-permute-done.1.got_z
  14.5 0.0 collective-permute-done.got_s
  14.5 0.2 shard_map.63.own_z
  14.7 0.7 %collective-permute-start.3 = (f32[40,256]{1,0:T(8,128)S(1)}, f32[40,256]{1,0:T(8,128)S(1)}, u32[]{:S(2)}, u32[]{:S(2)}) collective-permute-start(f32[40,256]{1,0:T(8,128)S(1)} %shard_map.63.own_z), channel_id=1, source_target_pairs={{1,2},{3,4},{5,6},{2,1},{4,3},{6,5},{9,10},{11,12},{13,14},{10,9},... | collective-permute-start | bytes 122888 | tf_op jit(solution)/shard_map/ppermute | solution.py:686
  15.4 0.2 shard_map.62
  15.7 3.9 %collective-permute-start.2 = (f32[40,256]{1,0:T(8,128)S(1)}, f32[40,256]{1,0:T(8,128)S(1)}, u32[]{:S(2)}, u32[]{:S(2)}) collective-permute-start(f32[40,256]{1,0:T(8,128)S(1)} %get-tuple-element.10.own_s), channel_id=1, source_target_pairs={{0,1},{1,0},{2,3},{3,2},{4,5},{5,4},{6,7},{7,6},{8,9},{9,8},{10,11... | collective-permute-start | bytes 122888 | tf_op jit(solution)/shard_map/ppermute | solution.py:686
  19.6 0.0 collective-permute-done.3.side_z.got_z
  19.6 1.4 %collective-permute-done.2.side_s.got_s = f32[40,256]{1,0:T(8,128)S(1)} collective-permute-done((f32[40,256]{1,0:T(8,128)S(1)}, f32[40,256]{1,0:T(8,128)S(1)}, u32[]{:S(2)}, u32[]{:S(2)}) %collective-permute-start.2) | collective-permute-done | bytes 40992 | tf_op jit(solution)/shard_map/ppermute | solution.py:686
  21.0 1.4 %shard_map.65 = (f32[3,32,512]{2,1,0:T(8,128)S(1)}, f32[256,128]{1,0:T(8,128)}) custom-call(f32[40,512]{1,0:T(8,128)S(1)} %get-tuple-element.11.wide, f32[40,256]{1,0:T(8,128)S(1)} %get-tuple-element.10.own_s, f32[40,256]{1,0:T(8,128)S(1)} %shard_map.63.own_z, f32[40,256]{1,0:T(8,128)S(1)} %collective-permute-done.2.side_s.got_s, ...), custom_call_target="tpu_custom_call" | custom-call | flops 983040 | bytes 573440 | tf_op jit(solution)/shard_map/pallas_call | solution.py:669
  22.4 9.2 %all-to-all-start = ((f32[256,1,128]{2,1,0:T(1,128)}), f32[256,1,128]{2,1,0:T(1,128)S(1)}, u32[]{:S(2)}, u32[]{:S(2)}) async-start(f32[256,1,128]{2,1,0:T(1,128)} %bitcast.1), calls=%async_computation | async-start | bytes 262144 | tf_op jit(solution)/shard_map/all_to_all | solution.py:761
  31.6 3.1 %shard_map.64 = f32[19,32,512]{2,1,0:T(8,128)} custom-call(f32[19,32,512]{2,1,0:T(8,128)} %forward_far.1, f32[19,32,512]{2,1,0:T(8,128)} %adjoint_far.1, f32[32,512]{1,0:T(8,128)} %design_far.1, s32[32,512]{1,0:T(8,128)} %node_far.1, f32[16,512]{1,0:T(8,128)S(1)} %collective-permute-done.got_s, f32[16,512]{1,0:T(8,128)S(1)} %collective-permute-done.1.got_z, ...), custom_call_target="tpu_custom_call" | custom-call | flops 6553600 | bytes 4014080 | tf_op jit(solution)/shard_map/pallas_call | solution.py:669
  34.7 9.7 %all-to-all-done = f32[256,1,128]{2,1,0:T(1,128)S(1)} async-done(((f32[256,1,128]{2,1,0:T(1,128)}), f32[256,1,128]{2,1,0:T(1,128)S(1)}, u32[]{:S(2)}, u32[]{:S(2)}) %all-to-all-start) | async-done | bytes 131104 | tf_op jit(solution)/shard_map/all_to_all | solution.py:761
  44.4 0.8 %shard_map.66 = f32[32,512]{1,0:T(8,128)} custom-call(f32[256,128]{1,0:T(8,128)S(1)} %bitcast.4, f32[3,32,512]{2,1,0:T(8,128)S(1)} %get-tuple-element.13.basis), custom_call_target="tpu_custom_call" | custom-call | flops 163840 | bytes 393216 | tf_op jit(solution)/shard_map/pallas_call | solution.py:669
Async XLA Ops:
  1.8 12.7 %collective-permute-start.1 = (f32[16,512]{1,0:T(8,128)S(1)}, f32[16,512]{1,0:T(8,128)S(1)}, u32[]{:S(2)}, u32[]{:S(2)}) collective-permute-start(f32[16,512]{1,0:T(8,128)S(1)} %shard_map.60.own_z), channel_id=1, source_target_pairs={{8,16},{24,32},{40,48},{56,64},{72,80},{88,96},{104,112},{120,128}... | collective-permute-start | bytes 98312 | tf_op jit(solution)/shard_map/ppermute | solution.py:686
  6.1 8.4 %collective-permute-start = (f32[16,512]{1,0:T(8,128)S(1)}, f32[16,512]{1,0:T(8,128)S(1)}, u32[]{:S(2)}, u32[]{:S(2)}) collective-permute-start(f32[16,512]{1,0:T(8,128)S(1)} %shard_map.59.own_s), channel_id=1, source_target_pairs={{0,8},{8,0},{16,24},{24,16},{32,40},{40,32},{48,56},{56,48},{64,72... | collective-permute-start | bytes 98312 | tf_op jit(solution)/shard_map/ppermute | solution.py:686
  14.7 4.8 %collective-permute-start.3 = (f32[40,256]{1,0:T(8,128)S(1)}, f32[40,256]{1,0:T(8,128)S(1)}, u32[]{:S(2)}, u32[]{:S(2)}) collective-permute-start(f32[40,256]{1,0:T(8,128)S(1)} %shard_map.63.own_z), channel_id=1, source_target_pairs={{1,2},{3,4},{5,6},{2,1},{4,3},{6,5},{9,10},{11,12},{13,14},{10,9},... | collective-permute-start | bytes 122888 | tf_op jit(solution)/shard_map/ppermute | solution.py:686
  15.7 5.3 %collective-permute-start.2 = (f32[40,256]{1,0:T(8,128)S(1)}, f32[40,256]{1,0:T(8,128)S(1)}, u32[]{:S(2)}, u32[]{:S(2)}) collective-permute-start(f32[40,256]{1,0:T(8,128)S(1)} %get-tuple-element.10.own_s), channel_id=1, source_target_pairs={{0,1},{1,0},{2,3},{3,2},{4,5},{5,4},{6,7},{7,6},{8,9},{9,8},{10,11... | collective-permute-start | bytes 122888 | tf_op jit(solution)/shard_map/ppermute | solution.py:686
  22.4 22.0 %all-to-all-start = ((f32[256,1,128]{2,1,0:T(1,128)}), f32[256,1,128]{2,1,0:T(1,128)S(1)}, u32[]{:S(2)}, u32[]{:S(2)}) async-start(f32[256,1,128]{2,1,0:T(1,128)} %bitcast.1), calls=%async_computation | async-start | bytes 262144 | tf_op jit(solution)/shard_map/all_to_all | solution.py:761

commit v9 on v8

--- a/solution.py
+++ b/solution.py
@@ -264,17 +264,15 @@
                 copy.wait()
 
 
-def collide_kernel(forward, adjoint, node_type, partial, edges, moving, carried, kinds, sems):
+def collide_kernel(forward, adjoint, node_type, partial, edges):
     layers, columns = partial.shape
-    groups = fetch_tiles((forward, adjoint, node_type), (moving, carried, kinds), sems)
     for tile in range(layers // ROWS):
         rows = slice(tile * ROWS, tile * ROWS + ROWS)
-        take(groups, tile)
-        gains = gains_of(lambda member: moving[member, rows, :], kinds[rows, :])
+        gains = gains_of(lambda member: forward[member, rows, :], node_type[rows, :])
         partial[rows, :] = inner_sensitivity(
-            gains, lambda member, step: row_tile(carried, member, tile, step)
+            gains, lambda member, step: row_tile(adjoint, member, tile, step)
         )
-        edges[rows, :] = pack_edges(gains, lambda member: carried[member, rows, :])
+        edges[rows, :] = pack_edges(gains, lambda member: adjoint[member, rows, :])
 
 
 def face_reads(faces, sign):
@@ -725,13 +723,6 @@
         forward,
         adjoint,
         node_type,
-        far=3,
-        scratch=[
-            field,
-            field,
-            pltpu.VMEM(plane, jnp.int32),
-            pltpu.SemaphoreType.DMA((tiles, 3)),
-        ],
         flops=150 * sites,
     )
     given = (partial, edges, own_s, own_z, got_s, got_z)

time: 45.5 us -> 45.5 us (level)
  Pallas kernels: 10.2 us -> 8.6 us
  starting transfers between devices: 23.2 us -> 24.4 us
    pallas_call x8, Pallas kernels: 10.2 us -> 8.6 us  [run(): pl.pallas_call(kernel, out_shape=sizes, in_specs=[away if i < far else ne...]
    all_to_all x1, starting transfers between devices: 9.21 us -> 10.4 us  [shards(): spread = lax.all_to_all(shares.reshape(devices, 1, 128), ('gx', 'gy'), 0, 0)]
  transfers between devices with their start and end apart: 5 -> 5, of which waited for: 2 -> 3; matrix products, arithmetic and copies ran while one was open for 0% -> 0% of each run, Pallas kernels for 14% -> 11%
where the time goes in v9:
time: 45.5 us; the launch traced here: 45.2 us
  starting transfers between devices  24.4 us (54%)
  waiting for transfers between devices  11.4 us (25%)
  Pallas kernels  8.6 us (19%)
  between operations  0.72 us (2%)
    ppermute x4, starting transfers between devices, swap(): return (lax.ppermute(first, axis, far), lax.ppermute(second, axis, near))  14 us
    all_to_all x1, starting transfers between devices, shards(): spread = lax.all_to_all(shares.reshape(devices, 1, 128), ('gx', 'gy'), 0, 0)  10.4 us
    all_to_all x1, waiting for transfers between devices, shards(): spread = lax.all_to_all(shares.reshape(devices, 1, 128), ('gx', 'gy'), 0, 0)  9.66 us
    pallas_call x8, Pallas kernels, run(): pl.pallas_call(kernel, out_shape=sizes, in_specs=[away if i < far else ne...  8.6 us
    ppermute x4, waiting for transfers between devices, swap(): return (lax.ppermute(first, axis, far), lax.ppermute(second, axis, near))  1.77 us
  transfers between devices with their start and end apart: 5, of which 3 were waited for; matrix products, arithmetic and copies ran while one was open for 0% of the time, Pallas kernels for 11%

profile of v9, /device:TPU:1, one launch (start us, length us, event | category | flops | bytes accessed | tf_op | source)
XLA Modules:
  0.0 45.2 jit_solution(18037887455471921158)
XLA Ops:
  0.6 1.2 %shard_map.60.own_z = f32[16,512]{1,0:T(8,128)S(1)} custom-call(f32[19,32,512]{2,1,0:T(8,128)} %forward_far.1, f32[19,32,512]{2,1,0:T(8,128)} %adjoint_far.1, s32[32,512]{1,0:T(8,128)} %node_far.1), custom_call_target="tpu_custom_call" | custom-call | flops 655360 | bytes 2588672 | tf_op jit(solution)/shard_map/pallas_call | solution.py:667
  1.8 0.0 copy-start
  1.8 0.0 copy-start.1
  1.9 0.0 copy-start.2
  1.9 3.1 %collective-permute-start.1 = (f32[16,512]{1,0:T(8,128)S(1)}, f32[16,512]{1,0:T(8,128)S(1)}, u32[]{:S(2)}, u32[]{:S(2)}) collective-permute-start(f32[16,512]{1,0:T(8,128)S(1)} %shard_map.60.own_z), channel_id=1, source_target_pairs={{8,16},{24,32},{40,48},{56,64},{72,80},{88,96},{104,112},{120,128}... | collective-permute-start | bytes 98312 | tf_op jit(solution)/shard_map/ppermute | solution.py:684
  5.0 1.2 %shard_map.59.own_s = f32[16,512]{1,0:T(8,128)S(1)} custom-call(f32[19,32,512]{2,1,0:T(8,128)} %forward_far.1, f32[19,32,512]{2,1,0:T(8,128)} %adjoint_far.1, s32[32,512]{1,0:T(8,128)} %node_far.1), custom_call_target="tpu_custom_call" | custom-call | flops 655360 | bytes 2588672 | tf_op jit(solution)/shard_map/pallas_call | solution.py:667
  6.2 6.3 %collective-permute-start = (f32[16,512]{1,0:T(8,128)S(1)}, f32[16,512]{1,0:T(8,128)S(1)}, u32[]{:S(2)}, u32[]{:S(2)}) collective-permute-start(f32[16,512]{1,0:T(8,128)S(1)} %shard_map.59.own_s), channel_id=1, source_target_pairs={{0,8},{8,0},{16,24},{24,16},{32,40},{40,32},{48,56},{56,48},{64,72... | collective-permute-start | bytes 98312 | tf_op jit(solution)/shard_map/ppermute | solution.py:684
  12.5 0.0 copy-done
  12.5 0.0 copy-done.1
  12.5 0.0 copy-done.2
  12.5 0.5 %shard_map.61 = (f32[32,512]{1,0:T(8,128)S(1)}, f32[32,512]{1,0:T(8,128)S(1)}) custom-call(f32[19,32,512]{2,1,0:T(8,128)S(1)} %copy-done, f32[19,32,512]{2,1,0:T(8,128)S(1)} %copy-done.1, s32[32,512]{1,0:T(8,128)S(1)} %copy-done.2), custom_call_target="tpu_custom_call" | custom-call | flops 2457600 | bytes 2686976 | tf_op jit(solution)/shard_map/pallas_call | solution.py:667
  13.0 0.0 collective-permute-done.1.got_z
  13.0 0.4 collective-permute-done.got_s
  13.3 0.2 shard_map.63.own_z
  13.6 0.7 %collective-permute-start.3 = (f32[40,256]{1,0:T(8,128)S(1)}, f32[40,256]{1,0:T(8,128)S(1)}, u32[]{:S(2)}, u32[]{:S(2)}) collective-permute-start(f32[40,256]{1,0:T(8,128)S(1)} %shard_map.63.own_z), channel_id=1, source_target_pairs={{1,2},{3,4},{5,6},{2,1},{4,3},{6,5},{9,10},{11,12},{13,14},{10,9},... | collective-permute-start | bytes 122888 | tf_op jit(solution)/shard_map/ppermute | solution.py:684
  14.2 0.2 shard_map.62
  14.5 3.9 %collective-permute-start.2 = (f32[40,256]{1,0:T(8,128)S(1)}, f32[40,256]{1,0:T(8,128)S(1)}, u32[]{:S(2)}, u32[]{:S(2)}) collective-permute-start(f32[40,256]{1,0:T(8,128)S(1)} %get-tuple-element.10.own_s), channel_id=1, source_target_pairs={{0,1},{1,0},{2,3},{3,2},{4,5},{5,4},{6,7},{7,6},{8,9},{9,8},{10,11... | collective-permute-start | bytes 122888 | tf_op jit(solution)/shard_map/ppermute | solution.py:684
  18.4 0.0 collective-permute-done.3.side_z.got_z
  18.4 1.4 %collective-permute-done.2.side_s.got_s = f32[40,256]{1,0:T(8,128)S(1)} collective-permute-done((f32[40,256]{1,0:T(8,128)S(1)}, f32[40,256]{1,0:T(8,128)S(1)}, u32[]{:S(2)}, u32[]{:S(2)}) %collective-permute-start.2) | collective-permute-done | bytes 40992 | tf_op jit(solution)/shard_map/ppermute | solution.py:684
  19.8 1.4 %shard_map.65 = (f32[3,32,512]{2,1,0:T(8,128)S(1)}, f32[256,128]{1,0:T(8,128)}) custom-call(f32[40,512]{1,0:T(8,128)S(1)} %get-tuple-element.11.wide, f32[40,256]{1,0:T(8,128)S(1)} %get-tuple-element.10.own_s, f32[40,256]{1,0:T(8,128)S(1)} %shard_map.63.own_z, f32[40,256]{1,0:T(8,128)S(1)} %collective-permute-done.2.side_s.got_s, ...), custom_call_target="tpu_custom_call" | custom-call | flops 983040 | bytes 573440 | tf_op jit(solution)/shard_map/pallas_call | solution.py:667
  21.2 10.4 %all-to-all-start = ((f32[256,1,128]{2,1,0:T(1,128)}), f32[256,1,128]{2,1,0:T(1,128)S(1)}, u32[]{:S(2)}, u32[]{:S(2)}) async-start(f32[256,1,128]{2,1,0:T(1,128)} %bitcast.1), calls=%async_computation | async-start | bytes 262144 | tf_op jit(solution)/shard_map/all_to_all | solution.py:752
  31.6 3.1 %shard_map.64 = f32[19,32,512]{2,1,0:T(8,128)} custom-call(f32[19,32,512]{2,1,0:T(8,128)} %forward_far.1, f32[19,32,512]{2,1,0:T(8,128)} %adjoint_far.1, f32[32,512]{1,0:T(8,128)} %design_far.1, s32[32,512]{1,0:T(8,128)} %node_far.1, f32[16,512]{1,0:T(8,128)S(1)} %collective-permute-done.got_s, f32[16,512]{1,0:T(8,128)S(1)} %collective-permute-done.1.got_z, ...), custom_call_target="tpu_custom_call" | custom-call | flops 6553600 | bytes 4014080 | tf_op jit(solution)/shard_map/pallas_call | solution.py:667
  34.7 9.7 %all-to-all-done = f32[256,1,128]{2,1,0:T(1,128)S(1)} async-done(((f32[256,1,128]{2,1,0:T(1,128)}), f32[256,1,128]{2,1,0:T(1,128)S(1)}, u32[]{:S(2)}, u32[]{:S(2)}) %all-to-all-start) | async-done | bytes 131104 | tf_op jit(solution)/shard_map/all_to_all | solution.py:752
  44.4 0.8 %shard_map.66 = f32[32,512]{1,0:T(8,128)} custom-call(f32[256,128]{1,0:T(8,128)S(1)} %bitcast.4, f32[3,32,512]{2,1,0:T(8,128)S(1)} %get-tuple-element.13.basis), custom_call_target="tpu_custom_call" | custom-call | flops 163840 | bytes 393216 | tf_op jit(solution)/shard_map/pallas_call | solution.py:667
Async XLA Ops:
  1.8 10.7 %copy-start = (f32[19,32,512]{2,1,0:T(8,128)S(1)}, f32[19,32,512]{2,1,0:T(8,128)}, u32[]{:S(2)}) copy-start(f32[19,32,512]{2,1,0:T(8,128)} %forward_far.1) | copy-start | bytes 3735556
  1.8 10.6 %copy-start.1 = (f32[19,32,512]{2,1,0:T(8,128)S(1)}, f32[19,32,512]{2,1,0:T(8,128)}, u32[]{:S(2)}) copy-start(f32[19,32,512]{2,1,0:T(8,128)} %adjoint_far.1) | copy-start | bytes 3735556
  1.9 10.6 %copy-start.2 = (s32[32,512]{1,0:T(8,128)S(1)}, s32[32,512]{1,0:T(8,128)}, u32[]{:S(2)}) copy-start(s32[32,512]{1,0:T(8,128)} %node_far.1) | copy-start | bytes 196612
  1.9 11.1 %collective-permute-start.1 = (f32[16,512]{1,0:T(8,128)S(1)}, f32[16,512]{1,0:T(8,128)S(1)}, u32[]{:S(2)}, u32[]{:S(2)}) collective-permute-start(f32[16,512]{1,0:T(8,128)S(1)} %shard_map.60.own_z), channel_id=1, source_target_pairs={{8,16},{24,32},{40,48},{56,64},{72,80},{88,96},{104,112},{120,128}... | collective-permute-start | bytes 98312 | tf_op jit(solution)/shard_map/ppermute | solution.py:684
  6.2 7.2 %collective-permute-start = (f32[16,512]{1,0:T(8,128)S(1)}, f32[16,512]{1,0:T(8,128)S(1)}, u32[]{:S(2)}, u32[]{:S(2)}) collective-permute-start(f32[16,512]{1,0:T(8,128)S(1)} %shard_map.59.own_s), channel_id=1, source_target_pairs={{0,8},{8,0},{16,24},{24,16},{32,40},{40,32},{48,56},{56,48},{64,72... | collective-permute-start | bytes 98312 | tf_op jit(solution)/shard_map/ppermute | solution.py:684
  13.6 4.8 %collective-permute-start.3 = (f32[40,256]{1,0:T(8,128)S(1)}, f32[40,256]{1,0:T(8,128)S(1)}, u32[]{:S(2)}, u32[]{:S(2)}) collective-permute-start(f32[40,256]{1,0:T(8,128)S(1)} %shard_map.63.own_z), channel_id=1, source_target_pairs={{1,2},{3,4},{5,6},{2,1},{4,3},{6,5},{9,10},{11,12},{13,14},{10,9},... | collective-permute-start | bytes 122888 | tf_op jit(solution)/shard_map/ppermute | solution.py:684
  14.5 5.3 %collective-permute-start.2 = (f32[40,256]{1,0:T(8,128)S(1)}, f32[40,256]{1,0:T(8,128)S(1)}, u32[]{:S(2)}, u32[]{:S(2)}) collective-permute-start(f32[40,256]{1,0:T(8,128)S(1)} %get-tuple-element.10.own_s), channel_id=1, source_target_pairs={{0,1},{1,0},{2,3},{3,2},{4,5},{5,4},{6,7},{7,6},{8,9},{9,8},{10,11... | collective-permute-start | bytes 122888 | tf_op jit(solution)/shard_map/ppermute | solution.py:684
  21.2 23.2 %all-to-all-start = ((f32[256,1,128]{2,1,0:T(1,128)}), f32[256,1,128]{2,1,0:T(1,128)S(1)}, u32[]{:S(2)}, u32[]{:S(2)}) async-start(f32[256,1,128]{2,1,0:T(1,128)} %bitcast.1), calls=%async_computation | async-start | bytes 262144 | tf_op jit(solution)/shard_map/all_to_all | solution.py:752
